TPU v7x, 128 devices: a whole 4x4x4 slice. The times are simulated.
128 devices in a mesh: section: 8 (over x, core), sector: 16 (over z, y).
Axes of the slice: x: 4, y: 4, z: 4, core: 2. Of those that a mesh axis runs over, the one named last changes fastest.
Arguments:
- wavefunction: bfloat16 [8, 16, 16, 256, 256], P('section', None, 'sector'), may hold values from -6 to 6
- left_env: bfloat16 [8, 14, 16, 256, 256], P('section', None, 'sector'), may hold values from -1 to 2
- right_env: bfloat16 [8, 14, 16, 256, 256], P('section', None, 'sector'), may hold values from -1 to 2
- term_table: int32 [16, 4], replicated, may hold values from 0 to 13
- source_table: int32 [16, 4], replicated, may hold values from 0 to 15
- live_sizes: int32 [8, 2, 16], P('section'), may hold values from 1 to 256, 3072 in all within a row
Outputs:
- next_basis: float32 [8, 16, 16, 256, 256], P('section', None, 'sector')
- projected: float32 [8, 3], P('section')
Inputs may be any that keep to these rules, and one draw needn't show every extreme that they name: `live_sizes`: each row of 16 live sizes sums to 3072 and its largest entry is exactly 256.
All inputs are finite; a program needn't handle non-finite values.
Results may differ from a plain program's by a relative error of at most 0.008.
Values may be sent and summed in bfloat16 or wider, within the bound.
No kernel may reach another device: no remote copies, remote signals or barrier semaphores. Data moves between devices by JAX's collectives and lax.ppermute only.
A program may use at most 128 MiB of HBM per device.

v0:
```python
import jax
import jax.numpy as jnp
from jax import lax
from jax.sharding import PartitionSpec as P

epsilon = 1e-06


def swapped(block, axis, distance):
    count = lax.axis_size(axis)
    route = []
    for low in range(count):
        high = low | 1 << distance
        if high != low and high < count:
            route += [(low, high), (high, low)]
    return lax.ppermute(block, axis, route)


def per_device(wavefunction, left_env, right_env, term_table, source_table, live_sizes):
    partner = swapped(right_env, "section", 0)[0]
    left_own = left_env[0]
    vector = wavefunction[0].astype(jnp.float32)
    sectors = vector.shape[0]
    local_sectors = vector.shape[1]
    block_size = vector.shape[2]
    cells = jnp.float32(sectors * sectors * block_size * block_size)
    offset = lax.axis_index("sector") * local_sectors
    positions = jnp.arange(block_size, dtype=jnp.int32)
    live_rows = positions[None, :] < live_sizes[0, 0][:, None]
    col_sizes = lax.dynamic_slice_in_dim(live_sizes[0, 1], offset, local_sectors, 0)
    live_cols = positions[None, :] < col_sizes[:, None]
    live_mask = (live_rows[:, None, :, None] & live_cols[None, :, None, :]).astype(jnp.float32)
    local_terms = lax.dynamic_slice_in_dim(term_table, offset, local_sectors, 0)
    own_rows = jnp.arange(local_sectors, dtype=jnp.int32)[:, None]
    picked_left = left_own[local_terms, own_rows]
    right_picked = partner[term_table]

    def apply_operator(vector_bf):
        inner_part = jnp.einsum(
            "akbij,akbjl->akbil",
            vector_bf[source_table],
            right_picked,
            preferred_element_type=jnp.float32,
        ).astype(jnp.bfloat16)
        regrouped = lax.all_to_all(inner_part, "sector", split_axis=0, concat_axis=2, tiled=True)
        partial_value = jnp.einsum(
            "akij,akbjl->abil", picked_left, regrouped, preferred_element_type=jnp.float32
        )
        image = lax.all_to_all(partial_value, "sector", split_axis=1, concat_axis=0, tiled=True)
        return image * live_mask

    masked = vector * live_mask
    start_mean = lax.psum(jnp.sum(masked * masked), "sector") / cells
    first_vector = masked * lax.rsqrt(start_mean + epsilon)
    first_image = apply_operator(first_vector.astype(jnp.bfloat16))
    rayleigh = lax.psum(jnp.sum(first_vector * first_image), "sector") / cells
    residual = first_image - rayleigh * first_vector
    residual_norm = lax.psum(jnp.sum(residual * residual), "sector") / cells
    second_vector = residual * lax.rsqrt(residual_norm + epsilon)
    second_image = apply_operator(second_vector.astype(jnp.bfloat16))
    upper_sum, lower_sum = lax.psum(
        (jnp.sum(first_vector * second_image), jnp.sum(second_vector * second_image)), "sector"
    )
    upper_entry = upper_sum / cells
    lower_entry = lower_sum / cells
    remainder = second_image - upper_entry * first_vector - lower_entry * second_vector
    remainder_norm = lax.psum(jnp.sum(remainder * remainder), "sector") / cells
    next_basis = remainder * lax.rsqrt(remainder_norm + epsilon)
    projected = jnp.stack([rayleigh, upper_entry, lower_entry])[None, :]
    return (next_basis[None], projected)


def solution(mesh):
    in_specs = (
        P("section", None, "sector", None, None),
        P("section", None, "sector", None, None),
        P("section", None, "sector", None, None),
        P(),
        P(),
        P("section", None, None),
    )
    out_specs = (P("section", None, "sector", None, None), P("section", None))
    return jax.shard_map(
        per_device, mesh=mesh, in_specs=in_specs, out_specs=out_specs, check_vma=False
    )
```

profile of v0, /device:TPU:0, one launch (start us, length us, event | category | flops | bytes accessed | tf_op | source)
XLA Modules:
  0.0 601.0 jit_solution(18397833894718464991)
XLA Ops:
  0.6 0.0 copy-start
  0.6 0.0 copy-start.9
  0.7 0.0 copy-start.7
  0.7 0.0 copy-start.8
  0.7 0.1 collective-permute-start
  0.8 4.0 copy.24
  4.8 0.0 copy-done.9
  4.8 0.6 constant_dynamic-slice_fusion
  5.4 0.6 iota_compare_fusion.1
  6.0 0.1 iota_compare_fusion
  6.1 3.3 fusion.18
  9.5 42.7 %psum.42 = f32[]{:T(128)} all-reduce(f32[]{:T(128)} %fusion.18), channel_id=1, replica_groups=mesh['section'=8,'sector'=16] {'sector'}, use_global_device_ids=true, to_apply=%region_1.0 | all-reduce | flops 1 | bytes 8 | tf_op jit(solution)/shard_map/psum | solution.py:53
  52.1 0.0 copy-done.7
  52.1 0.1 copy.26
  52.2 0.1 reshape.286
  52.3 0.0 copy-done.8
  52.3 0.1 copy.25
  52.4 0.1 reshape.276
  53.2 3.7 fusion.35
  56.9 7.1 %gather_fusion = bf16[64,256,256]{1,2,0:T(8,128)(2,1)} fusion(bf16[16,256,256]{1,2,0:T(8,128)(2,1)} %fusion.35, s32[1024]{0:T(1024)S(1)} %pad_clamp_fusion.1), kind=kCustom, calls=%fused_computation | custom fusion | bytes 16777472 | tf_op jit(solution)/shard_map/gather | solution.py:41
  64.1 0.0 collective-permute-done
  64.1 7.0 %gather_fusion.1 = bf16[64,256,256]{2,1,0:T(8,128)(2,1)} fusion(bf16[14,256,256]{2,1,0:T(8,128)(2,1)} %bitcast.5, s32[1024]{0:T(1024)S(1)} %pad_clamp_fusion), kind=kCustom, calls=%fused_computation.1 | custom fusion | bytes 16777472 | tf_op jit(solution)/shard_map/gather | solution.py:36
  71.1 9.8 %convert_bitcast_fusion.1 = bf16[16,4,1,256,256]{4,3,1,2,0:T(8,128)(2,1)} fusion(bf16[16,4,256,256]{2,3,1,0:T(8,128)(2,1)} %bitcast.146, bf16[16,4,256,256]{3,2,1,0:T(8,128)(2,1)} %bitcast.144), kind=kOutput, calls=%fused_computation.9 | convolution fusion | flops 2151677952 | bytes 25165824 | tf_op jit(solution)/shard_map/akbij,akbjl->akbil/dot_general | solution.py:39
  80.9 4.8 all-to-all-start
  85.7 0.2 fusion.38
  85.9 0.0 copy-done
  85.9 0.6 gather_fusion.2
  86.5 105.4 %all-to-all-done = bf16[16,4,1,256,256]{4,3,1,2,0:T(8,128)(2,1)} async-done(((bf16[16,4,1,256,256]{4,3,1,2,0:T(8,128)(2,1)}), bf16[16,4,1,256,256]{4,3,1,2,0:T(8,128)(2,1)}, u32[]{:S(2)}, u32[]{:S(2)}) %all-to-all-start) | async-done | bytes 8388640 | tf_op jit(solution)/shard_map/all_to_all | solution.py:45
  191.9 12.3 %copy.29 = bf16[16,4,1,256,256]{3,4,1,0,2:T(8,128)(2,1)} copy(bf16[16,4,1,256,256]{4,3,1,2,0:T(8,128)(2,1)} %all-to-all-done) | data formatting | bytes 16777216 | tf_op jit(solution)/shard_map/all_to_all | solution.py:45
  204.2 5.8 fusion.28
  210.0 0.0 copy-start.4
  210.0 53.1 %all_to_all.60 = f32[1,16,256,256]{2,3,0,1:T(8,128)S(1)} all-to-all(f32[1,16,256,256]{2,3,0,1:T(8,128)S(1)} %fusion.28), channel_id=1, replica_groups=mesh['section'=8,'sector'=16] {'sector'}, dimensions={1} | all-to-all | bytes 8388608 | tf_op jit(solution)/shard_map/all_to_all | solution.py:49
  263.1 0.0 copy-start.2
  263.1 2.0 copy-done.2
  265.1 0.0 copy-done.4
  265.1 1.8 fusion.11
  266.8 37.4 %psum.43 = f32[]{:T(128)} all-reduce(f32[]{:T(128)} %fusion.11), channel_id=1, replica_groups=mesh['section'=8,'sector'=16] {'sector'}, use_global_device_ids=true, to_apply=%region_3.0 | all-reduce | flops 1 | bytes 8 | tf_op jit(solution)/shard_map/psum | solution.py:56
  304.9 4.9 multiply_reduce_fusion.1
  309.8 36.9 %psum.44 = f32[]{:T(128)} all-reduce(f32[]{:T(128)} %multiply_reduce_fusion.1), channel_id=1, replica_groups=mesh['section'=8,'sector'=16] {'sector'}, use_global_device_ids=true, to_apply=%region_5.0 | all-reduce | flops 1 | bytes 8 | tf_op jit(solution)/shard_map/psum | solution.py:58
  347.4 5.5 fusion.34
  352.9 7.1 %gather_fusion.3 = bf16[64,256,256]{1,2,0:T(8,128)(2,1)} fusion(bf16[16,256,256]{1,2,0:T(8,128)(2,1)} %fusion.34, s32[1024]{0:T(1024)S(1)} %pad_clamp_fusion.1), kind=kCustom, calls=%fused_computation.3 | custom fusion | bytes 16777472 | tf_op jit(solution)/shard_map/gather | solution.py:41
  360.0 7.8 %convert_bitcast_fusion = bf16[16,4,1,256,256]{4,3,1,2,0:T(8,128)(2,1)S(1)} fusion(bf16[16,4,256,256]{2,3,1,0:T(8,128)(2,1)} %bitcast.147, bf16[16,4,256,256]{3,2,1,0:T(8,128)(2,1)} %bitcast.145), kind=kOutput, calls=%fused_computation.8 | convolution fusion | flops 2151677952 | bytes 25165824 | tf_op jit(solution)/shard_map/akbij,akbjl->akbil/dot_general | solution.py:39
  367.8 82.2 %all_to_all.61 = bf16[16,4,1,256,256]{4,3,1,2,0:T(8,128)(2,1)} all-to-all(bf16[16,4,1,256,256]{4,3,1,2,0:T(8,128)(2,1)S(1)} %convert_bitcast_fusion), channel_id=1, replica_groups=mesh['section'=8,'sector'=16] {'sector'}, dimensions={0} | all-to-all | bytes 16777216 | tf_op jit(solution)/shard_map/all_to_all | solution.py:45
  450.0 12.3 %copy.33 = bf16[16,4,1,256,256]{3,4,1,0,2:T(8,128)(2,1)} copy(bf16[16,4,1,256,256]{4,3,1,2,0:T(8,128)(2,1)} %all_to_all.61) | data formatting | bytes 16777216 | tf_op jit(solution)/shard_map/all_to_all | solution.py:45
  462.3 5.8 fusion.31
  468.0 0.0 copy-start.3
  468.1 0.0 copy-start.5
  468.1 35.7 %all_to_all.62 = f32[1,16,256,256]{2,3,0,1:T(8,128)S(1)} all-to-all(f32[1,16,256,256]{2,3,0,1:T(8,128)S(1)} %fusion.31), channel_id=1, replica_groups=mesh['section'=8,'sector'=16] {'sector'}, dimensions={1} | all-to-all | bytes 8388608 | tf_op jit(solution)/shard_map/all_to_all | solution.py:49
  503.7 0.0 copy-done.3
  503.8 0.0 copy-done.5
  503.8 0.0 copy-start.6
  503.8 2.7 fusion.13
  506.4 0.0 copy-done.6
  506.4 37.3 %all-reduce.1 = (f32[]{:T(128)}, f32[]{:T(128)}) all-reduce(f32[]{:T(128)} %get-tuple-element.9, f32[]{:T(128)} %get-tuple-element.8), channel_id=1, replica_groups=mesh['section'=8,'sector'=16] {'sector'}, use_global_device_ids=true, to_apply=%region_9.0 | all-reduce | flops 2 | bytes 16 | tf_op jit(solution)/shard_map/psum | solution.py:61
  545.0 5.9 fusion.17
  550.9 36.9 %psum.47 = f32[]{:T(128)} all-reduce(f32[]{:T(128)} %fusion.17), channel_id=1, replica_groups=mesh['section'=8,'sector'=16] {'sector'}, use_global_device_ids=true, to_apply=%region_11.0 | all-reduce | flops 1 | bytes 8 | tf_op jit(solution)/shard_map/psum | solution.py:67
  588.4 0.0 copy-start.1
  588.4 6.6 %fusion.21 = f32[1,16,1,256,256]{3,4,1,2,0:T(8,128)} fusion(bf16[1,16,1,256,256]{3,4,1,2,0:T(8,128)(2,1)} %copy.24, f32[1,16,256,256]{2,3,0,1:T(8,128)} %copy-done.2, f32[1,16,256,256]{2,3,0,1:T(8,128)} %copy-done.6, f32[]{:T(128)S(6)} %rsqrt.11, f32[]{:T(128)S(6)} %rsqrt.10, f32[]{:T(128)} %div.19, f32[]{:T(128)} %div.22, f32[]{:T(128)S(6)} %rsqrt.9, ...), kind=kLoop, calls=%fused_computation.34 | loop fusion | flops 14680064 | bytes 14684440 | tf_op jit(solution)/shard_map/mul | solution.py:68
  595.1 5.3 copy.35
  600.4 0.6 maximum_bitcast_fusion
  601.0 0.0 copy-done.1
  (7 shorter events, 0.0 us)
Async XLA Ops:
  0.6 85.2 %copy-start = (bf16[1,14,1,256,256]{4,3,2,1,0:T(8,128)(2,1)S(1)}, bf16[1,14,1,256,256]{4,3,2,1,0:T(8,128)(2,1)}, u32[]{:S(2)}) copy-start(bf16[1,14,1,256,256]{4,3,2,1,0:T(8,128)(2,1)} %param.7) | copy-start | bytes 5505028
  0.6 4.1 copy-start.9
  0.7 51.5 %copy-start.7 = (s32[16,4]{0,1:T(4,128)S(1)}, s32[16,4]{0,1:T(4,128)}, u32[]{:S(2)}) copy-start(s32[16,4]{0,1:T(4,128)} %param.9) | copy-start | bytes 772
  0.7 51.6 %copy-start.8 = (s32[16,4]{0,1:T(4,128)S(1)}, s32[16,4]{0,1:T(4,128)}, u32[]{:S(2)}) copy-start(s32[16,4]{0,1:T(4,128)} %param.10) | copy-start | bytes 772
  0.7 63.4 %collective-permute-start = (bf16[1,14,1,256,256]{4,3,2,1,0:T(8,128)(2,1)}, bf16[1,14,1,256,256]{4,3,2,1,0:T(8,128)(2,1)}, u32[]{:S(2)}, u32[]{:S(2)}) collective-permute-start(bf16[1,14,1,256,256]{4,3,2,1,0:T(8,128)(2,1)} %param.8), channel_id=1, source_target_pairs={{0,16},{16,0},{32,48},{48,32},{64,80},{80,64},{96,112},{112,96},{1... | collective-permute-start | bytes 5505032 | tf_op jit(solution)/shard_map/ppermute | solution.py:16
  80.9 111.1 %all-to-all-start = ((bf16[16,4,1,256,256]{4,3,1,2,0:T(8,128)(2,1)}), bf16[16,4,1,256,256]{4,3,1,2,0:T(8,128)(2,1)}, u32[]{:S(2)}, u32[]{:S(2)}) async-start(bf16[16,4,1,256,256]{4,3,1,2,0:T(8,128)(2,1)} %convert_bitcast_fusion.1), calls=%async_computation | async-start | bytes 16777216 | tf_op jit(solution)/shard_map/all_to_all | solution.py:45
  210.0 55.1 %copy-start.4 = (bf16[1,16,1,256,256]{3,4,1,2,0:T(8,128)(2,1)S(1)}, bf16[1,16,1,256,256]{3,4,1,2,0:T(8,128)(2,1)}, u32[]{:S(2)}) copy-start(bf16[1,16,1,256,256]{3,4,1,2,0:T(8,128)(2,1)} %copy.24) | copy-start | bytes 6291460
  263.1 2.0 copy-start.2
  468.0 35.7 %copy-start.3 = (f32[1,16,256,256]{2,3,0,1:T(8,128)S(1)}, f32[1,16,256,256]{2,3,0,1:T(8,128)}, u32[]{:S(2)}) copy-start(f32[1,16,256,256]{2,3,0,1:T(8,128)} %copy-done.2) | copy-start | bytes 12582916
  468.1 35.7 %copy-start.5 = (bf16[1,16,1,256,256]{3,4,1,2,0:T(8,128)(2,1)S(1)}, bf16[1,16,1,256,256]{3,4,1,2,0:T(8,128)(2,1)}, u32[]{:S(2)}) copy-start(bf16[1,16,1,256,256]{3,4,1,2,0:T(8,128)(2,1)} %copy.24) | copy-start | bytes 6291460
  503.8 2.7 copy-start.6
  588.4 12.6 %copy-start.1 = (bf16[1,14,1,256,256]{4,3,2,1,0:T(8,128)(2,1)S(1)}, bf16[1,14,1,256,256]{4,3,2,1,0:T(8,128)(2,1)}, u32[]{:S(2)}) copy-start(bf16[1,14,1,256,256]{4,3,2,1,0:T(8,128)(2,1)} %param.7) | copy-start | bytes 5505028
where the time goes:
time: 602 us; the launch traced here: 601 us
  blocking collectives  362 us (60%)
  waiting for transfers between devices  105 us (17%)
  local copies, waits for them, and re-layouts  58.7 us (10%)
  other arithmetic  35.9 us (6%)
  matrix products  29 us (5%)
    all_to_all x1, waiting for transfers between devices, apply_operator(): lax.all_to_all(inner_part, 'sector', split_axis=0, concat_axis=2, tiled=T...  105 us
    all_to_all x2, blocking collectives, apply_operator(): lax.all_to_all(partial_value, 'sector', split_axis=1, concat_axis=0, tile...  88.8 us
    all_to_all x1, blocking collectives, apply_operator(): lax.all_to_all(inner_part, 'sector', split_axis=0, concat_axis=2, tiled=T...  82.2 us
    psum x1, blocking collectives, per_device(): start_mean = lax.psum(jnp.sum(masked * masked), 'sector') / cells  42.7 us
    psum x1, blocking collectives, per_device(): rayleigh = lax.psum(jnp.sum(first_vector * first_image), 'sector') / cells  37.4 us
    psum x1, blocking collectives, per_device(): lax.psum((jnp.sum(first_vector * second_image), jnp.sum(second_vector * s...  37.3 us
    psum x1, blocking collectives, per_device(): residual_norm = lax.psum(jnp.sum(residual * residual), 'sector') / cells  36.9 us
    psum x1, blocking collectives, per_device(): remainder_norm = lax.psum(jnp.sum(remainder * remainder), 'sector') / cells  36.9 us
  transfers between devices with their start and end apart: 2, of which 1 were waited for; matrix products, arithmetic and copies ran while one was open for 3% of the time, Pallas kernels for 0%

commit v1 on v0

v1 whole, which is shorter than its diff:
```python
import functools

import jax
import jax.numpy as jnp
from jax import lax
from jax.experimental import pallas as pl
from jax.experimental.pallas import tpu as pltpu
from jax.sharding import PartitionSpec as P

epsilon = 1e-06
SIDE = 4
OFFSETS = (0, 3, 1, 2)
MIB = 1 << 20


def ring(dz, dy):
    return [
        (z * SIDE + y, ((z + dz) % SIDE) * SIDE + (y + dy) % SIDE)
        for z in range(SIDE)
        for y in range(SIDE)
    ]


def along(axis, step):
    return ring(step % SIDE, 0) if axis == "z" else ring(0, step % SIDE)


def send(block, axis, step):
    return lax.ppermute(block, "sector", along(axis, step))


def gather_halves(half_a, half_b):
    tie = lax.optimization_barrier
    routes = ((half_a, "y", "z"), (half_b, "z", "y"))
    near = [send(own, first, step) for own, first, _ in routes for step in (1, -1)]
    across = [send(own, first, 2) for own, first, _ in routes]
    near = tie(tuple(near))
    low = [jnp.stack([half_a, near[0]]), jnp.stack([half_b, near[2]])]
    across = tie(tuple(across))
    high = [jnp.stack([near[1], across[0]]), jnp.stack([near[3], across[1]])]
    axes = [second for _, _, second in routes]
    back_a, ahead_a, back_b, ahead_b = tie(
        (
            send(low[0], axes[0], 1),
            send(high[0], axes[0], -1),
            send(low[1], axes[1], 1),
            send(high[1], axes[1], -1),
        )
    )
    first = (back_a, back_b), (ahead_a, ahead_b)
    pieces = []
    for i, axis in enumerate(axes):
        low_back, high_ahead = first[0][i], first[1][i]
        high_back = send(high[i], axis, 1)
        low_ahead = send(low[i], axis, -1)
        low_across = send(low_back, axis, 1)
        high_across = send(high_ahead, axis, -1)
        pieces.append(
            [
                (low[i], high[i]),
                (low_back, high_back),
                (low_ahead, high_ahead),
                (low_across, high_across),
            ]
        )
    return pieces, near


def left_sector(sector, z_at, y_at):
    z = lax.rem(sector // SIDE + OFFSETS[z_at], SIDE)
    y = lax.rem(lax.rem(sector, SIDE) + OFFSETS[y_at], SIDE)
    return z * SIDE + y


def fold(block):
    return jnp.sum(block.reshape(block.shape[0] // 8, 8, block.shape[1]), axis=0)


def dot(a, b):
    return jnp.dot(a, b, preferred_element_type=jnp.float32)


def pick_kernel(sector, terms, sizes, left, half_a, half_b, blocks, sems):
    me = sector[0]
    copies = [pltpu.make_async_copy(left.at[0, terms[k, me], 0], blocks.at[k], sems.at[k]) for k in range(4)]
    for copy in copies:
        copy.start()
    size = blocks.shape[-1]
    keep = lax.broadcasted_iota(jnp.int32, (size, size), 0) < sizes[0, 0, me]
    for k, copy in enumerate(copies):
        copy.wait()
        block = jnp.where(keep, blocks[k].astype(jnp.float32), 0.0).astype(jnp.bfloat16)
        (half_a, half_b)[k // 2][k % 2] = block


def inner_product(a, k, terms, sources, vector, right):
    return dot(vector[sources[k, a]], right[terms[k, a]]).astype(jnp.bfloat16)


def left_block(pieces, z_at, y_at, k):
    if k < 2:
        return pieces[2 * z_at + y_at // 2][y_at % 2, k]
    return pieces[len(pieces) // 2 + 2 * y_at + z_at // 2][z_at % 2, k - 2]


def row_image(a, z_at, y_at, ks, terms, sources, vector, right, pieces):
    inner = [inner_product(a, k, terms, sources, vector, right) for k in ks]
    blocks = [left_block(pieces, z_at, y_at, k) for k in ks]
    return dot(jnp.concatenate(blocks, axis=1), jnp.concatenate(inner, axis=0))


WHOLE = [(z_at, y_at) for z_at in range(3) for y_at in range(3)]
LATE = [(3, 0), (3, 1), (3, 2), (0, 3), (1, 3), (2, 3), (3, 3)]


def late_ks(z_at, y_at):
    return ((0, 1) if z_at == 3 else ()) + ((2, 3) if y_at == 3 else ())


LATE_INNER = [(at, k) for at in LATE for k in late_ks(*at)]


def spread(total):
    return jnp.broadcast_to(jnp.sum(total, keepdims=True), (1, 128))


def first_kernel(sector, terms, sources, sizes, wave, right, *refs):
    pieces, (masked, right_live, field, part, inner, sums), (image,) = refs[:12], refs[12:18], refs[18:]
    size = image.shape[-1]
    me = sector[0]
    rows = lax.broadcasted_iota(jnp.int32, (size, size), 0)
    col_keep = lax.broadcasted_iota(jnp.int32, (size, size), 1) < sizes[0, 1, me]
    zero = jnp.zeros((8, size), jnp.float32)

    def mask_right(t, carry):
        right_live[t] = jnp.where(col_keep, right[0, t, 0].astype(jnp.float32), 0.0).astype(jnp.bfloat16)
        return carry

    def mask_wave(c, ww):
        keep = (rows < sizes[0, 0, c]) & col_keep
        w = jnp.where(keep, wave[0, c, 0].astype(jnp.float32), 0.0)
        masked[c] = w.astype(jnp.bfloat16)
        return ww + fold(w * w)

    lax.fori_loop(0, right_live.shape[0], mask_right, 0)
    ww = lax.fori_loop(0, masked.shape[0], mask_wave, zero)

    some_ww, some_wy = zero, zero
    for i, (z_at, y_at) in enumerate(WHOLE):
        a = left_sector(me, z_at, y_at)
        y = row_image(a, z_at, y_at, (0, 1, 2, 3), terms, sources, masked, right_live, pieces)
        image[i] = y
        w = masked[a].astype(jnp.float32)
        some_ww += fold(w * w)
        some_wy += fold(w * y)
    for i, (z_at, y_at) in enumerate(LATE[:6]):
        a = left_sector(me, z_at, y_at)
        ks = (2, 3) if z_at == 3 else (0, 1)
        part[i] = row_image(a, z_at, y_at, ks, terms, sources, masked, right_live, pieces)
    for i, ((z_at, y_at), k) in enumerate(LATE_INNER):
        a = left_sector(me, z_at, y_at)
        inner[i] = inner_product(a, k, terms, sources, masked, right_live)

    some_ww = jnp.sum(some_ww, keepdims=True)
    some_wy = jnp.sum(some_wy, keepdims=True)
    slope = jnp.where(some_ww > 0.0, some_wy / jnp.where(some_ww > 0.0, some_ww, 1.0), 0.0)
    wu, uu = zero, zero
    for i, (z_at, y_at) in enumerate(WHOLE):
        a = left_sector(me, z_at, y_at)
        w = masked[a].astype(jnp.float32)
        u = (image[i] - slope * w).astype(jnp.bfloat16)
        field[i] = u
        u = u.astype(jnp.float32)
        wu += fold(w * u)
        uu += fold(u * u)
    slope = jnp.broadcast_to(slope, (1, 128))
    sums[...] = jnp.concatenate([spread(ww), spread(wu), spread(uu)] + [slope] * 5, axis=0)


def second_kernel(sector, terms, sources, masked, right_live, field_some, part, inner, sums_first, *refs):
    pieces, (field, image, sums) = refs[:16], refs[16:]
    size = image.shape[-1]
    me = sector[0]
    zero = jnp.zeros((8, size), jnp.float32)
    slope = sums_first[3:4, :1]
    wu, uu = zero, zero
    at = 0
    for i, (z_at, y_at) in enumerate(LATE):
        a = left_sector(me, z_at, y_at)
        ks = late_ks(z_at, y_at)
        blocks = [left_block(pieces, z_at, y_at, k) for k in ks]
        late_inner = jnp.concatenate([inner[at + j] for j in range(len(ks))], axis=0)
        at += len(ks)
        y = dot(jnp.concatenate(blocks, axis=1), late_inner)
        if i < 6:
            y += part[i]
        w = masked[a].astype(jnp.float32)
        u = (y - slope * w).astype(jnp.bfloat16)
        field[a] = u
        u = u.astype(jnp.float32)
        wu += fold(w * u)
        uu += fold(u * u)
    for i, (z_at, y_at) in enumerate(WHOLE):
        field[left_sector(me, z_at, y_at)] = field_some[i]

    wv, uv, vv = zero, zero, zero
    for z_at in range(4):
        for y_at in range(4):
            a = left_sector(me, z_at, y_at)
            v = row_image(a, z_at, y_at, (0, 1, 2, 3), terms, sources, field, right_live, pieces)
            image[a] = v
            wv += fold(masked[a].astype(jnp.float32) * v)
            uv += fold(field[a].astype(jnp.float32) * v)
            vv += fold(v * v)

    head = sums_first[...]
    block = jnp.concatenate(
        [
            head[0:1],
            head[1:2] + spread(wu),
            head[2:3] + spread(uu),
            spread(wv),
            spread(uv),
            spread(vv),
            head[3:4],
            head[3:4],
        ],
        axis=0,
    )
    sums[...] = jnp.broadcast_to(block[None], sums.shape)


def last_kernel(cells, gathered, own, masked, field, image, out, projected, weights):
    step = pl.program_id(0)

    @pl.when(step == 0)
    def _():
        g = gathered[...]
        ww, wu, uu, wv, uv, vv, slope = (g[:, j, :] for j in range(7))

        def total(values):
            return jnp.sum(values, axis=0, keepdims=True) / cells

        alpha = lax.rsqrt(total(ww) + epsilon)
        wy = wu + slope * ww
        uy = uu + slope * wu
        theta = alpha * alpha * total(wy)
        delta = theta - slope
        beta = lax.rsqrt(alpha * alpha * total(uu - 2.0 * delta * wu + delta * delta * ww) + epsilon)
        scale = alpha * beta
        upper = alpha * scale * total(wv - delta * wy)
        lower = scale * scale * total(uv - delta * uy - delta * (wv - delta * wy))
        cu = delta + lower
        cw = delta * slope - lower * delta + upper / beta
        squares = vv + cu * cu * uu + cw * cw * ww - 2.0 * (cu * uv + cw * wv - cu * cw * wu)
        gamma = lax.rsqrt(scale * scale * total(squares) + epsilon)
        factor = gamma * scale
        own_slope = own[0, 6:7, :]
        own_delta = theta - own_slope
        own_cu = own_delta + lower
        own_cw = own_delta * own_slope - lower * own_delta + upper / beta
        weights[...] = jnp.concatenate([factor, factor * own_cu, factor * own_cw], axis=0)
        lane = lax.broadcasted_iota(jnp.int32, theta.shape, 1)
        entries = jnp.where(lane == 0, theta, jnp.where(lane == 1, upper, lower))
        projected[...] = entries[:, :3]

    def wide(j):
        row = weights[j : j + 1, :]
        return jnp.concatenate([row] * (out.shape[-1] // 128), axis=1)[None]

    per_step = out.shape[1]
    here = pl.ds(step * per_step, per_step)
    out[0, :, 0] = (
        image[here] * wide(0)
        - field[here].astype(jnp.float32) * wide(1)
        - masked[here].astype(jnp.float32) * wide(2)
    )


def per_device(wavefunction, left_env, right_env, term_table, source_table, live_sizes):
    sectors, size = wavefunction.shape[1], wavefunction.shape[3]
    terms_count = left_env.shape[1]
    smem = pl.BlockSpec(memory_space=pltpu.SMEM)
    vmem = pl.BlockSpec(memory_space=pltpu.VMEM)
    bf16, f32 = jnp.bfloat16, jnp.float32
    sector = lax.axis_index("sector").astype(jnp.int32)[None]
    terms, sources = term_table.T, source_table.T

    def blocks(count, dtype):
        return jax.ShapeDtypeStruct((count, size, size), dtype)

    half_a, half_b = pl.pallas_call(
        pick_kernel,
        out_shape=(blocks(2, bf16), blocks(2, bf16)),
        in_specs=[smem, smem, smem, pl.BlockSpec(memory_space=pl.ANY)],
        out_specs=(vmem, vmem),
        scratch_shapes=[pltpu.VMEM((4, size, size), bf16), pltpu.SemaphoreType.DMA((4,))],
        compiler_params=pltpu.CompilerParams(vmem_limit_bytes=4 * MIB),
        name="pick_left",
    )(sector, terms, live_sizes, left_env)

    (pairs_a, pairs_b), near = gather_halves(half_a, half_b)
    early = [p for pairs in (pairs_a, pairs_b) for pair in pairs[:3] for p in pair]
    every = [p for pairs in (pairs_a, pairs_b) for pair in pairs for p in pair]
    count = lax.axis_size("section")
    right_env, _ = lax.optimization_barrier((right_env, near[0]))
    partner = lax.ppermute(right_env, "section", [(s, s ^ 1) for s in range(count)])

    flop = 2 * size * size * size
    masked, right_live, field_some, part, inner, sums_first = pl.pallas_call(
        first_kernel,
        out_shape=(
            blocks(sectors, bf16),
            blocks(terms_count, bf16),
            blocks(len(WHOLE), bf16),
            blocks(6, f32),
            blocks(len(LATE_INNER), bf16),
            jax.ShapeDtypeStruct((8, 128), f32),
        ),
        in_specs=[smem] * 4 + [vmem] * 14,
        out_specs=(vmem,) * 6,
        scratch_shapes=[pltpu.VMEM((len(WHOLE), size, size), f32)],
        compiler_params=pltpu.CompilerParams(vmem_limit_bytes=20 * MIB),
        cost_estimate=pl.CostEstimate(flops=112 * flop, bytes_accessed=16 * MIB, transcendentals=0),
        name="first_image",
    )(sector, terms, sources, live_sizes, wavefunction, partner, *early)

    field, image, sums = pl.pallas_call(
        second_kernel,
        out_shape=(
            blocks(sectors, bf16),
            blocks(sectors, f32),
            jax.ShapeDtypeStruct((sectors, 8, 128), f32),
        ),
        in_specs=[smem] * 3 + [vmem] * 22,
        out_specs=(vmem,) * 3,
        compiler_params=pltpu.CompilerParams(vmem_limit_bytes=20 * MIB),
        cost_estimate=pl.CostEstimate(flops=144 * flop, bytes_accessed=24 * MIB, transcendentals=0),
        name="second_image",
    )(sector, terms, sources, masked, right_live, field_some, part, inner, sums_first, *every)

    gathered = lax.all_to_all(sums, "sector", 0, 0)
    per_step = 2
    cells = float(sectors * sectors * size * size)
    next_basis, projected = pl.pallas_call(
        functools.partial(last_kernel, cells),
        grid=(sectors // per_step,),
        out_shape=(
            jax.ShapeDtypeStruct((1, sectors, 1, size, size), f32),
            jax.ShapeDtypeStruct((1, 3), f32),
        ),
        in_specs=[vmem] * 5,
        out_specs=(
            pl.BlockSpec((1, per_step, 1, size, size), lambda i: (0, i, 0, 0, 0)),
            pl.BlockSpec((1, 3), lambda i: (0, 0)),
        ),
        scratch_shapes=[pltpu.VMEM((3, 128), f32)],
        compiler_params=pltpu.CompilerParams(vmem_limit_bytes=8 * MIB),
        name="next_basis",
    )(gathered, sums, masked, field, image)
    return next_basis, projected


def solution(mesh):
    in_specs = (
        P("section", None, "sector", None, None),
        P("section", None, "sector", None, None),
        P("section", None, "sector", None, None),
        P(),
        P(),
        P("section", None, None),
    )
    out_specs = (P("section", None, "sector", None, None), P("section", None))
    return jax.shard_map(
        per_device, mesh=mesh, in_specs=in_specs, out_specs=out_specs, check_vma=False
    )
```

time: 602 us -> 98.1 us (0.16)
  blocking collectives: 362 us -> 13.1 us
  waiting for transfers between devices: 105 us -> 22.2 us
  local copies, waits for them, and re-layouts: 58.7 us -> 2.87 us
  other arithmetic: 35.9 us -> 0.2 us
  starting transfers between devices: 4.88 us -> 39.1 us
  matrix products: 29 us -> 0 us
  Pallas kernels: 0 us -> 19.5 us
    psum x5 -> x0, blocking collectives: 191 us -> none  [the longest x1 42.7 us: per_device(): start_mean = lax.psum(jnp.sum(masked * masked), 'sector') / cells]
    all_to_all x3 -> x1, blocking collectives: 171 us -> 13.1 us  [per_device(): gathered = lax.all_to_all(sums, 'sector', 0, 0)]
    all_to_all x1 -> x0, waiting for transfers between devices: 105 us -> none  [apply_operator(): lax.all_to_all(inner_part, 'sector', split_axis=0, concat_axis=2, tiled=T...]
    ppermute x1 -> x19, starting transfers between devices: 0.09 us -> 39.1 us  [the longest x18 39.1 us: send(): return lax.ppermute(block, 'sector', along(axis, step))]
    dot_general x4 -> x0, matrix products: 29 us -> none  [the longest x2 17.5 us: apply_operator(): jnp.einsum('akbij,akbjl->akbil', vector_bf[source_table], right_picked, p...]
    all_to_all x2 -> x0, local copies, waits for them, and re-layouts: 24.6 us -> none  [apply_operator(): lax.all_to_all(inner_part, 'sector', split_axis=0, concat_axis=2, tiled=T...]
    ppermute x1 -> x19, waiting for transfers between devices: 0.01 us -> 22.2 us  [the longest x18 22.2 us: send(): return lax.ppermute(block, 'sector', along(axis, step))]
    gather x4 -> x0, local copies, waits for them, and re-layouts: 21.8 us -> none  [the longest x2 14.2 us: apply_operator(): vector_bf[source_table]]
  transfers between devices with their start and end apart: 2 -> 19, of which waited for: 1 -> 7; matrix products, arithmetic and copies ran while one was open for 3% -> 0% of each run, Pallas kernels for 0% -> 8%
where the time goes in v1:
time: 98.1 us; the launch traced here: 97.9 us
  starting transfers between devices  39.1 us (40%)
  waiting for transfers between devices  22.2 us (23%)
  Pallas kernels  19.5 us (20%)
  blocking collectives  13.1 us (13%)
  local copies, waits for them, and re-layouts  2.87 us (3%)
    ppermute x18, starting transfers between devices, send(): return lax.ppermute(block, 'sector', along(axis, step))  39.1 us
    ppermute x18, waiting for transfers between devices, send(): return lax.ppermute(block, 'sector', along(axis, step))  22.2 us
    all_to_all x1, blocking collectives, per_device(): gathered = lax.all_to_all(sums, 'sector', 0, 0)  13.1 us
    pallas_call x1, Pallas kernels, per_device(): pl.pallas_call(first_kernel, out_shape=(blocks(sectors, bf16), blocks(ter...  7.56 us
    pallas_call x1, Pallas kernels, per_device(): pl.pallas_call(second_kernel, out_shape=(blocks(sectors, bf16), blocks(se...  6.63 us
    pallas_call x1, Pallas kernels, per_device(): pl.pallas_call(functools.partial(last_kernel, cells), grid=(sectors // pe...  3.94 us
    unnamed x14, local copies, waits for them, and re-layouts  2.87 us
  transfers between devices with their start and end apart: 19, of which 7 were waited for; matrix products, arithmetic and copies ran while one was open for 0% of the time, Pallas kernels for 8%

profile of v1, /device:TPU:0, one launch (start us, length us, event | category | flops | bytes accessed | tf_op | source)
XLA Modules:
  0.0 97.9 jit_solution(2907089742387112699)
XLA Ops:
  0.6 0.0 copy-start
  0.6 1.5 %copy-done = bf16[1,14,1,256,256]{4,3,2,1,0:T(8,128)(2,1)S(1)} copy-done((bf16[1,14,1,256,256]{4,3,2,1,0:T(8,128)(2,1)S(1)}, bf16[1,14,1,256,256]{4,3,2,1,0:T(8,128)(2,1)}, u32[]{:S(2)}) %copy-start) | copy-done | bytes 1835032
  2.1 0.0 copy-start.1
  2.1 0.7 copy-done.1
  2.8 0.0 copy-start.3
  2.8 0.7 copy-done.3
  3.5 1.4 %pick_left.1 = (bf16[2,256,256]{2,1,0:T(8,128)(2,1)S(1)}, bf16[2,256,256]{2,1,0:T(8,128)(2,1)S(1)}) custom-call(s32[1]{0:T(128)} %bitcast.sector, s32[4,16]{1,0:T(4,128)S(1)} %bitcast.13, s32[1,2,16]{2,1,0:T(2,128)S(1)} %copy-done.3, bf16[1,14,1,256,256]{4,3,2,1,0:T(8,128)(2,1)S(1)} %copy-done), custom_call_target="tpu_custom_call" | custom-call | tf_op jit(solution)/shard_map/pick_left/pallas_call | solution.py:292
  4.9 3.2 %collective-permute-start.1 = (bf16[2,256,256]{2,1,0:T(8,128)(2,1)S(1)}, bf16[2,256,256]{2,1,0:T(8,128)(2,1)S(1)}, u32[]{:S(2)}, u32[]{:S(2)}) collective-permute-start(bf16[2,256,256]{2,1,0:T(8,128)(2,1)S(1)} %get-tuple-element.24), channel_id=1, source_target_pairs={{0,3},{1,0},{2,1},{3,2},{4,7},{5,4},{6,5},{7,6},{8,11},{9,8},{10,9... | collective-permute-start | bytes 786440 | tf_op jit(solution)/shard_map/ppermute | solution.py:29
  8.1 0.0 collective-permute-start
  8.1 4.0 %collective-permute-start.3 = (bf16[2,256,256]{2,1,0:T(8,128)(2,1)S(1)}, bf16[2,256,256]{2,1,0:T(8,128)(2,1)S(1)}, u32[]{:S(2)}, u32[]{:S(2)}) collective-permute-start(bf16[2,256,256]{2,1,0:T(8,128)(2,1)S(1)} %get-tuple-element.25), channel_id=1, source_target_pairs={{0,12},{1,13},{2,14},{3,15},{4,0},{5,1},{6,2},{7,3},{8,4},{9,5},{1... | collective-permute-start | bytes 786440 | tf_op jit(solution)/shard_map/ppermute | solution.py:29
  12.1 0.0 collective-permute-start.2
  12.1 2.2 %collective-permute-start.5 = (bf16[2,256,256]{2,1,0:T(8,128)(2,1)S(1)}, bf16[2,256,256]{2,1,0:T(8,128)(2,1)S(1)}, u32[]{:S(2)}, u32[]{:S(2)}) collective-permute-start(bf16[2,256,256]{2,1,0:T(8,128)(2,1)S(1)} %get-tuple-element.24), channel_id=1, source_target_pairs={{0,2},{1,3},{2,0},{3,1},{4,6},{5,7},{6,4},{7,5},{8,10},{9,11},{10,... | collective-permute-start | bytes 786440 | tf_op jit(solution)/shard_map/ppermute | solution.py:29
  14.3 0.0 collective-permute-done.1
  14.3 8.8 %collective-permute-start.6 = (bf16[2,256,256]{2,1,0:T(8,128)(2,1)S(1)}, bf16[2,256,256]{2,1,0:T(8,128)(2,1)S(1)}, u32[]{:S(2)}, u32[]{:S(2)}) collective-permute-start(bf16[2,256,256]{2,1,0:T(8,128)(2,1)S(1)} %get-tuple-element.25), channel_id=1, source_target_pairs={{0,8},{1,9},{2,10},{3,11},{4,12},{5,13},{6,14},{7,15},{8,0},{9,1},... | collective-permute-start | bytes 786440 | tf_op jit(solution)/shard_map/ppermute | solution.py:29
  23.2 0.0 collective-permute-done
  23.2 0.0 collective-permute-done.3
  23.2 0.4 collective-permute-done.2
  23.6 0.0 collective-permute-start.4
  23.6 0.0 collective-permute-done.5
  23.6 5.1 %collective-permute-done.6 = bf16[2,256,256]{2,1,0:T(8,128)(2,1)S(1)} collective-permute-done((bf16[2,256,256]{2,1,0:T(8,128)(2,1)S(1)}, bf16[2,256,256]{2,1,0:T(8,128)(2,1)S(1)}, u32[]{:S(2)}, u32[]{:S(2)}) %collective-permute-start.6) | collective-permute-done | bytes 262176 | tf_op jit(solution)/shard_map/ppermute | solution.py:29
  28.7 0.0 copy-start.2
  28.7 0.0 copy-start.4
  28.7 0.0 copy-start.5
  28.7 0.0 copy-start.6
  28.7 0.1 pad_maximum_fusion.refs_0_
  28.8 0.5 collective-permute-start.7
  29.2 0.1 pad_maximum_fusion.3.refs_7_.refs_9_
  29.3 4.4 %collective-permute-start.10 = (bf16[2,2,256,256]{3,2,1,0:T(8,128)(2,1)S(1)}, bf16[2,2,256,256]{3,2,1,0:T(8,128)(2,1)S(1)}, u32[]{:S(2)}, u32[]{:S(2)}) collective-permute-start(bf16[2,2,256,256]{3,2,1,0:T(8,128)(2,1)S(1)} %pad_maximum_fusion.3.refs_7_.refs_9_), channel_id=1, source_target_pairs={{0,3},{1,0},{2,1},{3,2},{4,7},{5,4},{6,5},{7,6},{8,11},{9,8},{10,9... | collective-permute-start | bytes 1572872 | tf_op jit(solution)/shard_map/ppermute | solution.py:29
  33.7 0.1 pad_maximum_fusion.2.refs_6_.refs_8_
  33.8 0.1 collective-permute-start.9
  33.8 0.1 pad_maximum_fusion.1.refs_1_
  33.9 3.3 %collective-permute-start.8 = (bf16[2,2,256,256]{3,2,1,0:T(8,128)(2,1)S(1)}, bf16[2,2,256,256]{3,2,1,0:T(8,128)(2,1)S(1)}, u32[]{:S(2)}, u32[]{:S(2)}) collective-permute-start(bf16[2,2,256,256]{3,2,1,0:T(8,128)(2,1)S(1)} %pad_maximum_fusion.1.refs_1_), channel_id=1, source_target_pairs={{0,12},{1,13},{2,14},{3,15},{4,0},{5,1},{6,2},{7,3},{8,4},{9,5},{1... | collective-permute-start | bytes 1572872 | tf_op jit(solution)/shard_map/ppermute | solution.py:29
  37.2 2.3 %collective-permute-done.7.refs_2_ = bf16[2,2,256,256]{3,2,1,0:T(8,128)(2,1)S(1)} collective-permute-done((bf16[2,2,256,256]{3,2,1,0:T(8,128)(2,1)S(1)}, bf16[2,2,256,256]{3,2,1,0:T(8,128)(2,1)S(1)}, u32[]{:S(2)}, u32[]{:S(2)}) %collective-permute-start.7) | collective-permute-done | bytes 524320 | tf_op jit(solution)/shard_map/ppermute | solution.py:29
  39.5 1.7 %collective-permute-start.12 = (bf16[2,2,256,256]{3,2,1,0:T(8,128)(2,1)S(1)}, bf16[2,2,256,256]{3,2,1,0:T(8,128)(2,1)S(1)}, u32[]{:S(2)}, u32[]{:S(2)}) collective-permute-start(bf16[2,2,256,256]{3,2,1,0:T(8,128)(2,1)S(1)} %pad_maximum_fusion.refs_0_), channel_id=1, source_target_pairs={{0,12},{1,13},{2,14},{3,15},{4,0},{5,1},{6,2},{7,3},{8,4},{9,5},{1... | collective-permute-start | bytes 1572872 | tf_op jit(solution)/shard_map/ppermute | solution.py:29
  41.2 0.0 collective-permute-done.10.refs_11_.refs_13_
  41.2 1.2 %collective-permute-start.13 = (bf16[2,2,256,256]{3,2,1,0:T(8,128)(2,1)S(1)}, bf16[2,2,256,256]{3,2,1,0:T(8,128)(2,1)S(1)}, u32[]{:S(2)}, u32[]{:S(2)}) collective-permute-start(bf16[2,2,256,256]{3,2,1,0:T(8,128)(2,1)S(1)} %pad_maximum_fusion.3.refs_7_.refs_9_), channel_id=1, source_target_pairs={{0,1},{1,2},{2,3},{3,0},{4,5},{5,6},{6,7},{7,4},{8,9},{9,10},{10,1... | collective-permute-start | bytes 1572872 | tf_op jit(solution)/shard_map/ppermute | solution.py:29
  42.5 6.1 %collective-permute-done.9.refs_8_.refs_10_ = bf16[2,2,256,256]{3,2,1,0:T(8,128)(2,1)S(1)} collective-permute-done((bf16[2,2,256,256]{3,2,1,0:T(8,128)(2,1)S(1)}, bf16[2,2,256,256]{3,2,1,0:T(8,128)(2,1)S(1)}, u32[]{:S(2)}, u32[]{:S(2)}) %collective-permute-start.9) | collective-permute-done | bytes 524320 | tf_op jit(solution)/shard_map/ppermute | solution.py:29
  48.5 0.0 collective-permute-start.14
  48.5 1.1 %collective-permute-done.8.refs_5_ = bf16[2,2,256,256]{3,2,1,0:T(8,128)(2,1)S(1)} collective-permute-done((bf16[2,2,256,256]{3,2,1,0:T(8,128)(2,1)S(1)}, bf16[2,2,256,256]{3,2,1,0:T(8,128)(2,1)S(1)}, u32[]{:S(2)}, u32[]{:S(2)}) %collective-permute-start.8) | collective-permute-done | bytes 524320 | tf_op jit(solution)/shard_map/ppermute | solution.py:29
  49.7 3.0 %collective-permute-start.11 = (bf16[2,2,256,256]{3,2,1,0:T(8,128)(2,1)S(1)}, bf16[2,2,256,256]{3,2,1,0:T(8,128)(2,1)S(1)}, u32[]{:S(2)}, u32[]{:S(2)}) collective-permute-start(bf16[2,2,256,256]{3,2,1,0:T(8,128)(2,1)S(1)} %pad_maximum_fusion.1.refs_1_), channel_id=1, source_target_pairs={{0,4},{1,5},{2,6},{3,7},{4,8},{5,9},{6,10},{7,11},{8,12},{9,13},{1... | collective-permute-start | bytes 1572872 | tf_op jit(solution)/shard_map/ppermute | solution.py:29
  52.7 2.6 %collective-permute-done.12.refs_4_ = bf16[2,2,256,256]{3,2,1,0:T(8,128)(2,1)S(1)} collective-permute-done((bf16[2,2,256,256]{3,2,1,0:T(8,128)(2,1)S(1)}, bf16[2,2,256,256]{3,2,1,0:T(8,128)(2,1)S(1)}, u32[]{:S(2)}, u32[]{:S(2)}) %collective-permute-start.12) | collective-permute-done | bytes 524320 | tf_op jit(solution)/shard_map/ppermute | solution.py:29
  55.3 1.7 %collective-permute-start.15 = (bf16[2,2,256,256]{3,2,1,0:T(8,128)(2,1)S(1)}, bf16[2,2,256,256]{3,2,1,0:T(8,128)(2,1)S(1)}, u32[]{:S(2)}, u32[]{:S(2)}) collective-permute-start(bf16[2,2,256,256]{3,2,1,0:T(8,128)(2,1)S(1)} %collective-permute-done.7.refs_2_), channel_id=1, source_target_pairs={{0,4},{1,5},{2,6},{3,7},{4,8},{5,9},{6,10},{7,11},{8,12},{9,13},{1... | collective-permute-start | bytes 1572872 | tf_op jit(solution)/shard_map/ppermute | solution.py:29
  57.0 0.0 collective-permute-done.13.refs_9_.refs_11_
  57.0 1.7 %collective-permute-start.16 = (bf16[2,2,256,256]{3,2,1,0:T(8,128)(2,1)S(1)}, bf16[2,2,256,256]{3,2,1,0:T(8,128)(2,1)S(1)}, u32[]{:S(2)}, u32[]{:S(2)}) collective-permute-start(bf16[2,2,256,256]{3,2,1,0:T(8,128)(2,1)S(1)} %collective-permute-done.8.refs_5_), channel_id=1, source_target_pairs={{0,12},{1,13},{2,14},{3,15},{4,0},{5,1},{6,2},{7,3},{8,4},{9,5},{1... | collective-permute-start | bytes 1572872 | tf_op jit(solution)/shard_map/ppermute | solution.py:29
  58.7 0.0 collective-permute-done.14.refs_10_.refs_12_
  58.7 0.6 collective-permute-start.17
  59.3 4.5 %collective-permute-done.11.refs_3_ = bf16[2,2,256,256]{3,2,1,0:T(8,128)(2,1)S(1)} collective-permute-done((bf16[2,2,256,256]{3,2,1,0:T(8,128)(2,1)S(1)}, bf16[2,2,256,256]{3,2,1,0:T(8,128)(2,1)S(1)}, u32[]{:S(2)}, u32[]{:S(2)}) %collective-permute-start.11) | collective-permute-done | bytes 524320 | tf_op jit(solution)/shard_map/ppermute | solution.py:29
  63.8 2.7 %collective-permute-start.18 = (bf16[2,2,256,256]{3,2,1,0:T(8,128)(2,1)S(1)}, bf16[2,2,256,256]{3,2,1,0:T(8,128)(2,1)S(1)}, u32[]{:S(2)}, u32[]{:S(2)}) collective-permute-start(bf16[2,2,256,256]{3,2,1,0:T(8,128)(2,1)S(1)} %collective-permute-done.10.refs_11_.refs_13_), channel_id=1, source_target_pairs={{0,3},{1,0},{2,1},{3,2},{4,7},{5,4},{6,5},{7,6},{8,11},{9,8},{10,9... | collective-permute-start | bytes 1572872 | tf_op jit(solution)/shard_map/ppermute | solution.py:29
  66.5 0.0 collective-permute-done.4.right
  66.5 0.0 copy-done.2
  66.5 0.0 copy-done.4
  66.5 0.0 copy-done.5
  66.5 0.0 copy-done.6
  66.5 7.6 %first_image.1 = (bf16[16,256,256]{2,1,0:T(8,128)(2,1)S(1)}, bf16[14,256,256]{2,1,0:T(8,128)(2,1)S(1)}, bf16[9,256,256]{2,1,0:T(8,128)(2,1)S(1)}, f32[6,256,256]...) custom-call(s32[1]{0:T(128)} %bitcast.sector, s32[4,16]{1,0:T(4,128)S(1)} %bitcast.14, ...), custom_call_target="tpu_custom_call" | custom-call | flops 3758096384 | bytes 16777216 | tf_op jit(solution)/shard_map/first_image/pallas_call | solution.py:310
  74.1 0.0 collective-permute-done.15.refs_6_
  74.1 0.0 collective-permute-done.16.refs_7_
  74.1 0.0 collective-permute-done.17.refs_14_
  74.1 0.0 collective-permute-done.18.refs_15_
  74.1 6.6 %second_image.1 = (bf16[16,256,256]{2,1,0:T(8,128)(2,1)S(1)}, f32[16,256,256]{2,1,0:T(8,128)S(1)}, f32[16,8,128]{2,1,0:T(8,128)S(1)}) custom-call(s32[1]{0:T(128)} %bitcast.sector, s32[4,16]{1,0:T(4,128)S(1)} %bitcast.15, s32[4,16]{1,0:T(4,128)S(1)} %bitcast.17, bf16[16,256,256]{2,1,0:T(8,128)(2,1)S(1)} %get-tuple-element.37.masked, ...), custom_call_target="tpu_custom_call" | custom-call | flops 4831838208 | bytes 25165824 | tf_op jit(solution)/shard_map/second_image/pallas_call | solution.py:328
  80.8 13.1 %all_to_all.5.gathered = f32[16,8,128]{2,1,0:T(8,128)S(1)} all-to-all(f32[16,8,128]{2,1,0:T(8,128)S(1)} %get-tuple-element.43.own), channel_id=1, replica_groups=mesh['section'=8,'sector'=16] {'sector'}, dimensions={0} | all-to-all | bytes 131072 | tf_op jit(solution)/shard_map/all_to_all | solution.py:342
  93.9 3.9 %next_basis.1 = (f32[1,16,1,256,256]{4,3,2,1,0:T(8,128)}, f32[1,3]{1,0:T(1,128)}) custom-call(f32[16,8,128]{2,1,0:T(8,128)S(1)} %all_to_all.5.gathered, f32[16,8,128]{2,1,0:T(8,128)S(1)} %get-tuple-element.43.own, bf16[16,256,256]{2,1,0:T(8,128)(2,1)S(1)} %get-tuple-element.37.masked, bf16[16,256,256]{2,1,0:T(8,128)(2,1)S(1)} %get-tuple-element.44.field, ...), custom_call_target="tpu_custom_call" | custom-call | tf_op jit(solution)/shard_map/next_basis/pallas_call | solution.py:345
Async XLA Ops:
  0.6 1.5 %copy-start = (bf16[1,14,1,256,256]{4,3,2,1,0:T(8,128)(2,1)S(1)}, bf16[1,14,1,256,256]{4,3,2,1,0:T(8,128)(2,1)}, u32[]{:S(2)}) copy-start(bf16[1,14,1,256,256]{4,3,2,1,0:T(8,128)(2,1)} %left.1) | copy-start | bytes 5505028
  2.1 0.7 copy-start.1
  2.8 0.7 copy-start.3
  4.9 9.4 %collective-permute-start.1 = (bf16[2,256,256]{2,1,0:T(8,128)(2,1)S(1)}, bf16[2,256,256]{2,1,0:T(8,128)(2,1)S(1)}, u32[]{:S(2)}, u32[]{:S(2)}) collective-permute-start(bf16[2,256,256]{2,1,0:T(8,128)(2,1)S(1)} %get-tuple-element.24), channel_id=1, source_target_pairs={{0,3},{1,0},{2,1},{3,2},{4,7},{5,4},{6,5},{7,6},{8,11},{9,8},{10,9... | collective-permute-start | bytes 786440 | tf_op jit(solution)/shard_map/ppermute | solution.py:29
  8.1 15.1 %collective-permute-start = (bf16[2,256,256]{2,1,0:T(8,128)(2,1)S(1)}, bf16[2,256,256]{2,1,0:T(8,128)(2,1)S(1)}, u32[]{:S(2)}, u32[]{:S(2)}) collective-permute-start(bf16[2,256,256]{2,1,0:T(8,128)(2,1)S(1)} %get-tuple-element.24), channel_id=1, source_target_pairs={{0,1},{1,2},{2,3},{3,0},{4,5},{5,6},{6,7},{7,4},{8,9},{9,10},{10,1... | collective-permute-start | bytes 786440 | tf_op jit(solution)/shard_map/ppermute | solution.py:29
  8.1 15.1 %collective-permute-start.3 = (bf16[2,256,256]{2,1,0:T(8,128)(2,1)S(1)}, bf16[2,256,256]{2,1,0:T(8,128)(2,1)S(1)}, u32[]{:S(2)}, u32[]{:S(2)}) collective-permute-start(bf16[2,256,256]{2,1,0:T(8,128)(2,1)S(1)} %get-tuple-element.25), channel_id=1, source_target_pairs={{0,12},{1,13},{2,14},{3,15},{4,0},{5,1},{6,2},{7,3},{8,4},{9,5},{1... | collective-permute-start | bytes 786440 | tf_op jit(solution)/shard_map/ppermute | solution.py:29
  12.1 11.5 %collective-permute-start.2 = (bf16[2,256,256]{2,1,0:T(8,128)(2,1)S(1)}, bf16[2,256,256]{2,1,0:T(8,128)(2,1)S(1)}, u32[]{:S(2)}, u32[]{:S(2)}) collective-permute-start(bf16[2,256,256]{2,1,0:T(8,128)(2,1)S(1)} %get-tuple-element.25), channel_id=1, source_target_pairs={{0,4},{1,5},{2,6},{3,7},{4,8},{5,9},{6,10},{7,11},{8,12},{9,13},{1... | collective-permute-start | bytes 786440 | tf_op jit(solution)/shard_map/ppermute | solution.py:29
  12.1 11.5 %collective-permute-start.5 = (bf16[2,256,256]{2,1,0:T(8,128)(2,1)S(1)}, bf16[2,256,256]{2,1,0:T(8,128)(2,1)S(1)}, u32[]{:S(2)}, u32[]{:S(2)}) collective-permute-start(bf16[2,256,256]{2,1,0:T(8,128)(2,1)S(1)} %get-tuple-element.24), channel_id=1, source_target_pairs={{0,2},{1,3},{2,0},{3,1},{4,6},{5,7},{6,4},{7,5},{8,10},{9,11},{10,... | collective-permute-start | bytes 786440 | tf_op jit(solution)/shard_map/ppermute | solution.py:29
  14.3 14.4 %collective-permute-start.6 = (bf16[2,256,256]{2,1,0:T(8,128)(2,1)S(1)}, bf16[2,256,256]{2,1,0:T(8,128)(2,1)S(1)}, u32[]{:S(2)}, u32[]{:S(2)}) collective-permute-start(bf16[2,256,256]{2,1,0:T(8,128)(2,1)S(1)} %get-tuple-element.25), channel_id=1, source_target_pairs={{0,8},{1,9},{2,10},{3,11},{4,12},{5,13},{6,14},{7,15},{8,0},{9,1},... | collective-permute-start | bytes 786440 | tf_op jit(solution)/shard_map/ppermute | solution.py:29
  23.6 42.9 %collective-permute-start.4 = (bf16[1,14,1,256,256]{4,3,2,1,0:T(8,128)(2,1)}, bf16[1,14,1,256,256]{4,3,2,1,0:T(8,128)(2,1)S(1)}, u32[]{:S(2)}, u32[]{:S(2)}) collective-permute-start(bf16[1,14,1,256,256]{4,3,2,1,0:T(8,128)(2,1)} %param.8), channel_id=1, source_target_pairs={{0,16},{16,0},{32,48},{48,32},{64,80},{80,64},{96,112},{112,96},{1... | collective-permute-start | bytes 5505032 | tf_op jit(solution)/shard_map/ppermute | solution.py:307
  28.7 37.8 %copy-start.2 = (s32[16,4]{0,1:T(4,128)S(1)}, s32[16,4]{0,1:T(4,128)}, u32[]{:S(2)}) copy-start(s32[16,4]{0,1:T(4,128)} %param.9) | copy-start | bytes 772
  28.7 37.8 %copy-start.4 = (s32[1,2,16]{2,1,0:T(2,128)S(1)}, s32[1,2,16]{2,1,0:T(2,128)}, u32[]{:S(2)}) copy-start(s32[1,2,16]{2,1,0:T(2,128)} %sizes.3) | copy-start | bytes 388
  28.7 37.8 %copy-start.5 = (bf16[1,16,1,256,256]{4,3,2,1,0:T(8,128)(2,1)S(1)}, bf16[1,16,1,256,256]{4,3,2,1,0:T(8,128)(2,1)}, u32[]{:S(2)}) copy-start(bf16[1,16,1,256,256]{4,3,2,1,0:T(8,128)(2,1)} %wave.1) | copy-start | bytes 6291460
  28.7 37.8 %copy-start.6 = (s32[16,4]{0,1:T(4,128)S(1)}, s32[16,4]{0,1:T(4,128)}, u32[]{:S(2)}) copy-start(s32[16,4]{0,1:T(4,128)} %param.10) | copy-start | bytes 772
  28.8 10.7 %collective-permute-start.7 = (bf16[2,2,256,256]{3,2,1,0:T(8,128)(2,1)S(1)}, bf16[2,2,256,256]{3,2,1,0:T(8,128)(2,1)S(1)}, u32[]{:S(2)}, u32[]{:S(2)}) collective-permute-start(bf16[2,2,256,256]{3,2,1,0:T(8,128)(2,1)S(1)} %pad_maximum_fusion.refs_0_), channel_id=1, source_target_pairs={{0,4},{1,5},{2,6},{3,7},{4,8},{5,9},{6,10},{7,11},{8,12},{9,13},{1... | collective-permute-start | bytes 1572872 | tf_op jit(solution)/shard_map/ppermute | solution.py:29
  29.3 12.0 %collective-permute-start.10 = (bf16[2,2,256,256]{3,2,1,0:T(8,128)(2,1)S(1)}, bf16[2,2,256,256]{3,2,1,0:T(8,128)(2,1)S(1)}, u32[]{:S(2)}, u32[]{:S(2)}) collective-permute-start(bf16[2,2,256,256]{3,2,1,0:T(8,128)(2,1)S(1)} %pad_maximum_fusion.3.refs_7_.refs_9_), channel_id=1, source_target_pairs={{0,3},{1,0},{2,1},{3,2},{4,7},{5,4},{6,5},{7,6},{8,11},{9,8},{10,9... | collective-permute-start | bytes 1572872 | tf_op jit(solution)/shard_map/ppermute | solution.py:29
  33.8 14.8 %collective-permute-start.9 = (bf16[2,2,256,256]{3,2,1,0:T(8,128)(2,1)S(1)}, bf16[2,2,256,256]{3,2,1,0:T(8,128)(2,1)S(1)}, u32[]{:S(2)}, u32[]{:S(2)}) collective-permute-start(bf16[2,2,256,256]{3,2,1,0:T(8,128)(2,1)S(1)} %pad_maximum_fusion.2.refs_6_.refs_8_), channel_id=1, source_target_pairs={{0,1},{1,2},{2,3},{3,0},{4,5},{5,6},{6,7},{7,4},{8,9},{9,10},{10,1... | collective-permute-start | bytes 1572872 | tf_op jit(solution)/shard_map/ppermute | solution.py:29
  33.9 15.8 %collective-permute-start.8 = (bf16[2,2,256,256]{3,2,1,0:T(8,128)(2,1)S(1)}, bf16[2,2,256,256]{3,2,1,0:T(8,128)(2,1)S(1)}, u32[]{:S(2)}, u32[]{:S(2)}) collective-permute-start(bf16[2,2,256,256]{3,2,1,0:T(8,128)(2,1)S(1)} %pad_maximum_fusion.1.refs_1_), channel_id=1, source_target_pairs={{0,12},{1,13},{2,14},{3,15},{4,0},{5,1},{6,2},{7,3},{8,4},{9,5},{1... | collective-permute-start | bytes 1572872 | tf_op jit(solution)/shard_map/ppermute | solution.py:29
  39.5 15.8 %collective-permute-start.12 = (bf16[2,2,256,256]{3,2,1,0:T(8,128)(2,1)S(1)}, bf16[2,2,256,256]{3,2,1,0:T(8,128)(2,1)S(1)}, u32[]{:S(2)}, u32[]{:S(2)}) collective-permute-start(bf16[2,2,256,256]{3,2,1,0:T(8,128)(2,1)S(1)} %pad_maximum_fusion.refs_0_), channel_id=1, source_target_pairs={{0,12},{1,13},{2,14},{3,15},{4,0},{5,1},{6,2},{7,3},{8,4},{9,5},{1... | collective-permute-start | bytes 1572872 | tf_op jit(solution)/shard_map/ppermute | solution.py:29
  41.2 15.8 %collective-permute-start.13 = (bf16[2,2,256,256]{3,2,1,0:T(8,128)(2,1)S(1)}, bf16[2,2,256,256]{3,2,1,0:T(8,128)(2,1)S(1)}, u32[]{:S(2)}, u32[]{:S(2)}) collective-permute-start(bf16[2,2,256,256]{3,2,1,0:T(8,128)(2,1)S(1)} %pad_maximum_fusion.3.refs_7_.refs_9_), channel_id=1, source_target_pairs={{0,1},{1,2},{2,3},{3,0},{4,5},{5,6},{6,7},{7,4},{8,9},{9,10},{10,1... | collective-permute-start | bytes 1572872 | tf_op jit(solution)/shard_map/ppermute | solution.py:29
  48.5 10.2 %collective-permute-start.14 = (bf16[2,2,256,256]{3,2,1,0:T(8,128)(2,1)S(1)}, bf16[2,2,256,256]{3,2,1,0:T(8,128)(2,1)S(1)}, u32[]{:S(2)}, u32[]{:S(2)}) collective-permute-start(bf16[2,2,256,256]{3,2,1,0:T(8,128)(2,1)S(1)} %pad_maximum_fusion.2.refs_6_.refs_8_), channel_id=1, source_target_pairs={{0,3},{1,0},{2,1},{3,2},{4,7},{5,4},{6,5},{7,6},{8,11},{9,8},{10,9... | collective-permute-start | bytes 1572872 | tf_op jit(solution)/shard_map/ppermute | solution.py:29
  49.7 14.1 %collective-permute-start.11 = (bf16[2,2,256,256]{3,2,1,0:T(8,128)(2,1)S(1)}, bf16[2,2,256,256]{3,2,1,0:T(8,128)(2,1)S(1)}, u32[]{:S(2)}, u32[]{:S(2)}) collective-permute-start(bf16[2,2,256,256]{3,2,1,0:T(8,128)(2,1)S(1)} %pad_maximum_fusion.1.refs_1_), channel_id=1, source_target_pairs={{0,4},{1,5},{2,6},{3,7},{4,8},{5,9},{6,10},{7,11},{8,12},{9,13},{1... | collective-permute-start | bytes 1572872 | tf_op jit(solution)/shard_map/ppermute | solution.py:29
  55.3 18.8 %collective-permute-start.15 = (bf16[2,2,256,256]{3,2,1,0:T(8,128)(2,1)S(1)}, bf16[2,2,256,256]{3,2,1,0:T(8,128)(2,1)S(1)}, u32[]{:S(2)}, u32[]{:S(2)}) collective-permute-start(bf16[2,2,256,256]{3,2,1,0:T(8,128)(2,1)S(1)} %collective-permute-done.7.refs_2_), channel_id=1, source_target_pairs={{0,4},{1,5},{2,6},{3,7},{4,8},{5,9},{6,10},{7,11},{8,12},{9,13},{1... | collective-permute-start | bytes 1572872 | tf_op jit(solution)/shard_map/ppermute | solution.py:29
  57.0 17.1 %collective-permute-start.16 = (bf16[2,2,256,256]{3,2,1,0:T(8,128)(2,1)S(1)}, bf16[2,2,256,256]{3,2,1,0:T(8,128)(2,1)S(1)}, u32[]{:S(2)}, u32[]{:S(2)}) collective-permute-start(bf16[2,2,256,256]{3,2,1,0:T(8,128)(2,1)S(1)} %collective-permute-done.8.refs_5_), channel_id=1, source_target_pairs={{0,12},{1,13},{2,14},{3,15},{4,0},{5,1},{6,2},{7,3},{8,4},{9,5},{1... | collective-permute-start | bytes 1572872 | tf_op jit(solution)/shard_map/ppermute | solution.py:29
  58.7 15.4 %collective-permute-start.17 = (bf16[2,2,256,256]{3,2,1,0:T(8,128)(2,1)S(1)}, bf16[2,2,256,256]{3,2,1,0:T(8,128)(2,1)S(1)}, u32[]{:S(2)}, u32[]{:S(2)}) collective-permute-start(bf16[2,2,256,256]{3,2,1,0:T(8,128)(2,1)S(1)} %collective-permute-done.9.refs_8_.refs_10_), channel_id=1, source_target_pairs={{0,1},{1,2},{2,3},{3,0},{4,5},{5,6},{6,7},{7,4},{8,9},{9,10},{10,1... | collective-permute-start | bytes 1572872 | tf_op jit(solution)/shard_map/ppermute | solution.py:29
  63.8 10.3 %collective-permute-start.18 = (bf16[2,2,256,256]{3,2,1,0:T(8,128)(2,1)S(1)}, bf16[2,2,256,256]{3,2,1,0:T(8,128)(2,1)S(1)}, u32[]{:S(2)}, u32[]{:S(2)}) collective-permute-start(bf16[2,2,256,256]{3,2,1,0:T(8,128)(2,1)S(1)} %collective-permute-done.10.refs_11_.refs_13_), channel_id=1, source_target_pairs={{0,3},{1,0},{2,1},{3,2},{4,7},{5,4},{6,5},{7,6},{8,11},{9,8},{10,9... | collective-permute-start | bytes 1572872 | tf_op jit(solution)/shard_map/ppermute | solution.py:29

commit v2 on v1

--- a/solution.py
+++ b/solution.py
@@ -29,41 +29,39 @@
     return lax.ppermute(block, "sector", along(axis, step))
 
 
+def after(value, *results):
+    return lax.optimization_barrier((value, *results))[0]
+
+
 def gather_halves(half_a, half_b):
-    tie = lax.optimization_barrier
-    routes = ((half_a, "y", "z"), (half_b, "z", "y"))
-    near = [send(own, first, step) for own, first, _ in routes for step in (1, -1)]
-    across = [send(own, first, 2) for own, first, _ in routes]
-    near = tie(tuple(near))
-    low = [jnp.stack([half_a, near[0]]), jnp.stack([half_b, near[2]])]
-    across = tie(tuple(across))
-    high = [jnp.stack([near[1], across[0]]), jnp.stack([near[3], across[1]])]
-    axes = [second for _, _, second in routes]
-    back_a, ahead_a, back_b, ahead_b = tie(
-        (
-            send(low[0], axes[0], 1),
-            send(high[0], axes[0], -1),
-            send(low[1], axes[1], 1),
-            send(high[1], axes[1], -1),
-        )
-    )
-    first = (back_a, back_b), (ahead_a, ahead_b)
+    own = (half_a, half_b)
+    first, second = ("y", "z"), ("z", "y")
+    near = {(i, step): send(own[i], first[i], step) for i in range(2) for step in (1, -1)}
+    across = [send(near[i, 1], first[i], 1) for i in range(2)]
+    last = {(first[i], step): near[i, step] for i in range(2) for step in (1, -1)}
+    last.update({(first[i], 1): across[i] for i in range(2)})
+    low = [jnp.stack([own[i], near[i, 1]]) for i in range(2)]
+    high = [jnp.stack([near[i, -1], across[i]]) for i in range(2)]
+    low_next, high_next = {}, {}
+    for i in range(2):
+        for step in (1, -1):
+            low_next[i, step] = send(after(low[i], last[second[i], step]), second[i], step)
+    for i in range(2):
+        for step in (1, -1):
+            high_next[i, step] = send(after(high[i], low_next[i, step]), second[i], step)
     pieces = []
-    for i, axis in enumerate(axes):
-        low_back, high_ahead = first[0][i], first[1][i]
-        high_back = send(high[i], axis, 1)
-        low_ahead = send(low[i], axis, -1)
-        low_across = send(low_back, axis, 1)
-        high_across = send(high_ahead, axis, -1)
+    for i in range(2):
+        low_across = send(after(low_next[i, 1], high_next[i, 1]), second[i], 1)
+        high_across = send(high_next[i, -1], second[i], -1)
         pieces.append(
             [
                 (low[i], high[i]),
-                (low_back, high_back),
-                (low_ahead, high_ahead),
+                (low_next[i, 1], high_next[i, 1]),
+                (low_next[i, -1], high_next[i, -1]),
                 (low_across, high_across),
             ]
         )
-    return pieces, near
+    return pieces
 
 
 def left_sector(sector, z_at, y_at):
@@ -292,19 +290,20 @@
     half_a, half_b = pl.pallas_call(
         pick_kernel,
         out_shape=(blocks(2, bf16), blocks(2, bf16)),
-        in_specs=[smem, smem, smem, pl.BlockSpec(memory_space=pl.ANY)],
+        in_specs=[smem, smem, smem, pl.BlockSpec(memory_space=pltpu.HBM)],
         out_specs=(vmem, vmem),
         scratch_shapes=[pltpu.VMEM((4, size, size), bf16), pltpu.SemaphoreType.DMA((4,))],
         compiler_params=pltpu.CompilerParams(vmem_limit_bytes=4 * MIB),
         name="pick_left",
     )(sector, terms, live_sizes, left_env)
 
-    (pairs_a, pairs_b), near = gather_halves(half_a, half_b)
+    pairs_a, pairs_b = gather_halves(half_a, half_b)
     early = [p for pairs in (pairs_a, pairs_b) for pair in pairs[:3] for p in pair]
     every = [p for pairs in (pairs_a, pairs_b) for pair in pairs for p in pair]
     count = lax.axis_size("section")
-    right_env, _ = lax.optimization_barrier((right_env, near[0]))
-    partner = lax.ppermute(right_env, "section", [(s, s ^ 1) for s in range(count)])
+    partner = lax.ppermute(
+        right_env, "section", [(s, s ^ 1) for s in range(count)]
+    )
 
     flop = 2 * size * size * size
     masked, right_live, field_some, part, inner, sums_first = pl.pallas_call(
@@ -321,7 +320,6 @@
         out_specs=(vmem,) * 6,
         scratch_shapes=[pltpu.VMEM((len(WHOLE), size, size), f32)],
         compiler_params=pltpu.CompilerParams(vmem_limit_bytes=20 * MIB),
-        cost_estimate=pl.CostEstimate(flops=112 * flop, bytes_accessed=16 * MIB, transcendentals=0),
         name="first_image",
     )(sector, terms, sources, live_sizes, wavefunction, partner, *early)
 

time: 98.1 us -> 88.2 us (0.90)
  starting transfers between devices: 39.1 us -> 29.2 us
  waiting for transfers between devices: 22.2 us -> 23.9 us
  blocking collectives: 13.1 us -> 11.6 us
    ppermute x18, starting transfers between devices: 39.1 us -> 29.2 us  [send(): return lax.ppermute(block, 'sector', along(axis, step))]
    ppermute x18, waiting for transfers between devices: 22.2 us -> 23.9 us  [send(): return lax.ppermute(block, 'sector', along(axis, step))]
    all_to_all x1, blocking collectives: 13.1 us -> 11.6 us  [per_device(): gathered = lax.all_to_all(sums, 'sector', 0, 0)]
  transfers between devices with their start and end apart: 19 -> 19, of which waited for: 7 -> 9; matrix products, arithmetic and copies ran while one was open for 0% -> 0% of each run, Pallas kernels for 8% -> 9%
where the time goes in v2:
time: 88.2 us; the launch traced here: 88 us
  starting transfers between devices  29.2 us (33%)
  waiting for transfers between devices  23.9 us (27%)
  Pallas kernels  19.5 us (22%)
  blocking collectives  11.6 us (13%)
  local copies, waits for them, and re-layouts  2.87 us (3%)
    ppermute x18, starting transfers between devices, send(): return lax.ppermute(block, 'sector', along(axis, step))  29.2 us
    ppermute x18, waiting for transfers between devices, send(): return lax.ppermute(block, 'sector', along(axis, step))  23.9 us
    all_to_all x1, blocking collectives, per_device(): gathered = lax.all_to_all(sums, 'sector', 0, 0)  11.6 us
    pallas_call x1, Pallas kernels, per_device(): pl.pallas_call(first_kernel, out_shape=(blocks(sectors, bf16), blocks(ter...  7.56 us
    pallas_call x1, Pallas kernels, per_device(): pl.pallas_call(second_kernel, out_shape=(blocks(sectors, bf16), blocks(se...  6.59 us
    pallas_call x1, Pallas kernels, per_device(): pl.pallas_call(functools.partial(last_kernel, cells), grid=(sectors // pe...  3.94 us
    unnamed x14, local copies, waits for them, and re-layouts  2.87 us
  transfers between devices with their start and end apart: 19, of which 9 were waited for; matrix products, arithmetic and copies ran while one was open for 0% of the time, Pallas kernels for 9%

profile of v2, /device:TPU:0, one launch (start us, length us, event | category | flops | bytes accessed | tf_op | source)
XLA Modules:
  0.0 88.0 jit_solution(7664901555587464496)
XLA Ops:
  0.6 0.0 copy-start.1
  0.6 1.5 %copy-done.1 = bf16[1,14,1,256,256]{4,3,2,1,0:T(8,128)(2,1)S(1)} copy-done((bf16[1,14,1,256,256]{4,3,2,1,0:T(8,128)(2,1)S(1)}, bf16[1,14,1,256,256]{4,3,2,1,0:T(8,128)(2,1)}, u32[]{:S(2)}) %copy-start.1) | copy-done | bytes 1835032
  2.1 0.0 copy-start.2
  2.1 0.7 copy-done.2
  2.8 0.0 copy-start.4
  2.8 0.7 copy-done.4
  3.5 1.4 %pick_left.1 = (bf16[2,256,256]{2,1,0:T(8,128)(2,1)S(1)}, bf16[2,256,256]{2,1,0:T(8,128)(2,1)S(1)}) custom-call(s32[1]{0:T(128)} %bitcast.sector, s32[4,16]{1,0:T(4,128)S(1)} %bitcast.13, s32[1,2,16]{2,1,0:T(2,128)S(1)} %copy-done.4, bf16[1,14,1,256,256]{4,3,2,1,0:T(8,128)(2,1)S(1)} %copy-done.1), custom_call_target="tpu_custom_call" | custom-call | tf_op jit(solution)/shard_map/pick_left/pallas_call | solution.py:290
  4.9 2.1 %collective-permute-start.4 = (bf16[2,256,256]{2,1,0:T(8,128)(2,1)S(1)}, bf16[2,256,256]{2,1,0:T(8,128)(2,1)S(1)}, u32[]{:S(2)}, u32[]{:S(2)}) collective-permute-start(bf16[2,256,256]{2,1,0:T(8,128)(2,1)S(1)} %get-tuple-element.24), channel_id=1, source_target_pairs={{0,4},{1,5},{2,6},{3,7},{4,8},{5,9},{6,10},{7,11},{8,12},{9,13},{1... | collective-permute-start | bytes 786440 | tf_op jit(solution)/shard_map/ppermute | solution.py:29
  7.0 1.6 %collective-permute-start.1 = (bf16[2,256,256]{2,1,0:T(8,128)(2,1)S(1)}, bf16[2,256,256]{2,1,0:T(8,128)(2,1)S(1)}, u32[]{:S(2)}, u32[]{:S(2)}) collective-permute-start(bf16[2,256,256]{2,1,0:T(8,128)(2,1)S(1)} %get-tuple-element.23), channel_id=1, source_target_pairs={{0,1},{1,2},{2,3},{3,0},{4,5},{5,6},{6,7},{7,4},{8,9},{9,10},{10,1... | collective-permute-start | bytes 786440 | tf_op jit(solution)/shard_map/ppermute | solution.py:29
  8.6 1.7 %collective-permute-start.2 = (bf16[2,256,256]{2,1,0:T(8,128)(2,1)S(1)}, bf16[2,256,256]{2,1,0:T(8,128)(2,1)S(1)}, u32[]{:S(2)}, u32[]{:S(2)}) collective-permute-start(bf16[2,256,256]{2,1,0:T(8,128)(2,1)S(1)} %get-tuple-element.23), channel_id=1, source_target_pairs={{0,3},{1,0},{2,1},{3,2},{4,7},{5,4},{6,5},{7,6},{8,11},{9,8},{10,9... | collective-permute-start | bytes 786440 | tf_op jit(solution)/shard_map/ppermute | solution.py:29
  10.2 2.2 %collective-permute-start.8 = (bf16[2,256,256]{2,1,0:T(8,128)(2,1)S(1)}, bf16[2,256,256]{2,1,0:T(8,128)(2,1)S(1)}, u32[]{:S(2)}, u32[]{:S(2)}) collective-permute-start(bf16[2,256,256]{2,1,0:T(8,128)(2,1)S(1)} %get-tuple-element.24), channel_id=1, source_target_pairs={{0,12},{1,13},{2,14},{3,15},{4,0},{5,1},{6,2},{7,3},{8,4},{9,5},{1... | collective-permute-start | bytes 786440 | tf_op jit(solution)/shard_map/ppermute | solution.py:29
  12.4 3.0 %collective-permute-done.4 = bf16[2,256,256]{2,1,0:T(8,128)(2,1)S(1)} collective-permute-done((bf16[2,256,256]{2,1,0:T(8,128)(2,1)S(1)}, bf16[2,256,256]{2,1,0:T(8,128)(2,1)S(1)}, u32[]{:S(2)}, u32[]{:S(2)}) %collective-permute-start.4) | collective-permute-done | bytes 262176 | tf_op jit(solution)/shard_map/ppermute | solution.py:29
  15.4 0.0 collective-permute-start.5
  15.4 0.6 collective-permute-done.1
  16.0 1.0 %collective-permute-start.3 = (bf16[2,256,256]{2,1,0:T(8,128)(2,1)S(1)}, bf16[2,256,256]{2,1,0:T(8,128)(2,1)S(1)}, u32[]{:S(2)}, u32[]{:S(2)}) collective-permute-start(bf16[2,256,256]{2,1,0:T(8,128)(2,1)S(1)} %collective-permute-done.1), channel_id=1, source_target_pairs={{0,1},{1,2},{2,3},{3,0},{4,5},{5,6},{6,7},{7,4},{8,9},{9,10},{10,1... | collective-permute-start | bytes 786440 | tf_op jit(solution)/shard_map/ppermute | solution.py:29
  17.0 0.0 collective-permute-start
  17.0 0.0 copy-start
  17.0 0.0 copy-start.3
  17.0 0.0 copy-start.5
  17.0 0.0 copy-start.6
  17.0 0.1 pad_maximum_fusion.2.refs_6_.refs_8_
  17.1 0.0 collective-permute-done.2
  17.1 2.3 %collective-permute-start.13 = (bf16[2,2,256,256]{3,2,1,0:T(8,128)(2,1)S(1)}, bf16[2,2,256,256]{3,2,1,0:T(8,128)(2,1)S(1)}, u32[]{:S(2)}, u32[]{:S(2)}) collective-permute-start(bf16[2,2,256,256]{3,2,1,0:T(8,128)(2,1)S(1)} %pad_maximum_fusion.2.refs_6_.refs_8_), channel_id=1, source_target_pairs={{0,3},{1,0},{2,1},{3,2},{4,7},{5,4},{6,5},{7,6},{8,11},{9,8},{10,9... | collective-permute-start | bytes 1572872 | tf_op jit(solution)/shard_map/ppermute | solution.py:29
  19.4 0.1 pad_maximum_fusion.refs_0_
  19.5 0.0 collective-permute-done.8
  19.5 2.7 %collective-permute-start.9 = (bf16[2,2,256,256]{3,2,1,0:T(8,128)(2,1)S(1)}, bf16[2,2,256,256]{3,2,1,0:T(8,128)(2,1)S(1)}, u32[]{:S(2)}, u32[]{:S(2)}) collective-permute-start(bf16[2,2,256,256]{3,2,1,0:T(8,128)(2,1)S(1)} %pad_maximum_fusion.refs_0_), channel_id=1, source_target_pairs={{0,12},{1,13},{2,14},{3,15},{4,0},{5,1},{6,2},{7,3},{8,4},{9,5},{1... | collective-permute-start | bytes 1572872 | tf_op jit(solution)/shard_map/ppermute | solution.py:29
  22.2 1.9 %collective-permute-done.5 = bf16[2,256,256]{2,1,0:T(8,128)(2,1)S(1)} collective-permute-done((bf16[2,256,256]{2,1,0:T(8,128)(2,1)S(1)}, bf16[2,256,256]{2,1,0:T(8,128)(2,1)S(1)}, u32[]{:S(2)}, u32[]{:S(2)}) %collective-permute-start.5) | collective-permute-done | bytes 262176 | tf_op jit(solution)/shard_map/ppermute | solution.py:29
  24.1 0.0 collective-permute-start.6
  24.1 0.1 collective-permute-done.3
  24.2 1.5 %collective-permute-start.11 = (bf16[2,2,256,256]{3,2,1,0:T(8,128)(2,1)S(1)}, bf16[2,2,256,256]{3,2,1,0:T(8,128)(2,1)S(1)}, u32[]{:S(2)}, u32[]{:S(2)}) collective-permute-start(bf16[2,2,256,256]{3,2,1,0:T(8,128)(2,1)S(1)} %pad_maximum_fusion.2.refs_6_.refs_8_), channel_id=1, source_target_pairs={{0,1},{1,2},{2,3},{3,0},{4,5},{5,6},{6,7},{7,4},{8,9},{9,10},{10,1... | collective-permute-start | bytes 1572872 | tf_op jit(solution)/shard_map/ppermute | solution.py:29
  25.7 0.1 pad_maximum_fusion.3.refs_7_.refs_9_
  25.8 0.1 pad_maximum_fusion.1.refs_1_
  25.8 5.7 %collective-permute-done.13.refs_10_.refs_12_ = bf16[2,2,256,256]{3,2,1,0:T(8,128)(2,1)S(1)} collective-permute-done((bf16[2,2,256,256]{3,2,1,0:T(8,128)(2,1)S(1)}, bf16[2,2,256,256]{3,2,1,0:T(8,128)(2,1)S(1)}, u32[]{:S(2)}, u32[]{:S(2)}) %collective-permute-start.13) | collective-permute-done | bytes 524320 | tf_op jit(solution)/shard_map/ppermute | solution.py:29
  31.5 3.5 %collective-permute-start.14 = (bf16[2,2,256,256]{3,2,1,0:T(8,128)(2,1)S(1)}, bf16[2,2,256,256]{3,2,1,0:T(8,128)(2,1)S(1)}, u32[]{:S(2)}, u32[]{:S(2)}) collective-permute-start(bf16[2,2,256,256]{3,2,1,0:T(8,128)(2,1)S(1)} %pad_maximum_fusion.3.refs_7_.refs_9_), channel_id=1, source_target_pairs={{0,3},{1,0},{2,1},{3,2},{4,7},{5,4},{6,5},{7,6},{8,11},{9,8},{10,9... | collective-permute-start | bytes 1572872 | tf_op jit(solution)/shard_map/ppermute | solution.py:29
  35.0 0.0 collective-permute-done.9.refs_4_
  35.0 2.6 %collective-permute-start.10 = (bf16[2,2,256,256]{3,2,1,0:T(8,128)(2,1)S(1)}, bf16[2,2,256,256]{3,2,1,0:T(8,128)(2,1)S(1)}, u32[]{:S(2)}, u32[]{:S(2)}) collective-permute-start(bf16[2,2,256,256]{3,2,1,0:T(8,128)(2,1)S(1)} %pad_maximum_fusion.1.refs_1_), channel_id=1, source_target_pairs={{0,12},{1,13},{2,14},{3,15},{4,0},{5,1},{6,2},{7,3},{8,4},{9,5},{1... | collective-permute-start | bytes 1572872 | tf_op jit(solution)/shard_map/ppermute | solution.py:29
  37.6 0.0 collective-permute-done.6.refs_2_
  37.6 0.0 collective-permute-start.7
  37.6 0.0 collective-permute-done.11.refs_8_.refs_10_
  37.6 1.5 %collective-permute-start.12 = (bf16[2,2,256,256]{3,2,1,0:T(8,128)(2,1)S(1)}, bf16[2,2,256,256]{3,2,1,0:T(8,128)(2,1)S(1)}, u32[]{:S(2)}, u32[]{:S(2)}) collective-permute-start(bf16[2,2,256,256]{3,2,1,0:T(8,128)(2,1)S(1)} %pad_maximum_fusion.3.refs_7_.refs_9_), channel_id=1, source_target_pairs={{0,1},{1,2},{2,3},{3,0},{4,5},{5,6},{6,7},{7,4},{8,9},{9,10},{10,1... | collective-permute-start | bytes 1572872 | tf_op jit(solution)/shard_map/ppermute | solution.py:29
  39.1 6.9 %collective-permute-done.14.refs_11_.refs_13_ = bf16[2,2,256,256]{3,2,1,0:T(8,128)(2,1)S(1)} collective-permute-done((bf16[2,2,256,256]{3,2,1,0:T(8,128)(2,1)S(1)}, bf16[2,2,256,256]{3,2,1,0:T(8,128)(2,1)S(1)}, u32[]{:S(2)}, u32[]{:S(2)}) %collective-permute-start.14) | collective-permute-done | bytes 524320 | tf_op jit(solution)/shard_map/ppermute | solution.py:29
  46.0 3.7 %collective-permute-start.18 = (bf16[2,2,256,256]{3,2,1,0:T(8,128)(2,1)S(1)}, bf16[2,2,256,256]{3,2,1,0:T(8,128)(2,1)S(1)}, u32[]{:S(2)}, u32[]{:S(2)}) collective-permute-start(bf16[2,2,256,256]{3,2,1,0:T(8,128)(2,1)S(1)} %collective-permute-done.14.refs_11_.refs_13_), channel_id=1, source_target_pairs={{0,3},{1,0},{2,1},{3,2},{4,7},{5,4},{6,5},{7,6},{8,11},{9,8},{10,9... | collective-permute-start | bytes 1572872 | tf_op jit(solution)/shard_map/ppermute | solution.py:29
  49.7 0.0 collective-permute-done.10.refs_5_
  49.7 2.6 %collective-permute-start.16 = (bf16[2,2,256,256]{3,2,1,0:T(8,128)(2,1)S(1)}, bf16[2,2,256,256]{3,2,1,0:T(8,128)(2,1)S(1)}, u32[]{:S(2)}, u32[]{:S(2)}) collective-permute-start(bf16[2,2,256,256]{3,2,1,0:T(8,128)(2,1)S(1)} %collective-permute-done.10.refs_5_), channel_id=1, source_target_pairs={{0,12},{1,13},{2,14},{3,15},{4,0},{5,1},{6,2},{7,3},{8,4},{9,5},{1... | collective-permute-start | bytes 1572872 | tf_op jit(solution)/shard_map/ppermute | solution.py:29
  52.3 0.0 collective-permute-done.7.refs_3_
  52.4 0.0 collective-permute-start.15
  52.4 0.0 collective-permute-done.12.refs_9_.refs_11_
  52.4 0.3 collective-permute-start.17
  52.6 0.0 collective-permute-done.right
  52.6 0.0 copy-done
  52.6 0.0 copy-done.3
  52.7 0.0 copy-done.5
  52.7 0.0 copy-done.6
  52.7 7.6 %first_image.1 = (bf16[16,256,256]{2,1,0:T(8,128)(2,1)S(1)}, bf16[14,256,256]{2,1,0:T(8,128)(2,1)S(1)}, bf16[9,256,256]{2,1,0:T(8,128)(2,1)S(1)}, f32[6,256,256]...) custom-call(s32[1]{0:T(128)} %bitcast.sector, s32[4,16]{1,0:T(4,128)S(1)} %bitcast.14, ...), custom_call_target="tpu_custom_call" | custom-call | tf_op jit(solution)/shard_map/first_image/pallas_call | solution.py:309
  60.2 0.0 collective-permute-done.18.refs_15_
  60.3 2.0 %collective-permute-done.16.refs_7_ = bf16[2,2,256,256]{3,2,1,0:T(8,128)(2,1)S(1)} collective-permute-done((bf16[2,2,256,256]{3,2,1,0:T(8,128)(2,1)S(1)}, bf16[2,2,256,256]{3,2,1,0:T(8,128)(2,1)S(1)}, u32[]{:S(2)}, u32[]{:S(2)}) %collective-permute-start.16) | collective-permute-done | bytes 524320 | tf_op jit(solution)/shard_map/ppermute | solution.py:29
  62.3 3.4 %collective-permute-done.15.refs_6_ = bf16[2,2,256,256]{3,2,1,0:T(8,128)(2,1)S(1)} collective-permute-done((bf16[2,2,256,256]{3,2,1,0:T(8,128)(2,1)S(1)}, bf16[2,2,256,256]{3,2,1,0:T(8,128)(2,1)S(1)}, u32[]{:S(2)}, u32[]{:S(2)}) %collective-permute-start.15) | collective-permute-done | bytes 524320 | tf_op jit(solution)/shard_map/ppermute | solution.py:29
  65.7 0.3 collective-permute-done.17.refs_14_
  65.9 6.6 %second_image.1 = (bf16[16,256,256]{2,1,0:T(8,128)(2,1)S(1)}, f32[16,256,256]{2,1,0:T(8,128)S(1)}, f32[16,8,128]{2,1,0:T(8,128)S(1)}) custom-call(s32[1]{0:T(128)} %bitcast.sector, s32[4,16]{1,0:T(4,128)S(1)} %bitcast.15, s32[4,16]{1,0:T(4,128)S(1)} %bitcast.17, bf16[16,256,256]{2,1,0:T(8,128)(2,1)S(1)} %get-tuple-element.33.masked, ...), custom_call_target="tpu_custom_call" | custom-call | flops 4831838208 | bytes 25165824 | tf_op jit(solution)/shard_map/second_image/pallas_call | solution.py:326
  72.5 11.6 %all_to_all.5.gathered = f32[16,8,128]{2,1,0:T(8,128)S(1)} all-to-all(f32[16,8,128]{2,1,0:T(8,128)S(1)} %get-tuple-element.41.own), channel_id=1, replica_groups=mesh['section'=8,'sector'=16] {'sector'}, dimensions={0} | all-to-all | bytes 131072 | tf_op jit(solution)/shard_map/all_to_all | solution.py:340
  84.1 3.9 %next_basis.1 = (f32[1,16,1,256,256]{4,3,2,1,0:T(8,128)}, f32[1,3]{1,0:T(1,128)}) custom-call(f32[16,8,128]{2,1,0:T(8,128)S(1)} %all_to_all.5.gathered, f32[16,8,128]{2,1,0:T(8,128)S(1)} %get-tuple-element.41.own, bf16[16,256,256]{2,1,0:T(8,128)(2,1)S(1)} %get-tuple-element.33.masked, bf16[16,256,256]{2,1,0:T(8,128)(2,1)S(1)} %get-tuple-element.42.field, ...), custom_call_target="tpu_custom_call" | custom-call | tf_op jit(solution)/shard_map/next_basis/pallas_call | solution.py:343
Async XLA Ops:
  0.6 1.5 %copy-start.1 = (bf16[1,14,1,256,256]{4,3,2,1,0:T(8,128)(2,1)S(1)}, bf16[1,14,1,256,256]{4,3,2,1,0:T(8,128)(2,1)}, u32[]{:S(2)}) copy-start(bf16[1,14,1,256,256]{4,3,2,1,0:T(8,128)(2,1)} %left.1) | copy-start | bytes 5505028
  2.1 0.7 copy-start.2
  2.8 0.7 copy-start.4
  4.9 10.5 %collective-permute-start.4 = (bf16[2,256,256]{2,1,0:T(8,128)(2,1)S(1)}, bf16[2,256,256]{2,1,0:T(8,128)(2,1)S(1)}, u32[]{:S(2)}, u32[]{:S(2)}) collective-permute-start(bf16[2,256,256]{2,1,0:T(8,128)(2,1)S(1)} %get-tuple-element.24), channel_id=1, source_target_pairs={{0,4},{1,5},{2,6},{3,7},{4,8},{5,9},{6,10},{7,11},{8,12},{9,13},{1... | collective-permute-start | bytes 786440 | tf_op jit(solution)/shard_map/ppermute | solution.py:29
  7.0 9.0 %collective-permute-start.1 = (bf16[2,256,256]{2,1,0:T(8,128)(2,1)S(1)}, bf16[2,256,256]{2,1,0:T(8,128)(2,1)S(1)}, u32[]{:S(2)}, u32[]{:S(2)}) collective-permute-start(bf16[2,256,256]{2,1,0:T(8,128)(2,1)S(1)} %get-tuple-element.23), channel_id=1, source_target_pairs={{0,1},{1,2},{2,3},{3,0},{4,5},{5,6},{6,7},{7,4},{8,9},{9,10},{10,1... | collective-permute-start | bytes 786440 | tf_op jit(solution)/shard_map/ppermute | solution.py:29
  8.6 8.5 %collective-permute-start.2 = (bf16[2,256,256]{2,1,0:T(8,128)(2,1)S(1)}, bf16[2,256,256]{2,1,0:T(8,128)(2,1)S(1)}, u32[]{:S(2)}, u32[]{:S(2)}) collective-permute-start(bf16[2,256,256]{2,1,0:T(8,128)(2,1)S(1)} %get-tuple-element.23), channel_id=1, source_target_pairs={{0,3},{1,0},{2,1},{3,2},{4,7},{5,4},{6,5},{7,6},{8,11},{9,8},{10,9... | collective-permute-start | bytes 786440 | tf_op jit(solution)/shard_map/ppermute | solution.py:29
  10.2 9.3 %collective-permute-start.8 = (bf16[2,256,256]{2,1,0:T(8,128)(2,1)S(1)}, bf16[2,256,256]{2,1,0:T(8,128)(2,1)S(1)}, u32[]{:S(2)}, u32[]{:S(2)}) collective-permute-start(bf16[2,256,256]{2,1,0:T(8,128)(2,1)S(1)} %get-tuple-element.24), channel_id=1, source_target_pairs={{0,12},{1,13},{2,14},{3,15},{4,0},{5,1},{6,2},{7,3},{8,4},{9,5},{1... | collective-permute-start | bytes 786440 | tf_op jit(solution)/shard_map/ppermute | solution.py:29
  15.4 8.7 %collective-permute-start.5 = (bf16[2,256,256]{2,1,0:T(8,128)(2,1)S(1)}, bf16[2,256,256]{2,1,0:T(8,128)(2,1)S(1)}, u32[]{:S(2)}, u32[]{:S(2)}) collective-permute-start(bf16[2,256,256]{2,1,0:T(8,128)(2,1)S(1)} %collective-permute-done.4), channel_id=1, source_target_pairs={{0,4},{1,5},{2,6},{3,7},{4,8},{5,9},{6,10},{7,11},{8,12},{9,13},{1... | collective-permute-start | bytes 786440 | tf_op jit(solution)/shard_map/ppermute | solution.py:29
  16.0 8.2 %collective-permute-start.3 = (bf16[2,256,256]{2,1,0:T(8,128)(2,1)S(1)}, bf16[2,256,256]{2,1,0:T(8,128)(2,1)S(1)}, u32[]{:S(2)}, u32[]{:S(2)}) collective-permute-start(bf16[2,256,256]{2,1,0:T(8,128)(2,1)S(1)} %collective-permute-done.1), channel_id=1, source_target_pairs={{0,1},{1,2},{2,3},{3,0},{4,5},{5,6},{6,7},{7,4},{8,9},{9,10},{10,1... | collective-permute-start | bytes 786440 | tf_op jit(solution)/shard_map/ppermute | solution.py:29
  17.0 35.6 %collective-permute-start = (bf16[1,14,1,256,256]{4,3,2,1,0:T(8,128)(2,1)}, bf16[1,14,1,256,256]{4,3,2,1,0:T(8,128)(2,1)S(1)}, u32[]{:S(2)}, u32[]{:S(2)}) collective-permute-start(bf16[1,14,1,256,256]{4,3,2,1,0:T(8,128)(2,1)} %param.8), channel_id=1, source_target_pairs={{0,16},{16,0},{32,48},{48,32},{64,80},{80,64},{96,112},{112,96},{1... | collective-permute-start | bytes 5505032 | tf_op jit(solution)/shard_map/ppermute | solution.py:304
  17.0 35.6 %copy-start = (bf16[1,16,1,256,256]{4,3,2,1,0:T(8,128)(2,1)S(1)}, bf16[1,16,1,256,256]{4,3,2,1,0:T(8,128)(2,1)}, u32[]{:S(2)}) copy-start(bf16[1,16,1,256,256]{4,3,2,1,0:T(8,128)(2,1)} %wave.1) | copy-start | bytes 6291460
  17.0 35.6 %copy-start.3 = (s32[16,4]{0,1:T(4,128)S(1)}, s32[16,4]{0,1:T(4,128)}, u32[]{:S(2)}) copy-start(s32[16,4]{0,1:T(4,128)} %param.9) | copy-start | bytes 772
  17.0 35.7 %copy-start.5 = (s32[1,2,16]{2,1,0:T(2,128)S(1)}, s32[1,2,16]{2,1,0:T(2,128)}, u32[]{:S(2)}) copy-start(s32[1,2,16]{2,1,0:T(2,128)} %sizes.3) | copy-start | bytes 388
  17.0 35.7 %copy-start.6 = (s32[16,4]{0,1:T(4,128)S(1)}, s32[16,4]{0,1:T(4,128)}, u32[]{:S(2)}) copy-start(s32[16,4]{0,1:T(4,128)} %param.10) | copy-start | bytes 772
  17.1 14.4 %collective-permute-start.13 = (bf16[2,2,256,256]{3,2,1,0:T(8,128)(2,1)S(1)}, bf16[2,2,256,256]{3,2,1,0:T(8,128)(2,1)S(1)}, u32[]{:S(2)}, u32[]{:S(2)}) collective-permute-start(bf16[2,2,256,256]{3,2,1,0:T(8,128)(2,1)S(1)} %pad_maximum_fusion.2.refs_6_.refs_8_), channel_id=1, source_target_pairs={{0,3},{1,0},{2,1},{3,2},{4,7},{5,4},{6,5},{7,6},{8,11},{9,8},{10,9... | collective-permute-start | bytes 1572872 | tf_op jit(solution)/shard_map/ppermute | solution.py:29
  19.5 15.5 %collective-permute-start.9 = (bf16[2,2,256,256]{3,2,1,0:T(8,128)(2,1)S(1)}, bf16[2,2,256,256]{3,2,1,0:T(8,128)(2,1)S(1)}, u32[]{:S(2)}, u32[]{:S(2)}) collective-permute-start(bf16[2,2,256,256]{3,2,1,0:T(8,128)(2,1)S(1)} %pad_maximum_fusion.refs_0_), channel_id=1, source_target_pairs={{0,12},{1,13},{2,14},{3,15},{4,0},{5,1},{6,2},{7,3},{8,4},{9,5},{1... | collective-permute-start | bytes 1572872 | tf_op jit(solution)/shard_map/ppermute | solution.py:29
  24.1 13.5 %collective-permute-start.6 = (bf16[2,2,256,256]{3,2,1,0:T(8,128)(2,1)S(1)}, bf16[2,2,256,256]{3,2,1,0:T(8,128)(2,1)S(1)}, u32[]{:S(2)}, u32[]{:S(2)}) collective-permute-start(bf16[2,2,256,256]{3,2,1,0:T(8,128)(2,1)S(1)} %pad_maximum_fusion.refs_0_), channel_id=1, source_target_pairs={{0,4},{1,5},{2,6},{3,7},{4,8},{5,9},{6,10},{7,11},{8,12},{9,13},{1... | collective-permute-start | bytes 1572872 | tf_op jit(solution)/shard_map/ppermute | solution.py:29
  24.2 13.4 %collective-permute-start.11 = (bf16[2,2,256,256]{3,2,1,0:T(8,128)(2,1)S(1)}, bf16[2,2,256,256]{3,2,1,0:T(8,128)(2,1)S(1)}, u32[]{:S(2)}, u32[]{:S(2)}) collective-permute-start(bf16[2,2,256,256]{3,2,1,0:T(8,128)(2,1)S(1)} %pad_maximum_fusion.2.refs_6_.refs_8_), channel_id=1, source_target_pairs={{0,1},{1,2},{2,3},{3,0},{4,5},{5,6},{6,7},{7,4},{8,9},{9,10},{10,1... | collective-permute-start | bytes 1572872 | tf_op jit(solution)/shard_map/ppermute | solution.py:29
  31.5 14.5 %collective-permute-start.14 = (bf16[2,2,256,256]{3,2,1,0:T(8,128)(2,1)S(1)}, bf16[2,2,256,256]{3,2,1,0:T(8,128)(2,1)S(1)}, u32[]{:S(2)}, u32[]{:S(2)}) collective-permute-start(bf16[2,2,256,256]{3,2,1,0:T(8,128)(2,1)S(1)} %pad_maximum_fusion.3.refs_7_.refs_9_), channel_id=1, source_target_pairs={{0,3},{1,0},{2,1},{3,2},{4,7},{5,4},{6,5},{7,6},{8,11},{9,8},{10,9... | collective-permute-start | bytes 1572872 | tf_op jit(solution)/shard_map/ppermute | solution.py:29
  35.0 14.8 %collective-permute-start.10 = (bf16[2,2,256,256]{3,2,1,0:T(8,128)(2,1)S(1)}, bf16[2,2,256,256]{3,2,1,0:T(8,128)(2,1)S(1)}, u32[]{:S(2)}, u32[]{:S(2)}) collective-permute-start(bf16[2,2,256,256]{3,2,1,0:T(8,128)(2,1)S(1)} %pad_maximum_fusion.1.refs_1_), channel_id=1, source_target_pairs={{0,12},{1,13},{2,14},{3,15},{4,0},{5,1},{6,2},{7,3},{8,4},{9,5},{1... | collective-permute-start | bytes 1572872 | tf_op jit(solution)/shard_map/ppermute | solution.py:29
  37.6 14.8 %collective-permute-start.7 = (bf16[2,2,256,256]{3,2,1,0:T(8,128)(2,1)S(1)}, bf16[2,2,256,256]{3,2,1,0:T(8,128)(2,1)S(1)}, u32[]{:S(2)}, u32[]{:S(2)}) collective-permute-start(bf16[2,2,256,256]{3,2,1,0:T(8,128)(2,1)S(1)} %pad_maximum_fusion.1.refs_1_), channel_id=1, source_target_pairs={{0,4},{1,5},{2,6},{3,7},{4,8},{5,9},{6,10},{7,11},{8,12},{9,13},{1... | collective-permute-start | bytes 1572872 | tf_op jit(solution)/shard_map/ppermute | solution.py:29
  37.6 14.8 %collective-permute-start.12 = (bf16[2,2,256,256]{3,2,1,0:T(8,128)(2,1)S(1)}, bf16[2,2,256,256]{3,2,1,0:T(8,128)(2,1)S(1)}, u32[]{:S(2)}, u32[]{:S(2)}) collective-permute-start(bf16[2,2,256,256]{3,2,1,0:T(8,128)(2,1)S(1)} %pad_maximum_fusion.3.refs_7_.refs_9_), channel_id=1, source_target_pairs={{0,1},{1,2},{2,3},{3,0},{4,5},{5,6},{6,7},{7,4},{8,9},{9,10},{10,1... | collective-permute-start | bytes 1572872 | tf_op jit(solution)/shard_map/ppermute | solution.py:29
  46.0 14.2 %collective-permute-start.18 = (bf16[2,2,256,256]{3,2,1,0:T(8,128)(2,1)S(1)}, bf16[2,2,256,256]{3,2,1,0:T(8,128)(2,1)S(1)}, u32[]{:S(2)}, u32[]{:S(2)}) collective-permute-start(bf16[2,2,256,256]{3,2,1,0:T(8,128)(2,1)S(1)} %collective-permute-done.14.refs_11_.refs_13_), channel_id=1, source_target_pairs={{0,3},{1,0},{2,1},{3,2},{4,7},{5,4},{6,5},{7,6},{8,11},{9,8},{10,9... | collective-permute-start | bytes 1572872 | tf_op jit(solution)/shard_map/ppermute | solution.py:29
  49.7 12.6 %collective-permute-start.16 = (bf16[2,2,256,256]{3,2,1,0:T(8,128)(2,1)S(1)}, bf16[2,2,256,256]{3,2,1,0:T(8,128)(2,1)S(1)}, u32[]{:S(2)}, u32[]{:S(2)}) collective-permute-start(bf16[2,2,256,256]{3,2,1,0:T(8,128)(2,1)S(1)} %collective-permute-done.10.refs_5_), channel_id=1, source_target_pairs={{0,12},{1,13},{2,14},{3,15},{4,0},{5,1},{6,2},{7,3},{8,4},{9,5},{1... | collective-permute-start | bytes 1572872 | tf_op jit(solution)/shard_map/ppermute | solution.py:29
  52.4 13.3 %collective-permute-start.15 = (bf16[2,2,256,256]{3,2,1,0:T(8,128)(2,1)S(1)}, bf16[2,2,256,256]{3,2,1,0:T(8,128)(2,1)S(1)}, u32[]{:S(2)}, u32[]{:S(2)}) collective-permute-start(bf16[2,2,256,256]{3,2,1,0:T(8,128)(2,1)S(1)} %collective-permute-done.6.refs_2_), channel_id=1, source_target_pairs={{0,4},{1,5},{2,6},{3,7},{4,8},{5,9},{6,10},{7,11},{8,12},{9,13},{1... | collective-permute-start | bytes 1572872 | tf_op jit(solution)/shard_map/ppermute | solution.py:29
  52.4 13.6 %collective-permute-start.17 = (bf16[2,2,256,256]{3,2,1,0:T(8,128)(2,1)S(1)}, bf16[2,2,256,256]{3,2,1,0:T(8,128)(2,1)S(1)}, u32[]{:S(2)}, u32[]{:S(2)}) collective-permute-start(bf16[2,2,256,256]{3,2,1,0:T(8,128)(2,1)S(1)} %collective-permute-done.11.refs_8_.refs_10_), channel_id=1, source_target_pairs={{0,1},{1,2},{2,3},{3,0},{4,5},{5,6},{6,7},{7,4},{8,9},{9,10},{10,1... | collective-permute-start | bytes 1572872 | tf_op jit(solution)/shard_map/ppermute | solution.py:29

commit v3 on v2

--- a/solution.py
+++ b/solution.py
@@ -33,14 +33,14 @@
     return lax.optimization_barrier((value, *results))[0]
 
 
-def gather_halves(half_a, half_b):
-    own = (half_a, half_b)
+def gather_halves(half_a, half_b, stage_a, stage_b):
+    own, kept = (half_a, half_b), (stage_a, stage_b)
     first, second = ("y", "z"), ("z", "y")
     near = {(i, step): send(own[i], first[i], step) for i in range(2) for step in (1, -1)}
     across = [send(near[i, 1], first[i], 1) for i in range(2)]
     last = {(first[i], step): near[i, step] for i in range(2) for step in (1, -1)}
     last.update({(first[i], 1): across[i] for i in range(2)})
-    low = [jnp.stack([own[i], near[i, 1]]) for i in range(2)]
+    low = [jnp.stack([kept[i], near[i, 1]]) for i in range(2)]
     high = [jnp.stack([near[i, -1], across[i]]) for i in range(2)]
     low_next, high_next = {}, {}
     for i in range(2):
@@ -51,14 +51,19 @@
             high_next[i, step] = send(after(high[i], low_next[i, step]), second[i], step)
     pieces = []
     for i in range(2):
-        low_across = send(after(low_next[i, 1], high_next[i, 1]), second[i], 1)
-        high_across = send(high_next[i, -1], second[i], -1)
+        one, two = low_next[i, 1], low_next[i, -1]
+        up = jnp.concatenate([one[0, :1], one[1]])
+        down = jnp.concatenate([high_next[i, -1].reshape(4, *two.shape[2:]), two[0, 1:]])
         pieces.append(
             [
-                (low[i], high[i]),
-                (low_next[i, 1], high_next[i, 1]),
-                (low_next[i, -1], high_next[i, -1]),
-                (low_across, high_across),
+                low[i],
+                high[i],
+                low_next[i, 1],
+                high_next[i, 1],
+                low_next[i, -1],
+                high_next[i, -1],
+                send(after(up, high_next[i, 1]), second[i], 1),
+                send(down, second[i], -1),
             ]
         )
     return pieces
@@ -91,14 +96,26 @@
         (half_a, half_b)[k // 2][k % 2] = block
 
 
+def stage_kernel(half_a, half_b, stage_a, stage_b):
+    stage_a[...] = half_a[...]
+    stage_b[...] = half_b[...]
+
+
 def inner_product(a, k, terms, sources, vector, right):
     return dot(vector[sources[k, a]], right[terms[k, a]]).astype(jnp.bfloat16)
 
 
+ACROSS = (((6, 0), (7, 4)), ((6, 1), (6, 2)), ((7, 0), (7, 1)), ((7, 2), (7, 3)))
+
+
 def left_block(pieces, z_at, y_at, k):
-    if k < 2:
-        return pieces[2 * z_at + y_at // 2][y_at % 2, k]
-    return pieces[len(pieces) // 2 + 2 * y_at + z_at // 2][z_at % 2, k - 2]
+    half = k // 2
+    first_at, second_at = ((y_at, z_at), (z_at, y_at))[half]
+    of_half = pieces[len(pieces) // 2 * half :]
+    if second_at == 3:
+        array, entry = ACROSS[first_at][k % 2]
+        return of_half[array][entry]
+    return of_half[2 * second_at + first_at // 2][first_at % 2, k % 2]
 
 
 def row_image(a, z_at, y_at, ks, terms, sources, vector, right, pieces):
@@ -293,13 +310,22 @@
         in_specs=[smem, smem, smem, pl.BlockSpec(memory_space=pltpu.HBM)],
         out_specs=(vmem, vmem),
         scratch_shapes=[pltpu.VMEM((4, size, size), bf16), pltpu.SemaphoreType.DMA((4,))],
-        compiler_params=pltpu.CompilerParams(vmem_limit_bytes=4 * MIB),
+        compiler_params=pltpu.CompilerParams(vmem_limit_bytes=60 * MIB),
         name="pick_left",
     )(sector, terms, live_sizes, left_env)
 
-    pairs_a, pairs_b = gather_halves(half_a, half_b)
-    early = [p for pairs in (pairs_a, pairs_b) for pair in pairs[:3] for p in pair]
-    every = [p for pairs in (pairs_a, pairs_b) for pair in pairs for p in pair]
+    stage_a, stage_b = pl.pallas_call(
+        stage_kernel,
+        out_shape=(blocks(2, bf16), blocks(2, bf16)),
+        in_specs=[vmem, vmem],
+        out_specs=(vmem, vmem),
+        compiler_params=pltpu.CompilerParams(vmem_limit_bytes=4 * MIB),
+        cost_estimate=pl.CostEstimate(flops=1 << 20, bytes_accessed=MIB, transcendentals=0),
+        name="stage",
+    )(half_a, half_b)
+    pieces_a, pieces_b = gather_halves(half_a, half_b, stage_a, stage_b)
+    early = pieces_a[:6] + pieces_b[:6]
+    every = pieces_a + pieces_b
     count = lax.axis_size("section")
     partner = lax.ppermute(
         right_env, "section", [(s, s ^ 1) for s in range(count)]
@@ -338,7 +364,7 @@
     )(sector, terms, sources, masked, right_live, field_some, part, inner, sums_first, *every)
 
     gathered = lax.all_to_all(sums, "sector", 0, 0)
-    per_step = 2
+    per_step = 8
     cells = float(sectors * sectors * size * size)
     next_basis, projected = pl.pallas_call(
         functools.partial(last_kernel, cells),
@@ -353,7 +379,7 @@
             pl.BlockSpec((1, 3), lambda i: (0, 0)),
         ),
         scratch_shapes=[pltpu.VMEM((3, 128), f32)],
-        compiler_params=pltpu.CompilerParams(vmem_limit_bytes=8 * MIB),
+        compiler_params=pltpu.CompilerParams(vmem_limit_bytes=12 * MIB),
         name="next_basis",
     )(gathered, sums, masked, field, image)
     return next_basis, projected

time: 88.2 us -> 85.4 us (0.968)
  starting transfers between devices: 29.2 us -> 26.2 us
  blocking collectives: 11.6 us -> 14.5 us
  waiting for transfers between devices: 23.9 us -> 21.7 us
    ppermute x18, starting transfers between devices: 29.2 us -> 26.2 us  [send(): return lax.ppermute(block, 'sector', along(axis, step))]
    all_to_all x1, blocking collectives: 11.6 us -> 14.5 us  [per_device(): gathered = lax.all_to_all(sums, 'sector', 0, 0)]
    ppermute x18, waiting for transfers between devices: 23.9 us -> 21.7 us  [send(): return lax.ppermute(block, 'sector', along(axis, step))]
    pallas_call x1, Pallas kernels: 1.41 us -> 2.77 us  [per_device(): pl.pallas_call(pick_kernel, out_shape=(blocks(2, bf16), blocks(2, bf16)),...]
    pallas_call x1, Pallas kernels: 3.94 us -> 2.59 us  [per_device(): pl.pallas_call(functools.partial(last_kernel, cells), grid=(sectors // pe...]
    unnamed x14, local copies, waits for them, and re-layouts: 2.87 us -> 1.95 us
  transfers between devices with their start and end apart: 19 -> 19, of which waited for: 9 -> 7; matrix products, arithmetic and copies ran while one was open for 0% -> 1% of each run, Pallas kernels for 9% -> 9%
where the time goes in v3:
time: 85.4 us; the launch traced here: 85.1 us
  starting transfers between devices  26.2 us (31%)
  waiting for transfers between devices  21.7 us (25%)
  Pallas kernels  19.5 us (23%)
  blocking collectives  14.5 us (17%)
  local copies, waits for them, and re-layouts  2.03 us (2%)
    ppermute x18, starting transfers between devices, send(): return lax.ppermute(block, 'sector', along(axis, step))  26.2 us
    ppermute x18, waiting for transfers between devices, send(): return lax.ppermute(block, 'sector', along(axis, step))  21.7 us
    all_to_all x1, blocking collectives, per_device(): gathered = lax.all_to_all(sums, 'sector', 0, 0)  14.5 us
    pallas_call x1, Pallas kernels, per_device(): pl.pallas_call(first_kernel, out_shape=(blocks(sectors, bf16), blocks(ter...  7.5 us
    pallas_call x1, Pallas kernels, per_device(): pl.pallas_call(second_kernel, out_shape=(blocks(sectors, bf16), blocks(se...  6.58 us
    pallas_call x1, Pallas kernels, per_device(): pl.pallas_call(pick_kernel, out_shape=(blocks(2, bf16), blocks(2, bf16)),...  2.77 us
    pallas_call x1, Pallas kernels, per_device(): pl.pallas_call(functools.partial(last_kernel, cells), grid=(sectors // pe...  2.59 us
    unnamed x14, local copies, waits for them, and re-layouts  1.95 us
  transfers between devices with their start and end apart: 19, of which 7 were waited for; matrix products, arithmetic and copies ran while one was open for 1% of the time, Pallas kernels for 9%

profile of v3, /device:TPU:0, one launch (start us, length us, event | category | flops | bytes accessed | tf_op | source)
XLA Modules:
  0.0 85.1 jit_solution(8870364077216902269)
XLA Ops:
  0.6 0.0 copy-start.6
  0.6 2.8 %pick_left.1 = (bf16[2,256,256]{2,1,0:T(8,128)(2,1)}, bf16[2,256,256]{2,1,0:T(8,128)(2,1)}) custom-call(s32[1]{0:T(128)} %bitcast.sector, s32[4,16]{1,0:T(4,128)} %bitcast.29, s32[1,2,16]{2,1,0:T(2,128)} %sizes.3, bf16[1,14,1,256,256]{4,3,2,1,0:T(8,128)(2,1)} %left.1), custom_call_target="tpu_custom_call" | custom-call | tf_op jit(solution)/shard_map/pick_left/pallas_call | solution.py:307
  3.4 1.7 %collective-permute-start.1 = (bf16[2,256,256]{2,1,0:T(8,128)(2,1)}, bf16[2,256,256]{2,1,0:T(8,128)(2,1)S(1)}, u32[]{:S(2)}, u32[]{:S(2)}) collective-permute-start(bf16[2,256,256]{2,1,0:T(8,128)(2,1)} %get-tuple-element.25.half_a), channel_id=1, source_target_pairs={{0,1},{1,2},{2,3},{3,0},{4,5},{5,6},{6,7},{7,4},{8,9},{9,10},{10,1... | collective-permute-start | bytes 786440 | tf_op jit(solution)/shard_map/ppermute | solution.py:29
  5.2 4.0 %collective-permute-start.8 = (bf16[2,256,256]{2,1,0:T(8,128)(2,1)}, bf16[2,256,256]{2,1,0:T(8,128)(2,1)S(1)}, u32[]{:S(2)}, u32[]{:S(2)}) collective-permute-start(bf16[2,256,256]{2,1,0:T(8,128)(2,1)} %get-tuple-element.26.half_b), channel_id=1, source_target_pairs={{0,12},{1,13},{2,14},{3,15},{4,0},{5,1},{6,2},{7,3},{8,4},{9,5},{1... | collective-permute-start | bytes 786440 | tf_op jit(solution)/shard_map/ppermute | solution.py:29
  9.2 0.0 collective-permute-start.4
  9.2 1.7 %collective-permute-start.2 = (bf16[2,256,256]{2,1,0:T(8,128)(2,1)}, bf16[2,256,256]{2,1,0:T(8,128)(2,1)S(1)}, u32[]{:S(2)}, u32[]{:S(2)}) collective-permute-start(bf16[2,256,256]{2,1,0:T(8,128)(2,1)} %get-tuple-element.25.half_a), channel_id=1, source_target_pairs={{0,3},{1,0},{2,1},{3,2},{4,7},{5,4},{6,5},{7,6},{8,11},{9,8},{10,9... | collective-permute-start | bytes 786440 | tf_op jit(solution)/shard_map/ppermute | solution.py:29
  10.9 0.0 copy-start.1
  10.9 1.0 %copy-done.1 = bf16[2,256,256]{2,1,0:T(8,128)(2,1)S(1)} copy-done((bf16[2,256,256]{2,1,0:T(8,128)(2,1)S(1)}, bf16[2,256,256]{2,1,0:T(8,128)(2,1)}, u32[]{:S(2)}) %copy-start.1) | copy-done | bytes 262168
  11.8 0.0 copy-start.2
  11.8 0.9 %copy-done.2 = bf16[2,256,256]{2,1,0:T(8,128)(2,1)S(1)} copy-done((bf16[2,256,256]{2,1,0:T(8,128)(2,1)S(1)}, bf16[2,256,256]{2,1,0:T(8,128)(2,1)}, u32[]{:S(2)}) %copy-start.2) | copy-done | bytes 262168
  12.8 0.3 collective-permute-done.1
  13.1 0.1 pad_maximum_fusion.2.refs_0_
  13.2 1.6 %collective-permute-done.8 = bf16[2,256,256]{2,1,0:T(8,128)(2,1)S(1)} collective-permute-done((bf16[2,256,256]{2,1,0:T(8,128)(2,1)}, bf16[2,256,256]{2,1,0:T(8,128)(2,1)S(1)}, u32[]{:S(2)}, u32[]{:S(2)}) %collective-permute-start.8) | collective-permute-done | bytes 262176 | tf_op jit(solution)/shard_map/ppermute | solution.py:29
  14.8 3.6 %collective-permute-start.9 = (bf16[2,2,256,256]{3,2,1,0:T(8,128)(2,1)S(1)}, bf16[2,2,256,256]{3,2,1,0:T(8,128)(2,1)S(1)}, u32[]{:S(2)}, u32[]{:S(2)}) collective-permute-start(bf16[2,2,256,256]{3,2,1,0:T(8,128)(2,1)S(1)} %pad_maximum_fusion.2.refs_0_), channel_id=1, source_target_pairs={{0,12},{1,13},{2,14},{3,15},{4,0},{5,1},{6,2},{7,3},{8,4},{9,5},{1... | collective-permute-start | bytes 1572872 | tf_op jit(solution)/shard_map/ppermute | solution.py:29
  18.4 0.0 collective-permute-done.4
  18.4 0.1 pad_maximum_fusion.4.refs_6_.refs_8_
  18.4 0.0 collective-permute-done.2
  18.4 1.9 %collective-permute-start.13 = (bf16[2,2,256,256]{3,2,1,0:T(8,128)(2,1)S(1)}, bf16[2,2,256,256]{3,2,1,0:T(8,128)(2,1)S(1)}, u32[]{:S(2)}, u32[]{:S(2)}) collective-permute-start(bf16[2,2,256,256]{3,2,1,0:T(8,128)(2,1)S(1)} %pad_maximum_fusion.4.refs_6_.refs_8_), channel_id=1, source_target_pairs={{0,3},{1,0},{2,1},{3,2},{4,7},{5,4},{6,5},{7,6},{8,11},{9,8},{10,9... | collective-permute-start | bytes 1572872 | tf_op jit(solution)/shard_map/ppermute | solution.py:29
  20.3 0.2 collective-permute-start.3
  20.5 0.0 collective-permute-start.5
  20.5 0.0 copy-done.6
  20.5 0.0 collective-permute-start
  20.6 7.4 %collective-permute-done.3 = bf16[2,256,256]{2,1,0:T(8,128)(2,1)S(1)} collective-permute-done((bf16[2,256,256]{2,1,0:T(8,128)(2,1)S(1)}, bf16[2,256,256]{2,1,0:T(8,128)(2,1)S(1)}, u32[]{:S(2)}, u32[]{:S(2)}) %collective-permute-start.3) | collective-permute-done | bytes 262176 | tf_op jit(solution)/shard_map/ppermute | solution.py:29
  28.0 0.1 collective-permute-done.5
  28.1 0.0 collective-permute-start.6
  28.1 1.6 %collective-permute-start.11 = (bf16[2,2,256,256]{3,2,1,0:T(8,128)(2,1)S(1)}, bf16[2,2,256,256]{3,2,1,0:T(8,128)(2,1)S(1)}, u32[]{:S(2)}, u32[]{:S(2)}) collective-permute-start(bf16[2,2,256,256]{3,2,1,0:T(8,128)(2,1)S(1)} %pad_maximum_fusion.4.refs_6_.refs_8_), channel_id=1, source_target_pairs={{0,1},{1,2},{2,3},{3,0},{4,5},{5,6},{6,7},{7,4},{8,9},{9,10},{10,1... | collective-permute-start | bytes 1572872 | tf_op jit(solution)/shard_map/ppermute | solution.py:29
  29.7 0.1 pad_maximum_fusion.5.refs_7_.refs_9_
  29.8 0.1 pad_maximum_fusion.3.refs_1_
  29.8 0.0 collective-permute-done.9.refs_4_
  29.8 3.3 %collective-permute-start.10 = (bf16[2,2,256,256]{3,2,1,0:T(8,128)(2,1)S(1)}, bf16[2,2,256,256]{3,2,1,0:T(8,128)(2,1)S(1)}, u32[]{:S(2)}, u32[]{:S(2)}) collective-permute-start(bf16[2,2,256,256]{3,2,1,0:T(8,128)(2,1)S(1)} %pad_maximum_fusion.3.refs_1_), channel_id=1, source_target_pairs={{0,12},{1,13},{2,14},{3,15},{4,0},{5,1},{6,2},{7,3},{8,4},{9,5},{1... | collective-permute-start | bytes 1572872 | tf_op jit(solution)/shard_map/ppermute | solution.py:29
  33.1 0.0 collective-permute-done.13.refs_10_.refs_12_
  33.1 1.7 %collective-permute-start.14 = (bf16[2,2,256,256]{3,2,1,0:T(8,128)(2,1)S(1)}, bf16[2,2,256,256]{3,2,1,0:T(8,128)(2,1)S(1)}, u32[]{:S(2)}, u32[]{:S(2)}) collective-permute-start(bf16[2,2,256,256]{3,2,1,0:T(8,128)(2,1)S(1)} %pad_maximum_fusion.5.refs_7_.refs_9_), channel_id=1, source_target_pairs={{0,3},{1,0},{2,1},{3,2},{4,7},{5,4},{6,5},{7,6},{8,11},{9,8},{10,9... | collective-permute-start | bytes 1572872 | tf_op jit(solution)/shard_map/ppermute | solution.py:29
  34.8 5.5 %collective-permute-done.6.refs_2_ = bf16[2,2,256,256]{3,2,1,0:T(8,128)(2,1)S(1)} collective-permute-done((bf16[2,2,256,256]{3,2,1,0:T(8,128)(2,1)S(1)}, bf16[2,2,256,256]{3,2,1,0:T(8,128)(2,1)S(1)}, u32[]{:S(2)}, u32[]{:S(2)}) %collective-permute-start.6) | collective-permute-done | bytes 524320 | tf_op jit(solution)/shard_map/ppermute | solution.py:29
  40.3 0.0 collective-permute-start.7
  40.3 0.0 collective-permute-done.11.refs_8_.refs_10_
  40.3 1.5 %collective-permute-start.12 = (bf16[2,2,256,256]{3,2,1,0:T(8,128)(2,1)S(1)}, bf16[2,2,256,256]{3,2,1,0:T(8,128)(2,1)S(1)}, u32[]{:S(2)}, u32[]{:S(2)}) collective-permute-start(bf16[2,2,256,256]{3,2,1,0:T(8,128)(2,1)S(1)} %pad_maximum_fusion.5.refs_7_.refs_9_), channel_id=1, source_target_pairs={{0,1},{1,2},{2,3},{3,0},{4,5},{5,6},{6,7},{7,4},{8,9},{9,10},{10,1... | collective-permute-start | bytes 1572872 | tf_op jit(solution)/shard_map/ppermute | solution.py:29
  41.9 3.1 %collective-permute-done.14.refs_11_.refs_13_ = bf16[2,2,256,256]{3,2,1,0:T(8,128)(2,1)S(1)} collective-permute-done((bf16[2,2,256,256]{3,2,1,0:T(8,128)(2,1)S(1)}, bf16[2,2,256,256]{3,2,1,0:T(8,128)(2,1)S(1)}, u32[]{:S(2)}, u32[]{:S(2)}) %collective-permute-start.14) | collective-permute-done | bytes 524320 | tf_op jit(solution)/shard_map/ppermute | solution.py:29
  44.9 0.0 copy-start
  44.9 0.0 copy-start.3
  45.0 0.0 copy-start.4
  45.0 0.0 copy-start.5
  45.0 0.1 pad_maximum_fusion.1
  45.0 1.9 %collective-permute-start.18 = (bf16[5,256,256]{2,1,0:T(8,128)(2,1)S(1)}, bf16[5,256,256]{2,1,0:T(8,128)(2,1)S(1)}, u32[]{:S(2)}, u32[]{:S(2)}) collective-permute-start(bf16[5,256,256]{2,1,0:T(8,128)(2,1)S(1)} %pad_maximum_fusion.1), channel_id=1, source_target_pairs={{0,3},{1,0},{2,1},{3,2},{4,7},{5,4},{6,5},{7,6},{8,11},{9,8},{10,9... | collective-permute-start | bytes 1966088 | tf_op jit(solution)/shard_map/ppermute | solution.py:29
  46.9 0.0 collective-permute-done.10.refs_5_
  46.9 0.1 pad_maximum_fusion
  46.9 1.8 %collective-permute-start.16 = (bf16[5,256,256]{2,1,0:T(8,128)(2,1)S(1)}, bf16[5,256,256]{2,1,0:T(8,128)(2,1)S(1)}, u32[]{:S(2)}, u32[]{:S(2)}) collective-permute-start(bf16[5,256,256]{2,1,0:T(8,128)(2,1)S(1)} %pad_maximum_fusion), channel_id=1, source_target_pairs={{0,12},{1,13},{2,14},{3,15},{4,0},{5,1},{6,2},{7,3},{8,4},{9,5},{1... | collective-permute-start | bytes 1966088 | tf_op jit(solution)/shard_map/ppermute | solution.py:29
  48.8 3.6 %collective-permute-done.7.refs_3_ = bf16[2,2,256,256]{3,2,1,0:T(8,128)(2,1)S(1)} collective-permute-done((bf16[2,2,256,256]{3,2,1,0:T(8,128)(2,1)S(1)}, bf16[2,2,256,256]{3,2,1,0:T(8,128)(2,1)S(1)}, u32[]{:S(2)}, u32[]{:S(2)}) %collective-permute-start.7) | collective-permute-done | bytes 524320 | tf_op jit(solution)/shard_map/ppermute | solution.py:29
  52.4 0.0 collective-permute-start.15
  52.4 0.0 collective-permute-done.12.refs_9_.refs_11_
  52.4 1.5 %collective-permute-start.17 = (bf16[3,256,256]{2,1,0:T(8,128)(2,1)S(1)}, bf16[3,256,256]{2,1,0:T(8,128)(2,1)S(1)}, u32[]{:S(2)}, u32[]{:S(2)}) collective-permute-start(bf16[3,256,256]{2,1,0:T(8,128)(2,1)S(1)} %pad_maximum_fusion.7), channel_id=1, source_target_pairs={{0,1},{1,2},{2,3},{3,0},{4,5},{5,6},{6,7},{7,4},{8,9},{9,10},{10,1... | collective-permute-start | bytes 1179656 | tf_op jit(solution)/shard_map/ppermute | solution.py:29
  53.9 0.0 collective-permute-done.right
  53.9 0.0 copy-done
  53.9 0.0 copy-done.3
  53.9 0.0 copy-done.4
  53.9 0.0 copy-done.5
  53.9 7.5 %first_image.1 = (bf16[16,256,256]{2,1,0:T(8,128)(2,1)S(1)}, bf16[14,256,256]{2,1,0:T(8,128)(2,1)S(1)}, bf16[9,256,256]{2,1,0:T(8,128)(2,1)S(1)}, f32[6,256,256]...) custom-call(s32[1]{0:T(128)} %bitcast.sector, s32[4,16]{1,0:T(4,128)S(1)} %bitcast.30, ...), custom_call_target="tpu_custom_call" | custom-call | tf_op jit(solution)/shard_map/first_image/pallas_call | solution.py:335
  61.4 0.0 collective-permute-done.15.refs_6_
  61.4 0.0 collective-permute-done.17.refs_14_
  61.4 0.0 collective-permute-done.18.refs_15_
  61.5 0.0 collective-permute-done.16.refs_7_
  61.5 6.6 %second_image.1 = (bf16[16,256,256]{2,1,0:T(8,128)(2,1)S(1)}, f32[16,256,256]{2,1,0:T(8,128)S(1)}, f32[16,8,128]{2,1,0:T(8,128)S(1)}) custom-call(s32[1]{0:T(128)} %bitcast.sector, s32[4,16]{1,0:T(4,128)S(1)} %bitcast.31, s32[4,16]{1,0:T(4,128)S(1)} %bitcast.33, bf16[16,256,256]{2,1,0:T(8,128)(2,1)S(1)} %get-tuple-element.37.masked, ...), custom_call_target="tpu_custom_call" | custom-call | flops 4831838208 | bytes 25165824 | tf_op jit(solution)/shard_map/second_image/pallas_call | solution.py:352
  68.1 14.5 %all_to_all.5.gathered = f32[16,8,128]{2,1,0:T(8,128)S(1)} all-to-all(f32[16,8,128]{2,1,0:T(8,128)S(1)} %get-tuple-element.45.own), channel_id=1, replica_groups=mesh['section'=8,'sector'=16] {'sector'}, dimensions={0} | all-to-all | bytes 131072 | tf_op jit(solution)/shard_map/all_to_all | solution.py:366
  82.5 2.6 %next_basis.1 = (f32[1,16,1,256,256]{4,3,2,1,0:T(8,128)}, f32[1,3]{1,0:T(1,128)}) custom-call(f32[16,8,128]{2,1,0:T(8,128)S(1)} %all_to_all.5.gathered, f32[16,8,128]{2,1,0:T(8,128)S(1)} %get-tuple-element.45.own, bf16[16,256,256]{2,1,0:T(8,128)(2,1)S(1)} %get-tuple-element.37.masked, bf16[16,256,256]{2,1,0:T(8,128)(2,1)S(1)} %get-tuple-element.46.field, ...), custom_call_target="tpu_custom_call" | custom-call | tf_op jit(solution)/shard_map/next_basis/pallas_call | solution.py:369
  (9 shorter events, 0.2 us)
Async XLA Ops:
  0.6 19.9 %copy-start.6 = (bf16[1,14,1,256,256]{4,3,2,1,0:T(8,128)(2,1)S(1)}, bf16[1,14,1,256,256]{4,3,2,1,0:T(8,128)(2,1)}, u32[]{:S(2)}) copy-start(bf16[1,14,1,256,256]{4,3,2,1,0:T(8,128)(2,1)} %param.8) | copy-start | bytes 5505028
  3.4 9.7 %collective-permute-start.1 = (bf16[2,256,256]{2,1,0:T(8,128)(2,1)}, bf16[2,256,256]{2,1,0:T(8,128)(2,1)S(1)}, u32[]{:S(2)}, u32[]{:S(2)}) collective-permute-start(bf16[2,256,256]{2,1,0:T(8,128)(2,1)} %get-tuple-element.25.half_a), channel_id=1, source_target_pairs={{0,1},{1,2},{2,3},{3,0},{4,5},{5,6},{6,7},{7,4},{8,9},{9,10},{10,1... | collective-permute-start | bytes 786440 | tf_op jit(solution)/shard_map/ppermute | solution.py:29
  5.2 9.6 %collective-permute-start.8 = (bf16[2,256,256]{2,1,0:T(8,128)(2,1)}, bf16[2,256,256]{2,1,0:T(8,128)(2,1)S(1)}, u32[]{:S(2)}, u32[]{:S(2)}) collective-permute-start(bf16[2,256,256]{2,1,0:T(8,128)(2,1)} %get-tuple-element.26.half_b), channel_id=1, source_target_pairs={{0,12},{1,13},{2,14},{3,15},{4,0},{5,1},{6,2},{7,3},{8,4},{9,5},{1... | collective-permute-start | bytes 786440 | tf_op jit(solution)/shard_map/ppermute | solution.py:29
  9.2 9.2 %collective-permute-start.4 = (bf16[2,256,256]{2,1,0:T(8,128)(2,1)}, bf16[2,256,256]{2,1,0:T(8,128)(2,1)S(1)}, u32[]{:S(2)}, u32[]{:S(2)}) collective-permute-start(bf16[2,256,256]{2,1,0:T(8,128)(2,1)} %get-tuple-element.26.half_b), channel_id=1, source_target_pairs={{0,4},{1,5},{2,6},{3,7},{4,8},{5,9},{6,10},{7,11},{8,12},{9,13},{1... | collective-permute-start | bytes 786440 | tf_op jit(solution)/shard_map/ppermute | solution.py:29
  9.2 9.2 %collective-permute-start.2 = (bf16[2,256,256]{2,1,0:T(8,128)(2,1)}, bf16[2,256,256]{2,1,0:T(8,128)(2,1)S(1)}, u32[]{:S(2)}, u32[]{:S(2)}) collective-permute-start(bf16[2,256,256]{2,1,0:T(8,128)(2,1)} %get-tuple-element.25.half_a), channel_id=1, source_target_pairs={{0,3},{1,0},{2,1},{3,2},{4,7},{5,4},{6,5},{7,6},{8,11},{9,8},{10,9... | collective-permute-start | bytes 786440 | tf_op jit(solution)/shard_map/ppermute | solution.py:29
  10.9 1.0 %copy-start.1 = (bf16[2,256,256]{2,1,0:T(8,128)(2,1)S(1)}, bf16[2,256,256]{2,1,0:T(8,128)(2,1)}, u32[]{:S(2)}) copy-start(bf16[2,256,256]{2,1,0:T(8,128)(2,1)} %get-tuple-element.25.half_a) | copy-start | bytes 786436
  11.8 0.9 %copy-start.2 = (bf16[2,256,256]{2,1,0:T(8,128)(2,1)S(1)}, bf16[2,256,256]{2,1,0:T(8,128)(2,1)}, u32[]{:S(2)}) copy-start(bf16[2,256,256]{2,1,0:T(8,128)(2,1)} %get-tuple-element.26.half_b) | copy-start | bytes 786436
  14.8 15.0 %collective-permute-start.9 = (bf16[2,2,256,256]{3,2,1,0:T(8,128)(2,1)S(1)}, bf16[2,2,256,256]{3,2,1,0:T(8,128)(2,1)S(1)}, u32[]{:S(2)}, u32[]{:S(2)}) collective-permute-start(bf16[2,2,256,256]{3,2,1,0:T(8,128)(2,1)S(1)} %pad_maximum_fusion.2.refs_0_), channel_id=1, source_target_pairs={{0,12},{1,13},{2,14},{3,15},{4,0},{5,1},{6,2},{7,3},{8,4},{9,5},{1... | collective-permute-start | bytes 1572872 | tf_op jit(solution)/shard_map/ppermute | solution.py:29
  18.4 14.7 %collective-permute-start.13 = (bf16[2,2,256,256]{3,2,1,0:T(8,128)(2,1)S(1)}, bf16[2,2,256,256]{3,2,1,0:T(8,128)(2,1)S(1)}, u32[]{:S(2)}, u32[]{:S(2)}) collective-permute-start(bf16[2,2,256,256]{3,2,1,0:T(8,128)(2,1)S(1)} %pad_maximum_fusion.4.refs_6_.refs_8_), channel_id=1, source_target_pairs={{0,3},{1,0},{2,1},{3,2},{4,7},{5,4},{6,5},{7,6},{8,11},{9,8},{10,9... | collective-permute-start | bytes 1572872 | tf_op jit(solution)/shard_map/ppermute | solution.py:29
  20.3 7.7 %collective-permute-start.3 = (bf16[2,256,256]{2,1,0:T(8,128)(2,1)S(1)}, bf16[2,256,256]{2,1,0:T(8,128)(2,1)S(1)}, u32[]{:S(2)}, u32[]{:S(2)}) collective-permute-start(bf16[2,256,256]{2,1,0:T(8,128)(2,1)S(1)} %collective-permute-done.1), channel_id=1, source_target_pairs={{0,1},{1,2},{2,3},{3,0},{4,5},{5,6},{6,7},{7,4},{8,9},{9,10},{10,1... | collective-permute-start | bytes 786440 | tf_op jit(solution)/shard_map/ppermute | solution.py:29
  20.5 7.6 %collective-permute-start.5 = (bf16[2,256,256]{2,1,0:T(8,128)(2,1)S(1)}, bf16[2,256,256]{2,1,0:T(8,128)(2,1)S(1)}, u32[]{:S(2)}, u32[]{:S(2)}) collective-permute-start(bf16[2,256,256]{2,1,0:T(8,128)(2,1)S(1)} %collective-permute-done.4), channel_id=1, source_target_pairs={{0,4},{1,5},{2,6},{3,7},{4,8},{5,9},{6,10},{7,11},{8,12},{9,13},{1... | collective-permute-start | bytes 786440 | tf_op jit(solution)/shard_map/ppermute | solution.py:29
  20.5 33.3 %collective-permute-start = (bf16[1,14,1,256,256]{4,3,2,1,0:T(8,128)(2,1)S(1)}, bf16[1,14,1,256,256]{4,3,2,1,0:T(8,128)(2,1)S(1)}, u32[]{:S(2)}, u32[]{:S(2)}) collective-permute-start(bf16[1,14,1,256,256]{4,3,2,1,0:T(8,128)(2,1)S(1)} %copy-done.6), channel_id=1, source_target_pairs={{0,16},{16,0},{32,48},{48,32},{64,80},{80,64},{96,112},{112,96},{1... | collective-permute-start | bytes 5505032 | tf_op jit(solution)/shard_map/ppermute | solution.py:330
  28.1 12.2 %collective-permute-start.6 = (bf16[2,2,256,256]{3,2,1,0:T(8,128)(2,1)S(1)}, bf16[2,2,256,256]{3,2,1,0:T(8,128)(2,1)S(1)}, u32[]{:S(2)}, u32[]{:S(2)}) collective-permute-start(bf16[2,2,256,256]{3,2,1,0:T(8,128)(2,1)S(1)} %pad_maximum_fusion.2.refs_0_), channel_id=1, source_target_pairs={{0,4},{1,5},{2,6},{3,7},{4,8},{5,9},{6,10},{7,11},{8,12},{9,13},{1... | collective-permute-start | bytes 1572872 | tf_op jit(solution)/shard_map/ppermute | solution.py:29
  28.1 12.2 %collective-permute-start.11 = (bf16[2,2,256,256]{3,2,1,0:T(8,128)(2,1)S(1)}, bf16[2,2,256,256]{3,2,1,0:T(8,128)(2,1)S(1)}, u32[]{:S(2)}, u32[]{:S(2)}) collective-permute-start(bf16[2,2,256,256]{3,2,1,0:T(8,128)(2,1)S(1)} %pad_maximum_fusion.4.refs_6_.refs_8_), channel_id=1, source_target_pairs={{0,1},{1,2},{2,3},{3,0},{4,5},{5,6},{6,7},{7,4},{8,9},{9,10},{10,1... | collective-permute-start | bytes 1572872 | tf_op jit(solution)/shard_map/ppermute | solution.py:29
  29.8 17.1 %collective-permute-start.10 = (bf16[2,2,256,256]{3,2,1,0:T(8,128)(2,1)S(1)}, bf16[2,2,256,256]{3,2,1,0:T(8,128)(2,1)S(1)}, u32[]{:S(2)}, u32[]{:S(2)}) collective-permute-start(bf16[2,2,256,256]{3,2,1,0:T(8,128)(2,1)S(1)} %pad_maximum_fusion.3.refs_1_), channel_id=1, source_target_pairs={{0,12},{1,13},{2,14},{3,15},{4,0},{5,1},{6,2},{7,3},{8,4},{9,5},{1... | collective-permute-start | bytes 1572872 | tf_op jit(solution)/shard_map/ppermute | solution.py:29
  33.1 11.8 %collective-permute-start.14 = (bf16[2,2,256,256]{3,2,1,0:T(8,128)(2,1)S(1)}, bf16[2,2,256,256]{3,2,1,0:T(8,128)(2,1)S(1)}, u32[]{:S(2)}, u32[]{:S(2)}) collective-permute-start(bf16[2,2,256,256]{3,2,1,0:T(8,128)(2,1)S(1)} %pad_maximum_fusion.5.refs_7_.refs_9_), channel_id=1, source_target_pairs={{0,3},{1,0},{2,1},{3,2},{4,7},{5,4},{6,5},{7,6},{8,11},{9,8},{10,9... | collective-permute-start | bytes 1572872 | tf_op jit(solution)/shard_map/ppermute | solution.py:29
  40.3 12.1 %collective-permute-start.7 = (bf16[2,2,256,256]{3,2,1,0:T(8,128)(2,1)S(1)}, bf16[2,2,256,256]{3,2,1,0:T(8,128)(2,1)S(1)}, u32[]{:S(2)}, u32[]{:S(2)}) collective-permute-start(bf16[2,2,256,256]{3,2,1,0:T(8,128)(2,1)S(1)} %pad_maximum_fusion.3.refs_1_), channel_id=1, source_target_pairs={{0,4},{1,5},{2,6},{3,7},{4,8},{5,9},{6,10},{7,11},{8,12},{9,13},{1... | collective-permute-start | bytes 1572872 | tf_op jit(solution)/shard_map/ppermute | solution.py:29
  40.3 12.1 %collective-permute-start.12 = (bf16[2,2,256,256]{3,2,1,0:T(8,128)(2,1)S(1)}, bf16[2,2,256,256]{3,2,1,0:T(8,128)(2,1)S(1)}, u32[]{:S(2)}, u32[]{:S(2)}) collective-permute-start(bf16[2,2,256,256]{3,2,1,0:T(8,128)(2,1)S(1)} %pad_maximum_fusion.5.refs_7_.refs_9_), channel_id=1, source_target_pairs={{0,1},{1,2},{2,3},{3,0},{4,5},{5,6},{6,7},{7,4},{8,9},{9,10},{10,1... | collective-permute-start | bytes 1572872 | tf_op jit(solution)/shard_map/ppermute | solution.py:29
  44.9 8.9 %copy-start = (bf16[1,16,1,256,256]{4,3,2,1,0:T(8,128)(2,1)S(1)}, bf16[1,16,1,256,256]{4,3,2,1,0:T(8,128)(2,1)}, u32[]{:S(2)}) copy-start(bf16[1,16,1,256,256]{4,3,2,1,0:T(8,128)(2,1)} %wave.1) | copy-start | bytes 6291460
  44.9 8.9 %copy-start.3 = (s32[16,4]{0,1:T(4,128)S(1)}, s32[16,4]{0,1:T(4,128)}, u32[]{:S(2)}) copy-start(s32[16,4]{0,1:T(4,128)} %param.9) | copy-start | bytes 772
  45.0 9.0 %copy-start.4 = (s32[1,2,16]{2,1,0:T(2,128)S(1)}, s32[1,2,16]{2,1,0:T(2,128)}, u32[]{:S(2)}) copy-start(s32[1,2,16]{2,1,0:T(2,128)} %sizes.3) | copy-start | bytes 388
  45.0 9.0 %copy-start.5 = (s32[16,4]{0,1:T(4,128)S(1)}, s32[16,4]{0,1:T(4,128)}, u32[]{:S(2)}) copy-start(s32[16,4]{0,1:T(4,128)} %param.10) | copy-start | bytes 772
  45.0 16.4 %collective-permute-start.18 = (bf16[5,256,256]{2,1,0:T(8,128)(2,1)S(1)}, bf16[5,256,256]{2,1,0:T(8,128)(2,1)S(1)}, u32[]{:S(2)}, u32[]{:S(2)}) collective-permute-start(bf16[5,256,256]{2,1,0:T(8,128)(2,1)S(1)} %pad_maximum_fusion.1), channel_id=1, source_target_pairs={{0,3},{1,0},{2,1},{3,2},{4,7},{5,4},{6,5},{7,6},{8,11},{9,8},{10,9... | collective-permute-start | bytes 1966088 | tf_op jit(solution)/shard_map/ppermute | solution.py:29
  46.9 14.5 %collective-permute-start.16 = (bf16[5,256,256]{2,1,0:T(8,128)(2,1)S(1)}, bf16[5,256,256]{2,1,0:T(8,128)(2,1)S(1)}, u32[]{:S(2)}, u32[]{:S(2)}) collective-permute-start(bf16[5,256,256]{2,1,0:T(8,128)(2,1)S(1)} %pad_maximum_fusion), channel_id=1, source_target_pairs={{0,12},{1,13},{2,14},{3,15},{4,0},{5,1},{6,2},{7,3},{8,4},{9,5},{1... | collective-permute-start | bytes 1966088 | tf_op jit(solution)/shard_map/ppermute | solution.py:29
  52.4 9.0 %collective-permute-start.15 = (bf16[3,256,256]{2,1,0:T(8,128)(2,1)S(1)}, bf16[3,256,256]{2,1,0:T(8,128)(2,1)S(1)}, u32[]{:S(2)}, u32[]{:S(2)}) collective-permute-start(bf16[3,256,256]{2,1,0:T(8,128)(2,1)S(1)} %pad_maximum_fusion.6), channel_id=1, source_target_pairs={{0,4},{1,5},{2,6},{3,7},{4,8},{5,9},{6,10},{7,11},{8,12},{9,13},{1... | collective-permute-start | bytes 1179656 | tf_op jit(solution)/shard_map/ppermute | solution.py:29
  52.4 9.0 %collective-permute-start.17 = (bf16[3,256,256]{2,1,0:T(8,128)(2,1)S(1)}, bf16[3,256,256]{2,1,0:T(8,128)(2,1)S(1)}, u32[]{:S(2)}, u32[]{:S(2)}) collective-permute-start(bf16[3,256,256]{2,1,0:T(8,128)(2,1)S(1)} %pad_maximum_fusion.7), channel_id=1, source_target_pairs={{0,1},{1,2},{2,3},{3,0},{4,5},{5,6},{6,7},{7,4},{8,9},{9,10},{10,1... | collective-permute-start | bytes 1179656 | tf_op jit(solution)/shard_map/ppermute | solution.py:29

commit v4 on v3

--- a/solution.py
+++ b/solution.py
@@ -33,7 +33,7 @@
     return lax.optimization_barrier((value, *results))[0]
 
 
-def gather_halves(half_a, half_b, stage_a, stage_b):
+def gather_halves(half_a, half_b, stage_a, stage_b, gate):
     own, kept = (half_a, half_b), (stage_a, stage_b)
     first, second = ("y", "z"), ("z", "y")
     near = {(i, step): send(own[i], first[i], step) for i in range(2) for step in (1, -1)}
@@ -62,7 +62,7 @@
                 high_next[i, 1],
                 low_next[i, -1],
                 high_next[i, -1],
-                send(after(up, high_next[i, 1]), second[i], 1),
+                send(after(up, high_next[i, 1], gate), second[i], 1),
                 send(down, second[i], -1),
             ]
         )
@@ -118,10 +118,18 @@
     return of_half[2 * second_at + first_at // 2][first_at % 2, k % 2]
 
 
-def row_image(a, z_at, y_at, ks, terms, sources, vector, right, pieces):
-    inner = [inner_product(a, k, terms, sources, vector, right) for k in ks]
-    blocks = [left_block(pieces, z_at, y_at, k) for k in ks]
-    return dot(jnp.concatenate(blocks, axis=1), jnp.concatenate(inner, axis=0))
+def left_row(pieces, z_at, y_at, ks):
+    return jnp.concatenate([left_block(pieces, z_at, y_at, k) for k in ks], axis=1)
+
+
+def row_image(a, z_at, y_at, terms, sources, vector, right, pieces):
+    inner = [inner_product(a, k, terms, sources, vector, right) for k in range(4)]
+    return dot(left_row(pieces, z_at, y_at, range(4)), jnp.concatenate(inner, axis=0))
+
+
+def inner_rows(inner, z_at, y_at, ks):
+    at = 4 * (4 * z_at + y_at) + ks[0]
+    return inner[at : at + len(ks)].reshape(len(ks) * inner.shape[1], inner.shape[2])
 
 
 WHOLE = [(z_at, y_at) for z_at in range(3) for y_at in range(3)]
@@ -132,20 +140,15 @@
     return ((0, 1) if z_at == 3 else ()) + ((2, 3) if y_at == 3 else ())
 
 
-LATE_INNER = [(at, k) for at in LATE for k in late_ks(*at)]
-
-
 def spread(total):
     return jnp.broadcast_to(jnp.sum(total, keepdims=True), (1, 128))
 
 
-def first_kernel(sector, terms, sources, sizes, wave, right, *refs):
-    pieces, (masked, right_live, field, part, inner, sums), (image,) = refs[:12], refs[12:18], refs[18:]
-    size = image.shape[-1]
+def inner_kernel(sector, terms, sources, sizes, wave, right, masked, right_live, inner, sums):
+    size = inner.shape[-1]
     me = sector[0]
     rows = lax.broadcasted_iota(jnp.int32, (size, size), 0)
     col_keep = lax.broadcasted_iota(jnp.int32, (size, size), 1) < sizes[0, 1, me]
-    zero = jnp.zeros((8, size), jnp.float32)
 
     def mask_right(t, carry):
         right_live[t] = jnp.where(col_keep, right[0, t, 0].astype(jnp.float32), 0.0).astype(jnp.bfloat16)
@@ -158,38 +161,45 @@
         return ww + fold(w * w)
 
     lax.fori_loop(0, right_live.shape[0], mask_right, 0)
-    ww = lax.fori_loop(0, masked.shape[0], mask_wave, zero)
-
+    ww = lax.fori_loop(0, masked.shape[0], mask_wave, jnp.zeros((8, size), jnp.float32))
+    for z_at in range(4):
+        for y_at in range(4):
+            a = left_sector(me, z_at, y_at)
+            for k in range(4):
+                inner[4 * (4 * z_at + y_at) + k] = inner_product(a, k, terms, sources, masked, right_live)
+    sums[...] = jnp.broadcast_to(spread(ww), sums.shape)
+
+
+def first_kernel(sector, masked, inner, sums_wave, *refs):
+    pieces, (field, part, sums), (image,) = refs[:12], refs[12:15], refs[15:]
+    size = image.shape[-1]
+    me = sector[0]
+    zero = jnp.zeros((8, size), jnp.float32)
     some_ww, some_wy = zero, zero
     for i, (z_at, y_at) in enumerate(WHOLE):
-        a = left_sector(me, z_at, y_at)
-        y = row_image(a, z_at, y_at, (0, 1, 2, 3), terms, sources, masked, right_live, pieces)
+        ks = (0, 1, 2, 3)
+        y = dot(left_row(pieces, z_at, y_at, ks), inner_rows(inner, z_at, y_at, ks))
         image[i] = y
-        w = masked[a].astype(jnp.float32)
+        w = masked[left_sector(me, z_at, y_at)].astype(jnp.float32)
         some_ww += fold(w * w)
         some_wy += fold(w * y)
     for i, (z_at, y_at) in enumerate(LATE[:6]):
-        a = left_sector(me, z_at, y_at)
         ks = (2, 3) if z_at == 3 else (0, 1)
-        part[i] = row_image(a, z_at, y_at, ks, terms, sources, masked, right_live, pieces)
-    for i, ((z_at, y_at), k) in enumerate(LATE_INNER):
-        a = left_sector(me, z_at, y_at)
-        inner[i] = inner_product(a, k, terms, sources, masked, right_live)
+        part[i] = dot(left_row(pieces, z_at, y_at, ks), inner_rows(inner, z_at, y_at, ks))
 
     some_ww = jnp.sum(some_ww, keepdims=True)
     some_wy = jnp.sum(some_wy, keepdims=True)
     slope = jnp.where(some_ww > 0.0, some_wy / jnp.where(some_ww > 0.0, some_ww, 1.0), 0.0)
     wu, uu = zero, zero
     for i, (z_at, y_at) in enumerate(WHOLE):
-        a = left_sector(me, z_at, y_at)
-        w = masked[a].astype(jnp.float32)
+        w = masked[left_sector(me, z_at, y_at)].astype(jnp.float32)
         u = (image[i] - slope * w).astype(jnp.bfloat16)
         field[i] = u
         u = u.astype(jnp.float32)
         wu += fold(w * u)
         uu += fold(u * u)
     slope = jnp.broadcast_to(slope, (1, 128))
-    sums[...] = jnp.concatenate([spread(ww), spread(wu), spread(uu)] + [slope] * 5, axis=0)
+    sums[...] = jnp.concatenate([sums_wave[0:1], spread(wu), spread(uu)] + [slope] * 5, axis=0)
 
 
 def second_kernel(sector, terms, sources, masked, right_live, field_some, part, inner, sums_first, *refs):
@@ -199,14 +209,10 @@
     zero = jnp.zeros((8, size), jnp.float32)
     slope = sums_first[3:4, :1]
     wu, uu = zero, zero
-    at = 0
     for i, (z_at, y_at) in enumerate(LATE):
         a = left_sector(me, z_at, y_at)
         ks = late_ks(z_at, y_at)
-        blocks = [left_block(pieces, z_at, y_at, k) for k in ks]
-        late_inner = jnp.concatenate([inner[at + j] for j in range(len(ks))], axis=0)
-        at += len(ks)
-        y = dot(jnp.concatenate(blocks, axis=1), late_inner)
+        y = dot(left_row(pieces, z_at, y_at, ks), inner_rows(inner, z_at, y_at, ks))
         if i < 6:
             y += part[i]
         w = masked[a].astype(jnp.float32)
@@ -222,7 +228,7 @@
     for z_at in range(4):
         for y_at in range(4):
             a = left_sector(me, z_at, y_at)
-            v = row_image(a, z_at, y_at, (0, 1, 2, 3), terms, sources, field, right_live, pieces)
+            v = row_image(a, z_at, y_at, terms, sources, field, right_live, pieces)
             image[a] = v
             wv += fold(masked[a].astype(jnp.float32) * v)
             uv += fold(field[a].astype(jnp.float32) * v)
@@ -323,31 +329,35 @@
         cost_estimate=pl.CostEstimate(flops=1 << 20, bytes_accessed=MIB, transcendentals=0),
         name="stage",
     )(half_a, half_b)
-    pieces_a, pieces_b = gather_halves(half_a, half_b, stage_a, stage_b)
-    early = pieces_a[:6] + pieces_b[:6]
-    every = pieces_a + pieces_b
     count = lax.axis_size("section")
     partner = lax.ppermute(
         right_env, "section", [(s, s ^ 1) for s in range(count)]
     )
 
     flop = 2 * size * size * size
-    masked, right_live, field_some, part, inner, sums_first = pl.pallas_call(
+    row = jax.ShapeDtypeStruct((8, 128), f32)
+    masked, right_live, inner, sums_wave = pl.pallas_call(
+        inner_kernel,
+        out_shape=(blocks(sectors, bf16), blocks(terms_count, bf16), blocks(4 * sectors, bf16), row),
+        in_specs=[smem] * 4 + [vmem] * 2,
+        out_specs=(vmem,) * 4,
+        compiler_params=pltpu.CompilerParams(vmem_limit_bytes=16 * MIB),
+        cost_estimate=pl.CostEstimate(flops=64 * flop, bytes_accessed=12 * MIB, transcendentals=0),
+        name="inner_products",
+    )(sector, terms, sources, live_sizes, wavefunction, partner)
+
+    pieces_a, pieces_b = gather_halves(half_a, half_b, stage_a, stage_b, sums_wave)
+    early = pieces_a[:6] + pieces_b[:6]
+    every = pieces_a + pieces_b
+    field_some, part, sums_first = pl.pallas_call(
         first_kernel,
-        out_shape=(
-            blocks(sectors, bf16),
-            blocks(terms_count, bf16),
-            blocks(len(WHOLE), bf16),
-            blocks(6, f32),
-            blocks(len(LATE_INNER), bf16),
-            jax.ShapeDtypeStruct((8, 128), f32),
-        ),
-        in_specs=[smem] * 4 + [vmem] * 14,
-        out_specs=(vmem,) * 6,
+        out_shape=(blocks(len(WHOLE), bf16), blocks(6, f32), row),
+        in_specs=[smem] + [vmem] * 15,
+        out_specs=(vmem,) * 3,
         scratch_shapes=[pltpu.VMEM((len(WHOLE), size, size), f32)],
-        compiler_params=pltpu.CompilerParams(vmem_limit_bytes=20 * MIB),
+        compiler_params=pltpu.CompilerParams(vmem_limit_bytes=12 * MIB),
         name="first_image",
-    )(sector, terms, sources, live_sizes, wavefunction, partner, *early)
+    )(sector, masked, inner, sums_wave, *early)
 
     field, image, sums = pl.pallas_call(
         second_kernel,

time: 85.4 us -> 84.3 us (0.987)
  blocking collectives: 14.5 us -> 12.2 us
  waiting for transfers between devices: 21.7 us -> 23.3 us
    all_to_all x1, blocking collectives: 14.5 us -> 12.2 us  [per_device(): gathered = lax.all_to_all(sums, 'sector', 0, 0)]
    ppermute x18, waiting for transfers between devices: 21.7 us -> 23.3 us  [send(): return lax.ppermute(block, 'sector', along(axis, step))]
    pallas_call x1 -> x2, Pallas kernels: 7.5 us -> 7.51 us  [the longest x1 4.25 us: per_device(): pl.pallas_call(inner_kernel, out_shape=(blocks(sectors, bf16), blocks(ter...]
  transfers between devices with their start and end apart: 19 -> 19, of which waited for: 7 -> 10; matrix products, arithmetic and copies ran while one was open for 1% -> 1% of each run, Pallas kernels for 9% -> 9%
where the time goes in v4:
time: 84.3 us; the launch traced here: 84 us
  starting transfers between devices  25.5 us (30%)
  waiting for transfers between devices  23.3 us (28%)
  Pallas kernels  19.7 us (23%)
  blocking collectives  12.2 us (14%)
  local copies, waits for them, and re-layouts  2.04 us (2%)
  between operations  0.88 us (1%)
    ppermute x18, starting transfers between devices, send(): return lax.ppermute(block, 'sector', along(axis, step))  25.5 us
    ppermute x18, waiting for transfers between devices, send(): return lax.ppermute(block, 'sector', along(axis, step))  23.3 us
    all_to_all x1, blocking collectives, per_device(): gathered = lax.all_to_all(sums, 'sector', 0, 0)  12.2 us
    pallas_call x1, Pallas kernels, per_device(): pl.pallas_call(second_kernel, out_shape=(blocks(sectors, bf16), blocks(se...  6.74 us
    pallas_call x1, Pallas kernels, per_device(): pl.pallas_call(inner_kernel, out_shape=(blocks(sectors, bf16), blocks(ter...  4.25 us
    pallas_call x1, Pallas kernels, per_device(): pl.pallas_call(first_kernel, out_shape=(blocks(len(WHOLE), bf16), blocks(...  3.25 us
    pallas_call x1, Pallas kernels, per_device(): pl.pallas_call(pick_kernel, out_shape=(blocks(2, bf16), blocks(2, bf16)),...  2.78 us
    pallas_call x1, Pallas kernels, per_device(): pl.pallas_call(functools.partial(last_kernel, cells), grid=(sectors // pe...  2.59 us
  transfers between devices with their start and end apart: 19, of which 10 were waited for; matrix products, arithmetic and copies ran while one was open for 1% of the time, Pallas kernels for 9%

profile of v4, /device:TPU:0, one launch (start us, length us, event | category | flops | bytes accessed | tf_op | source)
XLA Modules:
  0.0 84.0 jit_solution(16981289788440868017)
XLA Ops:
  0.6 0.0 copy-start.6
  0.6 2.8 %pick_left.1 = (bf16[2,256,256]{2,1,0:T(8,128)(2,1)}, bf16[2,256,256]{2,1,0:T(8,128)(2,1)}) custom-call(s32[1]{0:T(128)} %bitcast.sector, s32[4,16]{1,0:T(4,128)} %bitcast.29, s32[1,2,16]{2,1,0:T(2,128)} %sizes.3, bf16[1,14,1,256,256]{4,3,2,1,0:T(8,128)(2,1)} %left.1), custom_call_target="tpu_custom_call" | custom-call | tf_op jit(solution)/shard_map/pick_left/pallas_call | solution.py:313
  3.4 1.7 %collective-permute-start.1 = (bf16[2,256,256]{2,1,0:T(8,128)(2,1)}, bf16[2,256,256]{2,1,0:T(8,128)(2,1)S(1)}, u32[]{:S(2)}, u32[]{:S(2)}) collective-permute-start(bf16[2,256,256]{2,1,0:T(8,128)(2,1)} %get-tuple-element.30.half_a), channel_id=1, source_target_pairs={{0,1},{1,2},{2,3},{3,0},{4,5},{5,6},{6,7},{7,4},{8,9},{9,10},{10,1... | collective-permute-start | bytes 786440 | tf_op jit(solution)/shard_map/ppermute | solution.py:29
  5.2 4.0 %collective-permute-start.8 = (bf16[2,256,256]{2,1,0:T(8,128)(2,1)}, bf16[2,256,256]{2,1,0:T(8,128)(2,1)S(1)}, u32[]{:S(2)}, u32[]{:S(2)}) collective-permute-start(bf16[2,256,256]{2,1,0:T(8,128)(2,1)} %get-tuple-element.31.half_b), channel_id=1, source_target_pairs={{0,12},{1,13},{2,14},{3,15},{4,0},{5,1},{6,2},{7,3},{8,4},{9,5},{1... | collective-permute-start | bytes 786440 | tf_op jit(solution)/shard_map/ppermute | solution.py:29
  9.2 0.0 collective-permute-start.4
  9.2 1.7 %collective-permute-start.2 = (bf16[2,256,256]{2,1,0:T(8,128)(2,1)}, bf16[2,256,256]{2,1,0:T(8,128)(2,1)S(1)}, u32[]{:S(2)}, u32[]{:S(2)}) collective-permute-start(bf16[2,256,256]{2,1,0:T(8,128)(2,1)} %get-tuple-element.30.half_a), channel_id=1, source_target_pairs={{0,3},{1,0},{2,1},{3,2},{4,7},{5,4},{6,5},{7,6},{8,11},{9,8},{10,9... | collective-permute-start | bytes 786440 | tf_op jit(solution)/shard_map/ppermute | solution.py:29
  10.9 0.0 copy-start
  10.9 1.0 %copy-done = bf16[2,256,256]{2,1,0:T(8,128)(2,1)S(1)} copy-done((bf16[2,256,256]{2,1,0:T(8,128)(2,1)S(1)}, bf16[2,256,256]{2,1,0:T(8,128)(2,1)}, u32[]{:S(2)}) %copy-start) | copy-done | bytes 262168
  11.8 0.0 copy-start.1
  11.8 0.9 %copy-done.1 = bf16[2,256,256]{2,1,0:T(8,128)(2,1)S(1)} copy-done((bf16[2,256,256]{2,1,0:T(8,128)(2,1)S(1)}, bf16[2,256,256]{2,1,0:T(8,128)(2,1)}, u32[]{:S(2)}) %copy-start.1) | copy-done | bytes 262168
  12.8 0.3 collective-permute-done.1
  13.1 0.1 pad_maximum_fusion.2.refs_0_
  13.2 1.6 %collective-permute-done.8 = bf16[2,256,256]{2,1,0:T(8,128)(2,1)S(1)} collective-permute-done((bf16[2,256,256]{2,1,0:T(8,128)(2,1)}, bf16[2,256,256]{2,1,0:T(8,128)(2,1)S(1)}, u32[]{:S(2)}, u32[]{:S(2)}) %collective-permute-start.8) | collective-permute-done | bytes 262176 | tf_op jit(solution)/shard_map/ppermute | solution.py:29
  14.8 3.6 %collective-permute-start.9 = (bf16[2,2,256,256]{3,2,1,0:T(8,128)(2,1)S(1)}, bf16[2,2,256,256]{3,2,1,0:T(8,128)(2,1)S(1)}, u32[]{:S(2)}, u32[]{:S(2)}) collective-permute-start(bf16[2,2,256,256]{3,2,1,0:T(8,128)(2,1)S(1)} %pad_maximum_fusion.2.refs_0_), channel_id=1, source_target_pairs={{0,12},{1,13},{2,14},{3,15},{4,0},{5,1},{6,2},{7,3},{8,4},{9,5},{1... | collective-permute-start | bytes 1572872 | tf_op jit(solution)/shard_map/ppermute | solution.py:29
  18.4 0.0 collective-permute-done.4
  18.4 0.1 pad_maximum_fusion.4.refs_6_.refs_8_
  18.4 0.0 collective-permute-done.2
  18.5 1.9 %collective-permute-start.13 = (bf16[2,2,256,256]{3,2,1,0:T(8,128)(2,1)S(1)}, bf16[2,2,256,256]{3,2,1,0:T(8,128)(2,1)S(1)}, u32[]{:S(2)}, u32[]{:S(2)}) collective-permute-start(bf16[2,2,256,256]{3,2,1,0:T(8,128)(2,1)S(1)} %pad_maximum_fusion.4.refs_6_.refs_8_), channel_id=1, source_target_pairs={{0,3},{1,0},{2,1},{3,2},{4,7},{5,4},{6,5},{7,6},{8,11},{9,8},{10,9... | collective-permute-start | bytes 1572872 | tf_op jit(solution)/shard_map/ppermute | solution.py:29
  20.3 0.2 collective-permute-start.3
  20.5 0.0 collective-permute-start.5
  20.5 0.0 copy-done.6
  20.6 0.0 collective-permute-start
  20.6 7.4 %collective-permute-done.3 = bf16[2,256,256]{2,1,0:T(8,128)(2,1)S(1)} collective-permute-done((bf16[2,256,256]{2,1,0:T(8,128)(2,1)S(1)}, bf16[2,256,256]{2,1,0:T(8,128)(2,1)S(1)}, u32[]{:S(2)}, u32[]{:S(2)}) %collective-permute-start.3) | collective-permute-done | bytes 262176 | tf_op jit(solution)/shard_map/ppermute | solution.py:29
  28.0 0.1 collective-permute-done.5
  28.1 0.0 collective-permute-start.6
  28.1 1.6 %collective-permute-start.11 = (bf16[2,2,256,256]{3,2,1,0:T(8,128)(2,1)S(1)}, bf16[2,2,256,256]{3,2,1,0:T(8,128)(2,1)S(1)}, u32[]{:S(2)}, u32[]{:S(2)}) collective-permute-start(bf16[2,2,256,256]{3,2,1,0:T(8,128)(2,1)S(1)} %pad_maximum_fusion.4.refs_6_.refs_8_), channel_id=1, source_target_pairs={{0,1},{1,2},{2,3},{3,0},{4,5},{5,6},{6,7},{7,4},{8,9},{9,10},{10,1... | collective-permute-start | bytes 1572872 | tf_op jit(solution)/shard_map/ppermute | solution.py:29
  29.7 0.1 pad_maximum_fusion.5.refs_7_.refs_9_
  29.8 0.1 pad_maximum_fusion.3.refs_1_
  29.8 0.0 collective-permute-done.9.refs_4_
  29.8 3.3 %collective-permute-start.10 = (bf16[2,2,256,256]{3,2,1,0:T(8,128)(2,1)S(1)}, bf16[2,2,256,256]{3,2,1,0:T(8,128)(2,1)S(1)}, u32[]{:S(2)}, u32[]{:S(2)}) collective-permute-start(bf16[2,2,256,256]{3,2,1,0:T(8,128)(2,1)S(1)} %pad_maximum_fusion.3.refs_1_), channel_id=1, source_target_pairs={{0,12},{1,13},{2,14},{3,15},{4,0},{5,1},{6,2},{7,3},{8,4},{9,5},{1... | collective-permute-start | bytes 1572872 | tf_op jit(solution)/shard_map/ppermute | solution.py:29
  33.1 0.0 collective-permute-done.13.refs_10_.refs_12_
  33.1 1.7 %collective-permute-start.14 = (bf16[2,2,256,256]{3,2,1,0:T(8,128)(2,1)S(1)}, bf16[2,2,256,256]{3,2,1,0:T(8,128)(2,1)S(1)}, u32[]{:S(2)}, u32[]{:S(2)}) collective-permute-start(bf16[2,2,256,256]{3,2,1,0:T(8,128)(2,1)S(1)} %pad_maximum_fusion.5.refs_7_.refs_9_), channel_id=1, source_target_pairs={{0,3},{1,0},{2,1},{3,2},{4,7},{5,4},{6,5},{7,6},{8,11},{9,8},{10,9... | collective-permute-start | bytes 1572872 | tf_op jit(solution)/shard_map/ppermute | solution.py:29
  34.8 5.5 %collective-permute-done.6.refs_2_ = bf16[2,2,256,256]{3,2,1,0:T(8,128)(2,1)S(1)} collective-permute-done((bf16[2,2,256,256]{3,2,1,0:T(8,128)(2,1)S(1)}, bf16[2,2,256,256]{3,2,1,0:T(8,128)(2,1)S(1)}, u32[]{:S(2)}, u32[]{:S(2)}) %collective-permute-start.6) | collective-permute-done | bytes 524320 | tf_op jit(solution)/shard_map/ppermute | solution.py:29
  40.3 0.0 collective-permute-start.7
  40.3 0.0 collective-permute-done.11.refs_8_.refs_10_
  40.3 1.5 %collective-permute-start.12 = (bf16[2,2,256,256]{3,2,1,0:T(8,128)(2,1)S(1)}, bf16[2,2,256,256]{3,2,1,0:T(8,128)(2,1)S(1)}, u32[]{:S(2)}, u32[]{:S(2)}) collective-permute-start(bf16[2,2,256,256]{3,2,1,0:T(8,128)(2,1)S(1)} %pad_maximum_fusion.5.refs_7_.refs_9_), channel_id=1, source_target_pairs={{0,1},{1,2},{2,3},{3,0},{4,5},{5,6},{6,7},{7,4},{8,9},{9,10},{10,1... | collective-permute-start | bytes 1572872 | tf_op jit(solution)/shard_map/ppermute | solution.py:29
  41.9 0.0 copy-start.2
  41.9 0.0 copy-start.3
  41.9 0.0 copy-start.4
  41.9 0.0 copy-start.5
  42.0 3.0 %collective-permute-done.14.refs_11_.refs_13_ = bf16[2,2,256,256]{3,2,1,0:T(8,128)(2,1)S(1)} collective-permute-done((bf16[2,2,256,256]{3,2,1,0:T(8,128)(2,1)S(1)}, bf16[2,2,256,256]{3,2,1,0:T(8,128)(2,1)S(1)}, u32[]{:S(2)}, u32[]{:S(2)}) %collective-permute-start.14) | collective-permute-done | bytes 524320 | tf_op jit(solution)/shard_map/ppermute | solution.py:29
  45.0 0.1 pad_maximum_fusion.1
  45.0 1.9 %collective-permute-start.18 = (bf16[5,256,256]{2,1,0:T(8,128)(2,1)S(1)}, bf16[5,256,256]{2,1,0:T(8,128)(2,1)S(1)}, u32[]{:S(2)}, u32[]{:S(2)}) collective-permute-start(bf16[5,256,256]{2,1,0:T(8,128)(2,1)S(1)} %pad_maximum_fusion.1), channel_id=1, source_target_pairs={{0,3},{1,0},{2,1},{3,2},{4,7},{5,4},{6,5},{7,6},{8,11},{9,8},{10,9... | collective-permute-start | bytes 1966088 | tf_op jit(solution)/shard_map/ppermute | solution.py:29
  46.9 0.0 collective-permute-done.10.refs_5_
  46.9 0.1 pad_maximum_fusion
  47.0 1.8 %collective-permute-start.16 = (bf16[5,256,256]{2,1,0:T(8,128)(2,1)S(1)}, bf16[5,256,256]{2,1,0:T(8,128)(2,1)S(1)}, u32[]{:S(2)}, u32[]{:S(2)}) collective-permute-start(bf16[5,256,256]{2,1,0:T(8,128)(2,1)S(1)} %pad_maximum_fusion), channel_id=1, source_target_pairs={{0,12},{1,13},{2,14},{3,15},{4,0},{5,1},{6,2},{7,3},{8,4},{9,5},{1... | collective-permute-start | bytes 1966088 | tf_op jit(solution)/shard_map/ppermute | solution.py:29
  48.7 0.0 collective-permute-done.right
  48.8 0.0 copy-done.2
  48.8 0.0 copy-done.3
  48.8 0.0 copy-done.4
  48.8 0.0 copy-done.5
  48.8 4.3 %inner_products.1 = (bf16[16,256,256]{2,1,0:T(8,128)(2,1)S(1)}, bf16[14,256,256]{2,1,0:T(8,128)(2,1)S(1)}, bf16[64,256,256]{2,1,0:T(8,128)(2,1)S(1)}, f32[8,128]{1,0:T(8,128)S(1)}) custom-call(s32[1]{0:T(128)} %bitcast.sector, s32[4,16]{1,0:T(4,128)S(1)} %bitcast.30, s32[4,16]{1,0:T(4,128)S(1)} %bitcast.32, s32[1,2,16]{2,1,0:T(2,128)S(1)} %copy-done.4, ...), custom_call_target="tpu_custom_call" | custom-call | flops 2147483648 | bytes 12582912 | tf_op jit(solution)/shard_map/inner_products/pallas_call | solution.py:339
  53.1 0.0 collective-permute-done.12.refs_9_.refs_11_
  53.1 0.0 collective-permute-done.7.refs_3_
  53.1 0.4 collective-permute-start.15
  53.5 0.4 collective-permute-start.17
  53.9 3.3 %first_image.1 = (bf16[9,256,256]{2,1,0:T(8,128)(2,1)S(1)}, f32[6,256,256]{2,1,0:T(8,128)S(1)}, f32[8,128]{1,0:T(8,128)S(1)}) custom-call(s32[1]{0:T(128)} %bitcast.sector, bf16[16,256,256]{2,1,0:T(8,128)(2,1)S(1)} %get-tuple-element.26.masked, bf16[64,256,256]{2,1,0:T(8,128)(2,1)S(1)} %get-tuple-element.28.inner, f32[8,128]{1,0:T(8,128)S(1)} %get-tuple-element.29.sums_wave, ...), custom_call_target="tpu_custom_call" | custom-call | tf_op jit(solution)/shard_map/first_image/pallas_call | solution.py:352
  57.2 0.2 collective-permute-done.18.refs_15_
  57.4 1.8 %collective-permute-done.16.refs_7_ = bf16[5,256,256]{2,1,0:T(8,128)(2,1)S(1)} collective-permute-done((bf16[5,256,256]{2,1,0:T(8,128)(2,1)S(1)}, bf16[5,256,256]{2,1,0:T(8,128)(2,1)S(1)}, u32[]{:S(2)}, u32[]{:S(2)}) %collective-permute-start.16) | collective-permute-done | bytes 655392 | tf_op jit(solution)/shard_map/ppermute | solution.py:29
  59.2 2.9 %collective-permute-done.15.refs_6_ = bf16[3,256,256]{2,1,0:T(8,128)(2,1)S(1)} collective-permute-done((bf16[3,256,256]{2,1,0:T(8,128)(2,1)S(1)}, bf16[3,256,256]{2,1,0:T(8,128)(2,1)S(1)}, u32[]{:S(2)}, u32[]{:S(2)}) %collective-permute-start.15) | collective-permute-done | bytes 393248 | tf_op jit(solution)/shard_map/ppermute | solution.py:29
  62.1 0.3 collective-permute-done.17.refs_14_
  62.5 6.7 %second_image.1 = (bf16[16,256,256]{2,1,0:T(8,128)(2,1)S(1)}, f32[16,256,256]{2,1,0:T(8,128)S(1)}, f32[16,8,128]{2,1,0:T(8,128)S(1)}) custom-call(s32[1]{0:T(128)} %bitcast.sector, s32[4,16]{1,0:T(4,128)S(1)} %bitcast.31, s32[4,16]{1,0:T(4,128)S(1)} %bitcast.33, bf16[16,256,256]{2,1,0:T(8,128)(2,1)S(1)} %get-tuple-element.26.masked, ...), custom_call_target="tpu_custom_call" | custom-call | flops 4831838208 | bytes 25165824 | tf_op jit(solution)/shard_map/second_image/pallas_call | solution.py:362
  69.2 12.2 %all_to_all.5.gathered = f32[16,8,128]{2,1,0:T(8,128)S(1)} all-to-all(f32[16,8,128]{2,1,0:T(8,128)S(1)} %get-tuple-element.47.own), channel_id=1, replica_groups=mesh['section'=8,'sector'=16] {'sector'}, dimensions={0} | all-to-all | bytes 131072 | tf_op jit(solution)/shard_map/all_to_all | solution.py:376
  81.4 2.6 %next_basis.1 = (f32[1,16,1,256,256]{4,3,2,1,0:T(8,128)}, f32[1,3]{1,0:T(1,128)}) custom-call(f32[16,8,128]{2,1,0:T(8,128)S(1)} %all_to_all.5.gathered, f32[16,8,128]{2,1,0:T(8,128)S(1)} %get-tuple-element.47.own, bf16[16,256,256]{2,1,0:T(8,128)(2,1)S(1)} %get-tuple-element.26.masked, bf16[16,256,256]{2,1,0:T(8,128)(2,1)S(1)} %get-tuple-element.48.field, ...), custom_call_target="tpu_custom_call" | custom-call | tf_op jit(solution)/shard_map/next_basis/pallas_call | solution.py:379
  (9 shorter events, 0.2 us)
Async XLA Ops:
  0.6 19.9 %copy-start.6 = (bf16[1,14,1,256,256]{4,3,2,1,0:T(8,128)(2,1)S(1)}, bf16[1,14,1,256,256]{4,3,2,1,0:T(8,128)(2,1)}, u32[]{:S(2)}) copy-start(bf16[1,14,1,256,256]{4,3,2,1,0:T(8,128)(2,1)} %param.8) | copy-start | bytes 5505028
  3.4 9.7 %collective-permute-start.1 = (bf16[2,256,256]{2,1,0:T(8,128)(2,1)}, bf16[2,256,256]{2,1,0:T(8,128)(2,1)S(1)}, u32[]{:S(2)}, u32[]{:S(2)}) collective-permute-start(bf16[2,256,256]{2,1,0:T(8,128)(2,1)} %get-tuple-element.30.half_a), channel_id=1, source_target_pairs={{0,1},{1,2},{2,3},{3,0},{4,5},{5,6},{6,7},{7,4},{8,9},{9,10},{10,1... | collective-permute-start | bytes 786440 | tf_op jit(solution)/shard_map/ppermute | solution.py:29
  5.2 9.6 %collective-permute-start.8 = (bf16[2,256,256]{2,1,0:T(8,128)(2,1)}, bf16[2,256,256]{2,1,0:T(8,128)(2,1)S(1)}, u32[]{:S(2)}, u32[]{:S(2)}) collective-permute-start(bf16[2,256,256]{2,1,0:T(8,128)(2,1)} %get-tuple-element.31.half_b), channel_id=1, source_target_pairs={{0,12},{1,13},{2,14},{3,15},{4,0},{5,1},{6,2},{7,3},{8,4},{9,5},{1... | collective-permute-start | bytes 786440 | tf_op jit(solution)/shard_map/ppermute | solution.py:29
  9.2 9.2 %collective-permute-start.4 = (bf16[2,256,256]{2,1,0:T(8,128)(2,1)}, bf16[2,256,256]{2,1,0:T(8,128)(2,1)S(1)}, u32[]{:S(2)}, u32[]{:S(2)}) collective-permute-start(bf16[2,256,256]{2,1,0:T(8,128)(2,1)} %get-tuple-element.31.half_b), channel_id=1, source_target_pairs={{0,4},{1,5},{2,6},{3,7},{4,8},{5,9},{6,10},{7,11},{8,12},{9,13},{1... | collective-permute-start | bytes 786440 | tf_op jit(solution)/shard_map/ppermute | solution.py:29
  9.2 9.2 %collective-permute-start.2 = (bf16[2,256,256]{2,1,0:T(8,128)(2,1)}, bf16[2,256,256]{2,1,0:T(8,128)(2,1)S(1)}, u32[]{:S(2)}, u32[]{:S(2)}) collective-permute-start(bf16[2,256,256]{2,1,0:T(8,128)(2,1)} %get-tuple-element.30.half_a), channel_id=1, source_target_pairs={{0,3},{1,0},{2,1},{3,2},{4,7},{5,4},{6,5},{7,6},{8,11},{9,8},{10,9... | collective-permute-start | bytes 786440 | tf_op jit(solution)/shard_map/ppermute | solution.py:29
  10.9 1.0 %copy-start = (bf16[2,256,256]{2,1,0:T(8,128)(2,1)S(1)}, bf16[2,256,256]{2,1,0:T(8,128)(2,1)}, u32[]{:S(2)}) copy-start(bf16[2,256,256]{2,1,0:T(8,128)(2,1)} %get-tuple-element.30.half_a) | copy-start | bytes 786436
  11.8 0.9 %copy-start.1 = (bf16[2,256,256]{2,1,0:T(8,128)(2,1)S(1)}, bf16[2,256,256]{2,1,0:T(8,128)(2,1)}, u32[]{:S(2)}) copy-start(bf16[2,256,256]{2,1,0:T(8,128)(2,1)} %get-tuple-element.31.half_b) | copy-start | bytes 786436
  14.8 15.0 %collective-permute-start.9 = (bf16[2,2,256,256]{3,2,1,0:T(8,128)(2,1)S(1)}, bf16[2,2,256,256]{3,2,1,0:T(8,128)(2,1)S(1)}, u32[]{:S(2)}, u32[]{:S(2)}) collective-permute-start(bf16[2,2,256,256]{3,2,1,0:T(8,128)(2,1)S(1)} %pad_maximum_fusion.2.refs_0_), channel_id=1, source_target_pairs={{0,12},{1,13},{2,14},{3,15},{4,0},{5,1},{6,2},{7,3},{8,4},{9,5},{1... | collective-permute-start | bytes 1572872 | tf_op jit(solution)/shard_map/ppermute | solution.py:29
  18.5 14.7 %collective-permute-start.13 = (bf16[2,2,256,256]{3,2,1,0:T(8,128)(2,1)S(1)}, bf16[2,2,256,256]{3,2,1,0:T(8,128)(2,1)S(1)}, u32[]{:S(2)}, u32[]{:S(2)}) collective-permute-start(bf16[2,2,256,256]{3,2,1,0:T(8,128)(2,1)S(1)} %pad_maximum_fusion.4.refs_6_.refs_8_), channel_id=1, source_target_pairs={{0,3},{1,0},{2,1},{3,2},{4,7},{5,4},{6,5},{7,6},{8,11},{9,8},{10,9... | collective-permute-start | bytes 1572872 | tf_op jit(solution)/shard_map/ppermute | solution.py:29
  20.3 7.7 %collective-permute-start.3 = (bf16[2,256,256]{2,1,0:T(8,128)(2,1)S(1)}, bf16[2,256,256]{2,1,0:T(8,128)(2,1)S(1)}, u32[]{:S(2)}, u32[]{:S(2)}) collective-permute-start(bf16[2,256,256]{2,1,0:T(8,128)(2,1)S(1)} %collective-permute-done.1), channel_id=1, source_target_pairs={{0,1},{1,2},{2,3},{3,0},{4,5},{5,6},{6,7},{7,4},{8,9},{9,10},{10,1... | collective-permute-start | bytes 786440 | tf_op jit(solution)/shard_map/ppermute | solution.py:29
  20.5 7.6 %collective-permute-start.5 = (bf16[2,256,256]{2,1,0:T(8,128)(2,1)S(1)}, bf16[2,256,256]{2,1,0:T(8,128)(2,1)S(1)}, u32[]{:S(2)}, u32[]{:S(2)}) collective-permute-start(bf16[2,256,256]{2,1,0:T(8,128)(2,1)S(1)} %collective-permute-done.4), channel_id=1, source_target_pairs={{0,4},{1,5},{2,6},{3,7},{4,8},{5,9},{6,10},{7,11},{8,12},{9,13},{1... | collective-permute-start | bytes 786440 | tf_op jit(solution)/shard_map/ppermute | solution.py:29
  20.6 28.2 %collective-permute-start = (bf16[1,14,1,256,256]{4,3,2,1,0:T(8,128)(2,1)S(1)}, bf16[1,14,1,256,256]{4,3,2,1,0:T(8,128)(2,1)S(1)}, u32[]{:S(2)}, u32[]{:S(2)}) collective-permute-start(bf16[1,14,1,256,256]{4,3,2,1,0:T(8,128)(2,1)S(1)} %copy-done.6), channel_id=1, source_target_pairs={{0,16},{16,0},{32,48},{48,32},{64,80},{80,64},{96,112},{112,96},{1... | collective-permute-start | bytes 5505032 | tf_op jit(solution)/shard_map/ppermute | solution.py:333
  28.1 12.2 %collective-permute-start.6 = (bf16[2,2,256,256]{3,2,1,0:T(8,128)(2,1)S(1)}, bf16[2,2,256,256]{3,2,1,0:T(8,128)(2,1)S(1)}, u32[]{:S(2)}, u32[]{:S(2)}) collective-permute-start(bf16[2,2,256,256]{3,2,1,0:T(8,128)(2,1)S(1)} %pad_maximum_fusion.2.refs_0_), channel_id=1, source_target_pairs={{0,4},{1,5},{2,6},{3,7},{4,8},{5,9},{6,10},{7,11},{8,12},{9,13},{1... | collective-permute-start | bytes 1572872 | tf_op jit(solution)/shard_map/ppermute | solution.py:29
  28.1 12.2 %collective-permute-start.11 = (bf16[2,2,256,256]{3,2,1,0:T(8,128)(2,1)S(1)}, bf16[2,2,256,256]{3,2,1,0:T(8,128)(2,1)S(1)}, u32[]{:S(2)}, u32[]{:S(2)}) collective-permute-start(bf16[2,2,256,256]{3,2,1,0:T(8,128)(2,1)S(1)} %pad_maximum_fusion.4.refs_6_.refs_8_), channel_id=1, source_target_pairs={{0,1},{1,2},{2,3},{3,0},{4,5},{5,6},{6,7},{7,4},{8,9},{9,10},{10,1... | collective-permute-start | bytes 1572872 | tf_op jit(solution)/shard_map/ppermute | solution.py:29
  29.8 17.1 %collective-permute-start.10 = (bf16[2,2,256,256]{3,2,1,0:T(8,128)(2,1)S(1)}, bf16[2,2,256,256]{3,2,1,0:T(8,128)(2,1)S(1)}, u32[]{:S(2)}, u32[]{:S(2)}) collective-permute-start(bf16[2,2,256,256]{3,2,1,0:T(8,128)(2,1)S(1)} %pad_maximum_fusion.3.refs_1_), channel_id=1, source_target_pairs={{0,12},{1,13},{2,14},{3,15},{4,0},{5,1},{6,2},{7,3},{8,4},{9,5},{1... | collective-permute-start | bytes 1572872 | tf_op jit(solution)/shard_map/ppermute | solution.py:29
  33.1 11.8 %collective-permute-start.14 = (bf16[2,2,256,256]{3,2,1,0:T(8,128)(2,1)S(1)}, bf16[2,2,256,256]{3,2,1,0:T(8,128)(2,1)S(1)}, u32[]{:S(2)}, u32[]{:S(2)}) collective-permute-start(bf16[2,2,256,256]{3,2,1,0:T(8,128)(2,1)S(1)} %pad_maximum_fusion.5.refs_7_.refs_9_), channel_id=1, source_target_pairs={{0,3},{1,0},{2,1},{3,2},{4,7},{5,4},{6,5},{7,6},{8,11},{9,8},{10,9... | collective-permute-start | bytes 1572872 | tf_op jit(solution)/shard_map/ppermute | solution.py:29
  40.3 12.7 %collective-permute-start.7 = (bf16[2,2,256,256]{3,2,1,0:T(8,128)(2,1)S(1)}, bf16[2,2,256,256]{3,2,1,0:T(8,128)(2,1)S(1)}, u32[]{:S(2)}, u32[]{:S(2)}) collective-permute-start(bf16[2,2,256,256]{3,2,1,0:T(8,128)(2,1)S(1)} %pad_maximum_fusion.3.refs_1_), channel_id=1, source_target_pairs={{0,4},{1,5},{2,6},{3,7},{4,8},{5,9},{6,10},{7,11},{8,12},{9,13},{1... | collective-permute-start | bytes 1572872 | tf_op jit(solution)/shard_map/ppermute | solution.py:29
  40.3 12.7 %collective-permute-start.12 = (bf16[2,2,256,256]{3,2,1,0:T(8,128)(2,1)S(1)}, bf16[2,2,256,256]{3,2,1,0:T(8,128)(2,1)S(1)}, u32[]{:S(2)}, u32[]{:S(2)}) collective-permute-start(bf16[2,2,256,256]{3,2,1,0:T(8,128)(2,1)S(1)} %pad_maximum_fusion.5.refs_7_.refs_9_), channel_id=1, source_target_pairs={{0,1},{1,2},{2,3},{3,0},{4,5},{5,6},{6,7},{7,4},{8,9},{9,10},{10,1... | collective-permute-start | bytes 1572872 | tf_op jit(solution)/shard_map/ppermute | solution.py:29
  41.9 6.8 %copy-start.2 = (s32[16,4]{0,1:T(4,128)S(1)}, s32[16,4]{0,1:T(4,128)}, u32[]{:S(2)}) copy-start(s32[16,4]{0,1:T(4,128)} %param.9) | copy-start | bytes 772
  41.9 6.8 %copy-start.3 = (s32[16,4]{0,1:T(4,128)S(1)}, s32[16,4]{0,1:T(4,128)}, u32[]{:S(2)}) copy-start(s32[16,4]{0,1:T(4,128)} %param.10) | copy-start | bytes 772
  41.9 6.8 %copy-start.4 = (s32[1,2,16]{2,1,0:T(2,128)S(1)}, s32[1,2,16]{2,1,0:T(2,128)}, u32[]{:S(2)}) copy-start(s32[1,2,16]{2,1,0:T(2,128)} %sizes.3) | copy-start | bytes 388
  41.9 6.8 %copy-start.5 = (bf16[1,16,1,256,256]{4,3,2,1,0:T(8,128)(2,1)S(1)}, bf16[1,16,1,256,256]{4,3,2,1,0:T(8,128)(2,1)}, u32[]{:S(2)}) copy-start(bf16[1,16,1,256,256]{4,3,2,1,0:T(8,128)(2,1)} %wave.1) | copy-start | bytes 6291460
  45.0 12.4 %collective-permute-start.18 = (bf16[5,256,256]{2,1,0:T(8,128)(2,1)S(1)}, bf16[5,256,256]{2,1,0:T(8,128)(2,1)S(1)}, u32[]{:S(2)}, u32[]{:S(2)}) collective-permute-start(bf16[5,256,256]{2,1,0:T(8,128)(2,1)S(1)} %pad_maximum_fusion.1), channel_id=1, source_target_pairs={{0,3},{1,0},{2,1},{3,2},{4,7},{5,4},{6,5},{7,6},{8,11},{9,8},{10,9... | collective-permute-start | bytes 1966088 | tf_op jit(solution)/shard_map/ppermute | solution.py:29
  47.0 12.2 %collective-permute-start.16 = (bf16[5,256,256]{2,1,0:T(8,128)(2,1)S(1)}, bf16[5,256,256]{2,1,0:T(8,128)(2,1)S(1)}, u32[]{:S(2)}, u32[]{:S(2)}) collective-permute-start(bf16[5,256,256]{2,1,0:T(8,128)(2,1)S(1)} %pad_maximum_fusion), channel_id=1, source_target_pairs={{0,12},{1,13},{2,14},{3,15},{4,0},{5,1},{6,2},{7,3},{8,4},{9,5},{1... | collective-permute-start | bytes 1966088 | tf_op jit(solution)/shard_map/ppermute | solution.py:29
  53.1 9.1 %collective-permute-start.15 = (bf16[3,256,256]{2,1,0:T(8,128)(2,1)S(1)}, bf16[3,256,256]{2,1,0:T(8,128)(2,1)S(1)}, u32[]{:S(2)}, u32[]{:S(2)}) collective-permute-start(bf16[3,256,256]{2,1,0:T(8,128)(2,1)S(1)} %pad_maximum_fusion.6), channel_id=1, source_target_pairs={{0,4},{1,5},{2,6},{3,7},{4,8},{5,9},{6,10},{7,11},{8,12},{9,13},{1... | collective-permute-start | bytes 1179656 | tf_op jit(solution)/shard_map/ppermute | solution.py:29
  53.5 9.0 %collective-permute-start.17 = (bf16[3,256,256]{2,1,0:T(8,128)(2,1)S(1)}, bf16[3,256,256]{2,1,0:T(8,128)(2,1)S(1)}, u32[]{:S(2)}, u32[]{:S(2)}) collective-permute-start(bf16[3,256,256]{2,1,0:T(8,128)(2,1)S(1)} %pad_maximum_fusion.7), channel_id=1, source_target_pairs={{0,1},{1,2},{2,3},{3,0},{4,5},{5,6},{6,7},{7,4},{8,9},{9,10},{10,1... | collective-permute-start | bytes 1179656 | tf_op jit(solution)/shard_map/ppermute | solution.py:29

commit v5 on v4

--- a/solution.py
+++ b/solution.py
@@ -52,8 +52,8 @@
     pieces = []
     for i in range(2):
         one, two = low_next[i, 1], low_next[i, -1]
-        up = jnp.concatenate([one[0, :1], one[1]])
-        down = jnp.concatenate([high_next[i, -1].reshape(4, *two.shape[2:]), two[0, 1:]])
+        up = one[1]
+        down = jnp.concatenate([high_next[i, -1].reshape(4, *two.shape[2:]), two[0]])
         pieces.append(
             [
                 low[i],
@@ -105,7 +105,7 @@
     return dot(vector[sources[k, a]], right[terms[k, a]]).astype(jnp.bfloat16)
 
 
-ACROSS = (((6, 0), (7, 4)), ((6, 1), (6, 2)), ((7, 0), (7, 1)), ((7, 2), (7, 3)))
+ACROSS = (((7, 4), (7, 5)), ((6, 0), (6, 1)), ((7, 0), (7, 1)), ((7, 2), (7, 3)))
 
 
 def left_block(pieces, z_at, y_at, k):

time: 84.3 us -> 83.4 us (0.989)
  waiting for transfers between devices: 23.3 us -> 20 us
  starting transfers between devices: 25.5 us -> 27.6 us
    ppermute x18, waiting for transfers between devices: 23.3 us -> 20 us  [send(): return lax.ppermute(block, 'sector', along(axis, step))]
    ppermute x18, starting transfers between devices: 25.5 us -> 27.6 us  [send(): return lax.ppermute(block, 'sector', along(axis, step))]
    unnamed x14 -> x12, local copies, waits for them, and re-layouts: 1.96 us -> 1.95 us
  transfers between devices with their start and end apart: 19 -> 19, of which waited for: 10 -> 7; matrix products, arithmetic and copies ran while one was open for 1% -> 0% of each run, Pallas kernels for 9% -> 9%
where the time goes in v5:
time: 83.4 us; the launch traced here: 83.2 us
  starting transfers between devices  27.6 us (33%)
  waiting for transfers between devices  20 us (24%)
  Pallas kernels  19.5 us (23%)
  blocking collectives  12.9 us (15%)
  local copies, waits for them, and re-layouts  2.02 us (2%)
    ppermute x18, starting transfers between devices, send(): return lax.ppermute(block, 'sector', along(axis, step))  27.6 us
    ppermute x18, waiting for transfers between devices, send(): return lax.ppermute(block, 'sector', along(axis, step))  20 us
    all_to_all x1, blocking collectives, per_device(): gathered = lax.all_to_all(sums, 'sector', 0, 0)  12.9 us
    pallas_call x1, Pallas kernels, per_device(): pl.pallas_call(second_kernel, out_shape=(blocks(sectors, bf16), blocks(se...  6.76 us
    pallas_call x1, Pallas kernels, per_device(): pl.pallas_call(inner_kernel, out_shape=(blocks(sectors, bf16), blocks(ter...  4.25 us
    pallas_call x1, Pallas kernels, per_device(): pl.pallas_call(first_kernel, out_shape=(blocks(len(WHOLE), bf16), blocks(...  3.25 us
    pallas_call x1, Pallas kernels, per_device(): pl.pallas_call(pick_kernel, out_shape=(blocks(2, bf16), blocks(2, bf16)),...  2.64 us
    pallas_call x1, Pallas kernels, per_device(): pl.pallas_call(functools.partial(last_kernel, cells), grid=(sectors // pe...  2.59 us
  transfers between devices with their start and end apart: 19, of which 7 were waited for; matrix products, arithmetic and copies ran while one was open for 0% of the time, Pallas kernels for 9%

profile of v5, /device:TPU:0, one launch (start us, length us, event | category | flops | bytes accessed | tf_op | source)
XLA Modules:
  0.0 83.2 jit_solution(581831900807735949)
XLA Ops:
  0.6 2.6 %pick_left.1 = (bf16[2,256,256]{2,1,0:T(8,128)(2,1)}, bf16[2,256,256]{2,1,0:T(8,128)(2,1)}) custom-call(s32[1]{0:T(128)} %bitcast.sector, s32[4,16]{1,0:T(4,128)} %bitcast.25, s32[1,2,16]{2,1,0:T(2,128)} %sizes.3, bf16[1,14,1,256,256]{4,3,2,1,0:T(8,128)(2,1)} %left.1), custom_call_target="tpu_custom_call" | custom-call | tf_op jit(solution)/shard_map/pick_left/pallas_call | solution.py:313
  3.3 2.1 %collective-permute-start.4 = (bf16[2,256,256]{2,1,0:T(8,128)(2,1)}, bf16[2,256,256]{2,1,0:T(8,128)(2,1)S(1)}, u32[]{:S(2)}, u32[]{:S(2)}) collective-permute-start(bf16[2,256,256]{2,1,0:T(8,128)(2,1)} %get-tuple-element.31.half_b), channel_id=1, source_target_pairs={{0,4},{1,5},{2,6},{3,7},{4,8},{5,9},{6,10},{7,11},{8,12},{9,13},{1... | collective-permute-start | bytes 786440 | tf_op jit(solution)/shard_map/ppermute | solution.py:29
  5.4 3.0 %collective-permute-start.2 = (bf16[2,256,256]{2,1,0:T(8,128)(2,1)}, bf16[2,256,256]{2,1,0:T(8,128)(2,1)S(1)}, u32[]{:S(2)}, u32[]{:S(2)}) collective-permute-start(bf16[2,256,256]{2,1,0:T(8,128)(2,1)} %get-tuple-element.30.half_a), channel_id=1, source_target_pairs={{0,3},{1,0},{2,1},{3,2},{4,7},{5,4},{6,5},{7,6},{8,11},{9,8},{10,9... | collective-permute-start | bytes 786440 | tf_op jit(solution)/shard_map/ppermute | solution.py:29
  8.4 0.0 collective-permute-start.1
  8.4 2.2 %collective-permute-start.8 = (bf16[2,256,256]{2,1,0:T(8,128)(2,1)}, bf16[2,256,256]{2,1,0:T(8,128)(2,1)S(1)}, u32[]{:S(2)}, u32[]{:S(2)}) collective-permute-start(bf16[2,256,256]{2,1,0:T(8,128)(2,1)} %get-tuple-element.31.half_b), channel_id=1, source_target_pairs={{0,12},{1,13},{2,14},{3,15},{4,0},{5,1},{6,2},{7,3},{8,4},{9,5},{1... | collective-permute-start | bytes 786440 | tf_op jit(solution)/shard_map/ppermute | solution.py:29
  10.6 0.0 collective-permute-start
  10.6 0.0 copy-start
  10.6 1.0 %copy-done = bf16[2,256,256]{2,1,0:T(8,128)(2,1)S(1)} copy-done((bf16[2,256,256]{2,1,0:T(8,128)(2,1)S(1)}, bf16[2,256,256]{2,1,0:T(8,128)(2,1)}, u32[]{:S(2)}) %copy-start) | copy-done | bytes 262168
  11.6 0.0 copy-start.1
  11.6 0.9 %copy-done.1 = bf16[2,256,256]{2,1,0:T(8,128)(2,1)S(1)} copy-done((bf16[2,256,256]{2,1,0:T(8,128)(2,1)S(1)}, bf16[2,256,256]{2,1,0:T(8,128)(2,1)}, u32[]{:S(2)}) %copy-start.1) | copy-done | bytes 262168
  12.5 1.4 %collective-permute-done.4 = bf16[2,256,256]{2,1,0:T(8,128)(2,1)S(1)} collective-permute-done((bf16[2,256,256]{2,1,0:T(8,128)(2,1)}, bf16[2,256,256]{2,1,0:T(8,128)(2,1)S(1)}, u32[]{:S(2)}, u32[]{:S(2)}) %collective-permute-start.4) | collective-permute-done | bytes 262176 | tf_op jit(solution)/shard_map/ppermute | solution.py:29
  14.0 0.1 pad_maximum_fusion.4.refs_6_.refs_8_
  14.0 0.0 collective-permute-done.2
  14.1 3.5 %collective-permute-start.13 = (bf16[2,2,256,256]{3,2,1,0:T(8,128)(2,1)S(1)}, bf16[2,2,256,256]{3,2,1,0:T(8,128)(2,1)S(1)}, u32[]{:S(2)}, u32[]{:S(2)}) collective-permute-start(bf16[2,2,256,256]{3,2,1,0:T(8,128)(2,1)S(1)} %pad_maximum_fusion.4.refs_6_.refs_8_), channel_id=1, source_target_pairs={{0,3},{1,0},{2,1},{3,2},{4,7},{5,4},{6,5},{7,6},{8,11},{9,8},{10,9... | collective-permute-start | bytes 1572872 | tf_op jit(solution)/shard_map/ppermute | solution.py:29
  17.6 0.0 collective-permute-done.1
  17.6 0.1 pad_maximum_fusion.2.refs_0_
  17.6 0.0 collective-permute-done.8
  17.6 2.5 %collective-permute-start.9 = (bf16[2,2,256,256]{3,2,1,0:T(8,128)(2,1)S(1)}, bf16[2,2,256,256]{3,2,1,0:T(8,128)(2,1)S(1)}, u32[]{:S(2)}, u32[]{:S(2)}) collective-permute-start(bf16[2,2,256,256]{3,2,1,0:T(8,128)(2,1)S(1)} %pad_maximum_fusion.2.refs_0_), channel_id=1, source_target_pairs={{0,12},{1,13},{2,14},{3,15},{4,0},{5,1},{6,2},{7,3},{8,4},{9,5},{1... | collective-permute-start | bytes 1572872 | tf_op jit(solution)/shard_map/ppermute | solution.py:29
  20.2 0.0 collective-permute-start.3
  20.2 0.0 collective-permute-start.5
  20.2 7.8 %collective-permute-done.3 = bf16[2,256,256]{2,1,0:T(8,128)(2,1)S(1)} collective-permute-done((bf16[2,256,256]{2,1,0:T(8,128)(2,1)S(1)}, bf16[2,256,256]{2,1,0:T(8,128)(2,1)S(1)}, u32[]{:S(2)}, u32[]{:S(2)}) %collective-permute-start.3) | collective-permute-done | bytes 262176 | tf_op jit(solution)/shard_map/ppermute | solution.py:29
  28.0 0.0 collective-permute-done.5
  28.0 0.0 collective-permute-start.6
  28.0 1.2 %collective-permute-start.11 = (bf16[2,2,256,256]{3,2,1,0:T(8,128)(2,1)S(1)}, bf16[2,2,256,256]{3,2,1,0:T(8,128)(2,1)S(1)}, u32[]{:S(2)}, u32[]{:S(2)}) collective-permute-start(bf16[2,2,256,256]{3,2,1,0:T(8,128)(2,1)S(1)} %pad_maximum_fusion.4.refs_6_.refs_8_), channel_id=1, source_target_pairs={{0,1},{1,2},{2,3},{3,0},{4,5},{5,6},{6,7},{7,4},{8,9},{9,10},{10,1... | collective-permute-start | bytes 1572872 | tf_op jit(solution)/shard_map/ppermute | solution.py:29
  29.2 0.1 pad_maximum_fusion.5.refs_7_.refs_9_
  29.3 0.0 collective-permute-done.13.refs_10_.refs_12_
  29.3 2.2 %collective-permute-start.14 = (bf16[2,2,256,256]{3,2,1,0:T(8,128)(2,1)S(1)}, bf16[2,2,256,256]{3,2,1,0:T(8,128)(2,1)S(1)}, u32[]{:S(2)}, u32[]{:S(2)}) collective-permute-start(bf16[2,2,256,256]{3,2,1,0:T(8,128)(2,1)S(1)} %pad_maximum_fusion.5.refs_7_.refs_9_), channel_id=1, source_target_pairs={{0,3},{1,0},{2,1},{3,2},{4,7},{5,4},{6,5},{7,6},{8,11},{9,8},{10,9... | collective-permute-start | bytes 1572872 | tf_op jit(solution)/shard_map/ppermute | solution.py:29
  31.5 0.1 pad_maximum_fusion.3.refs_1_
  31.5 0.0 collective-permute-done.9.refs_4_
  31.5 3.2 %collective-permute-start.10 = (bf16[2,2,256,256]{3,2,1,0:T(8,128)(2,1)S(1)}, bf16[2,2,256,256]{3,2,1,0:T(8,128)(2,1)S(1)}, u32[]{:S(2)}, u32[]{:S(2)}) collective-permute-start(bf16[2,2,256,256]{3,2,1,0:T(8,128)(2,1)S(1)} %pad_maximum_fusion.3.refs_1_), channel_id=1, source_target_pairs={{0,12},{1,13},{2,14},{3,15},{4,0},{5,1},{6,2},{7,3},{8,4},{9,5},{1... | collective-permute-start | bytes 1572872 | tf_op jit(solution)/shard_map/ppermute | solution.py:29
  34.8 5.7 %collective-permute-done.6.refs_2_ = bf16[2,2,256,256]{3,2,1,0:T(8,128)(2,1)S(1)} collective-permute-done((bf16[2,2,256,256]{3,2,1,0:T(8,128)(2,1)S(1)}, bf16[2,2,256,256]{3,2,1,0:T(8,128)(2,1)S(1)}, u32[]{:S(2)}, u32[]{:S(2)}) %collective-permute-start.6) | collective-permute-done | bytes 524320 | tf_op jit(solution)/shard_map/ppermute | solution.py:29
  40.5 0.0 collective-permute-start.7
  40.5 0.0 collective-permute-done.11.refs_8_.refs_10_
  40.5 0.8 collective-permute-start.12
  41.3 0.0 collective-permute-done.14.refs_11_.refs_13_
  41.3 0.0 copy-start.2
  41.3 0.0 copy-start.3
  41.3 0.0 copy-start.4
  41.3 0.0 copy-start.5
  41.3 0.1 pad_maximum_fusion.1
  41.4 3.2 %collective-permute-start.18 = (bf16[6,256,256]{2,1,0:T(8,128)(2,1)S(1)}, bf16[6,256,256]{2,1,0:T(8,128)(2,1)S(1)}, u32[]{:S(2)}, u32[]{:S(2)}) collective-permute-start(bf16[6,256,256]{2,1,0:T(8,128)(2,1)S(1)} %pad_maximum_fusion.1), channel_id=1, source_target_pairs={{0,3},{1,0},{2,1},{3,2},{4,7},{5,4},{6,5},{7,6},{8,11},{9,8},{10,9... | collective-permute-start | bytes 2359304 | tf_op jit(solution)/shard_map/ppermute | solution.py:29
  44.6 0.0 collective-permute-done.10.refs_5_
  44.6 0.1 pad_maximum_fusion
  44.7 2.8 %collective-permute-start.16 = (bf16[6,256,256]{2,1,0:T(8,128)(2,1)S(1)}, bf16[6,256,256]{2,1,0:T(8,128)(2,1)S(1)}, u32[]{:S(2)}, u32[]{:S(2)}) collective-permute-start(bf16[6,256,256]{2,1,0:T(8,128)(2,1)S(1)} %pad_maximum_fusion), channel_id=1, source_target_pairs={{0,12},{1,13},{2,14},{3,15},{4,0},{5,1},{6,2},{7,3},{8,4},{9,5},{1... | collective-permute-start | bytes 2359304 | tf_op jit(solution)/shard_map/ppermute | solution.py:29
  47.5 0.0 collective-permute-done.right
  47.5 0.0 copy-done.2
  47.5 0.0 copy-done.3
  47.5 0.0 copy-done.4
  47.5 0.0 copy-done.5
  47.5 4.3 %inner_products.1 = (bf16[16,256,256]{2,1,0:T(8,128)(2,1)S(1)}, bf16[14,256,256]{2,1,0:T(8,128)(2,1)S(1)}, bf16[64,256,256]{2,1,0:T(8,128)(2,1)S(1)}, f32[8,128]{1,0:T(8,128)S(1)}) custom-call(s32[1]{0:T(128)} %bitcast.sector, s32[4,16]{1,0:T(4,128)S(1)} %bitcast.26, s32[4,16]{1,0:T(4,128)S(1)} %bitcast.28, s32[1,2,16]{2,1,0:T(2,128)S(1)} %copy-done.4, ...), custom_call_target="tpu_custom_call" | custom-call | flops 2147483648 | bytes 12582912 | tf_op jit(solution)/shard_map/inner_products/pallas_call | solution.py:339
  51.8 0.5 collective-permute-done.12.refs_9_.refs_11_
  52.3 0.2 collective-permute-done.7.refs_3_
  52.5 0.0 collective-permute-start.15
  52.5 0.9 %collective-permute-start.17 = (bf16[2,256,256]{2,1,0:T(8,128)(2,1)S(1)}, bf16[2,256,256]{2,1,0:T(8,128)(2,1)S(1)}, u32[]{:S(2)}, u32[]{:S(2)}) collective-permute-start(bf16[2,256,256]{2,1,0:T(8,128)(2,1)S(1)} %slice_bitcast_fusion.1), channel_id=1, source_target_pairs={{0,1},{1,2},{2,3},{3,0},{4,5},{5,6},{6,7},{7,4},{8,9},{9,10},{10,1... | collective-permute-start | bytes 786440 | tf_op jit(solution)/shard_map/ppermute | solution.py:29
  53.4 3.2 %first_image.1 = (bf16[9,256,256]{2,1,0:T(8,128)(2,1)S(1)}, f32[6,256,256]{2,1,0:T(8,128)S(1)}, f32[8,128]{1,0:T(8,128)S(1)}) custom-call(s32[1]{0:T(128)} %bitcast.sector, bf16[16,256,256]{2,1,0:T(8,128)(2,1)S(1)} %get-tuple-element.26.masked, bf16[64,256,256]{2,1,0:T(8,128)(2,1)S(1)} %get-tuple-element.28.inner, f32[8,128]{1,0:T(8,128)S(1)} %get-tuple-element.29.sums_wave, ...), custom_call_target="tpu_custom_call" | custom-call | tf_op jit(solution)/shard_map/first_image/pallas_call | solution.py:352
  56.7 1.9 %collective-permute-done.18.refs_15_ = bf16[6,256,256]{2,1,0:T(8,128)(2,1)S(1)} collective-permute-done((bf16[6,256,256]{2,1,0:T(8,128)(2,1)S(1)}, bf16[6,256,256]{2,1,0:T(8,128)(2,1)S(1)}, u32[]{:S(2)}, u32[]{:S(2)}) %collective-permute-start.18) | collective-permute-done | bytes 786464 | tf_op jit(solution)/shard_map/ppermute | solution.py:29
  58.6 2.3 %collective-permute-done.16.refs_7_ = bf16[6,256,256]{2,1,0:T(8,128)(2,1)S(1)} collective-permute-done((bf16[6,256,256]{2,1,0:T(8,128)(2,1)S(1)}, bf16[6,256,256]{2,1,0:T(8,128)(2,1)S(1)}, u32[]{:S(2)}, u32[]{:S(2)}) %collective-permute-start.16) | collective-permute-done | bytes 786464 | tf_op jit(solution)/shard_map/ppermute | solution.py:29
  60.9 0.0 collective-permute-done.15.refs_6_
  60.9 0.0 collective-permute-done.17.refs_14_
  60.9 6.8 %second_image.1 = (bf16[16,256,256]{2,1,0:T(8,128)(2,1)S(1)}, f32[16,256,256]{2,1,0:T(8,128)S(1)}, f32[16,8,128]{2,1,0:T(8,128)S(1)}) custom-call(s32[1]{0:T(128)} %bitcast.sector, s32[4,16]{1,0:T(4,128)S(1)} %bitcast.27, s32[4,16]{1,0:T(4,128)S(1)} %bitcast.29, bf16[16,256,256]{2,1,0:T(8,128)(2,1)S(1)} %get-tuple-element.26.masked, ...), custom_call_target="tpu_custom_call" | custom-call | flops 4831838208 | bytes 25165824 | tf_op jit(solution)/shard_map/second_image/pallas_call | solution.py:362
  67.7 12.9 %all_to_all.5.gathered = f32[16,8,128]{2,1,0:T(8,128)S(1)} all-to-all(f32[16,8,128]{2,1,0:T(8,128)S(1)} %get-tuple-element.47.own), channel_id=1, replica_groups=mesh['section'=8,'sector'=16] {'sector'}, dimensions={0} | all-to-all | bytes 131072 | tf_op jit(solution)/shard_map/all_to_all | solution.py:376
  80.6 2.6 %next_basis.1 = (f32[1,16,1,256,256]{4,3,2,1,0:T(8,128)}, f32[1,3]{1,0:T(1,128)}) custom-call(f32[16,8,128]{2,1,0:T(8,128)S(1)} %all_to_all.5.gathered, f32[16,8,128]{2,1,0:T(8,128)S(1)} %get-tuple-element.47.own, bf16[16,256,256]{2,1,0:T(8,128)(2,1)S(1)} %get-tuple-element.26.masked, bf16[16,256,256]{2,1,0:T(8,128)(2,1)S(1)} %get-tuple-element.48.field, ...), custom_call_target="tpu_custom_call" | custom-call | tf_op jit(solution)/shard_map/next_basis/pallas_call | solution.py:379
  (5 shorter events, 0.1 us)
Async XLA Ops:
  3.3 10.7 %collective-permute-start.4 = (bf16[2,256,256]{2,1,0:T(8,128)(2,1)}, bf16[2,256,256]{2,1,0:T(8,128)(2,1)S(1)}, u32[]{:S(2)}, u32[]{:S(2)}) collective-permute-start(bf16[2,256,256]{2,1,0:T(8,128)(2,1)} %get-tuple-element.31.half_b), channel_id=1, source_target_pairs={{0,4},{1,5},{2,6},{3,7},{4,8},{5,9},{6,10},{7,11},{8,12},{9,13},{1... | collective-permute-start | bytes 786440 | tf_op jit(solution)/shard_map/ppermute | solution.py:29
  5.4 8.7 %collective-permute-start.2 = (bf16[2,256,256]{2,1,0:T(8,128)(2,1)}, bf16[2,256,256]{2,1,0:T(8,128)(2,1)S(1)}, u32[]{:S(2)}, u32[]{:S(2)}) collective-permute-start(bf16[2,256,256]{2,1,0:T(8,128)(2,1)} %get-tuple-element.30.half_a), channel_id=1, source_target_pairs={{0,3},{1,0},{2,1},{3,2},{4,7},{5,4},{6,5},{7,6},{8,11},{9,8},{10,9... | collective-permute-start | bytes 786440 | tf_op jit(solution)/shard_map/ppermute | solution.py:29
  8.4 9.2 %collective-permute-start.1 = (bf16[2,256,256]{2,1,0:T(8,128)(2,1)}, bf16[2,256,256]{2,1,0:T(8,128)(2,1)S(1)}, u32[]{:S(2)}, u32[]{:S(2)}) collective-permute-start(bf16[2,256,256]{2,1,0:T(8,128)(2,1)} %get-tuple-element.30.half_a), channel_id=1, source_target_pairs={{0,1},{1,2},{2,3},{3,0},{4,5},{5,6},{6,7},{7,4},{8,9},{9,10},{10,1... | collective-permute-start | bytes 786440 | tf_op jit(solution)/shard_map/ppermute | solution.py:29
  8.4 9.2 %collective-permute-start.8 = (bf16[2,256,256]{2,1,0:T(8,128)(2,1)}, bf16[2,256,256]{2,1,0:T(8,128)(2,1)S(1)}, u32[]{:S(2)}, u32[]{:S(2)}) collective-permute-start(bf16[2,256,256]{2,1,0:T(8,128)(2,1)} %get-tuple-element.31.half_b), channel_id=1, source_target_pairs={{0,12},{1,13},{2,14},{3,15},{4,0},{5,1},{6,2},{7,3},{8,4},{9,5},{1... | collective-permute-start | bytes 786440 | tf_op jit(solution)/shard_map/ppermute | solution.py:29
  10.6 36.9 %collective-permute-start = (bf16[1,14,1,256,256]{4,3,2,1,0:T(8,128)(2,1)}, bf16[1,14,1,256,256]{4,3,2,1,0:T(8,128)(2,1)S(1)}, u32[]{:S(2)}, u32[]{:S(2)}) collective-permute-start(bf16[1,14,1,256,256]{4,3,2,1,0:T(8,128)(2,1)} %param.8), channel_id=1, source_target_pairs={{0,16},{16,0},{32,48},{48,32},{64,80},{80,64},{96,112},{112,96},{1... | collective-permute-start | bytes 5505032 | tf_op jit(solution)/shard_map/ppermute | solution.py:333
  10.6 1.0 %copy-start = (bf16[2,256,256]{2,1,0:T(8,128)(2,1)S(1)}, bf16[2,256,256]{2,1,0:T(8,128)(2,1)}, u32[]{:S(2)}) copy-start(bf16[2,256,256]{2,1,0:T(8,128)(2,1)} %get-tuple-element.31.half_b) | copy-start | bytes 786436
  11.6 0.9 %copy-start.1 = (bf16[2,256,256]{2,1,0:T(8,128)(2,1)S(1)}, bf16[2,256,256]{2,1,0:T(8,128)(2,1)}, u32[]{:S(2)}) copy-start(bf16[2,256,256]{2,1,0:T(8,128)(2,1)} %get-tuple-element.30.half_a) | copy-start | bytes 786436
  14.1 15.2 %collective-permute-start.13 = (bf16[2,2,256,256]{3,2,1,0:T(8,128)(2,1)S(1)}, bf16[2,2,256,256]{3,2,1,0:T(8,128)(2,1)S(1)}, u32[]{:S(2)}, u32[]{:S(2)}) collective-permute-start(bf16[2,2,256,256]{3,2,1,0:T(8,128)(2,1)S(1)} %pad_maximum_fusion.4.refs_6_.refs_8_), channel_id=1, source_target_pairs={{0,3},{1,0},{2,1},{3,2},{4,7},{5,4},{6,5},{7,6},{8,11},{9,8},{10,9... | collective-permute-start | bytes 1572872 | tf_op jit(solution)/shard_map/ppermute | solution.py:29
  17.6 13.9 %collective-permute-start.9 = (bf16[2,2,256,256]{3,2,1,0:T(8,128)(2,1)S(1)}, bf16[2,2,256,256]{3,2,1,0:T(8,128)(2,1)S(1)}, u32[]{:S(2)}, u32[]{:S(2)}) collective-permute-start(bf16[2,2,256,256]{3,2,1,0:T(8,128)(2,1)S(1)} %pad_maximum_fusion.2.refs_0_), channel_id=1, source_target_pairs={{0,12},{1,13},{2,14},{3,15},{4,0},{5,1},{6,2},{7,3},{8,4},{9,5},{1... | collective-permute-start | bytes 1572872 | tf_op jit(solution)/shard_map/ppermute | solution.py:29
  20.2 7.8 %collective-permute-start.3 = (bf16[2,256,256]{2,1,0:T(8,128)(2,1)S(1)}, bf16[2,256,256]{2,1,0:T(8,128)(2,1)S(1)}, u32[]{:S(2)}, u32[]{:S(2)}) collective-permute-start(bf16[2,256,256]{2,1,0:T(8,128)(2,1)S(1)} %collective-permute-done.1), channel_id=1, source_target_pairs={{0,1},{1,2},{2,3},{3,0},{4,5},{5,6},{6,7},{7,4},{8,9},{9,10},{10,1... | collective-permute-start | bytes 786440 | tf_op jit(solution)/shard_map/ppermute | solution.py:29
  20.2 7.8 %collective-permute-start.5 = (bf16[2,256,256]{2,1,0:T(8,128)(2,1)S(1)}, bf16[2,256,256]{2,1,0:T(8,128)(2,1)S(1)}, u32[]{:S(2)}, u32[]{:S(2)}) collective-permute-start(bf16[2,256,256]{2,1,0:T(8,128)(2,1)S(1)} %collective-permute-done.4), channel_id=1, source_target_pairs={{0,4},{1,5},{2,6},{3,7},{4,8},{5,9},{6,10},{7,11},{8,12},{9,13},{1... | collective-permute-start | bytes 786440 | tf_op jit(solution)/shard_map/ppermute | solution.py:29
  28.0 12.5 %collective-permute-start.6 = (bf16[2,2,256,256]{3,2,1,0:T(8,128)(2,1)S(1)}, bf16[2,2,256,256]{3,2,1,0:T(8,128)(2,1)S(1)}, u32[]{:S(2)}, u32[]{:S(2)}) collective-permute-start(bf16[2,2,256,256]{3,2,1,0:T(8,128)(2,1)S(1)} %pad_maximum_fusion.2.refs_0_), channel_id=1, source_target_pairs={{0,4},{1,5},{2,6},{3,7},{4,8},{5,9},{6,10},{7,11},{8,12},{9,13},{1... | collective-permute-start | bytes 1572872 | tf_op jit(solution)/shard_map/ppermute | solution.py:29
  28.0 12.5 %collective-permute-start.11 = (bf16[2,2,256,256]{3,2,1,0:T(8,128)(2,1)S(1)}, bf16[2,2,256,256]{3,2,1,0:T(8,128)(2,1)S(1)}, u32[]{:S(2)}, u32[]{:S(2)}) collective-permute-start(bf16[2,2,256,256]{3,2,1,0:T(8,128)(2,1)S(1)} %pad_maximum_fusion.4.refs_6_.refs_8_), channel_id=1, source_target_pairs={{0,1},{1,2},{2,3},{3,0},{4,5},{5,6},{6,7},{7,4},{8,9},{9,10},{10,1... | collective-permute-start | bytes 1572872 | tf_op jit(solution)/shard_map/ppermute | solution.py:29
  29.3 12.0 %collective-permute-start.14 = (bf16[2,2,256,256]{3,2,1,0:T(8,128)(2,1)S(1)}, bf16[2,2,256,256]{3,2,1,0:T(8,128)(2,1)S(1)}, u32[]{:S(2)}, u32[]{:S(2)}) collective-permute-start(bf16[2,2,256,256]{3,2,1,0:T(8,128)(2,1)S(1)} %pad_maximum_fusion.5.refs_7_.refs_9_), channel_id=1, source_target_pairs={{0,3},{1,0},{2,1},{3,2},{4,7},{5,4},{6,5},{7,6},{8,11},{9,8},{10,9... | collective-permute-start | bytes 1572872 | tf_op jit(solution)/shard_map/ppermute | solution.py:29
  31.5 13.1 %collective-permute-start.10 = (bf16[2,2,256,256]{3,2,1,0:T(8,128)(2,1)S(1)}, bf16[2,2,256,256]{3,2,1,0:T(8,128)(2,1)S(1)}, u32[]{:S(2)}, u32[]{:S(2)}) collective-permute-start(bf16[2,2,256,256]{3,2,1,0:T(8,128)(2,1)S(1)} %pad_maximum_fusion.3.refs_1_), channel_id=1, source_target_pairs={{0,12},{1,13},{2,14},{3,15},{4,0},{5,1},{6,2},{7,3},{8,4},{9,5},{1... | collective-permute-start | bytes 1572872 | tf_op jit(solution)/shard_map/ppermute | solution.py:29
  40.5 12.0 %collective-permute-start.7 = (bf16[2,2,256,256]{3,2,1,0:T(8,128)(2,1)S(1)}, bf16[2,2,256,256]{3,2,1,0:T(8,128)(2,1)S(1)}, u32[]{:S(2)}, u32[]{:S(2)}) collective-permute-start(bf16[2,2,256,256]{3,2,1,0:T(8,128)(2,1)S(1)} %pad_maximum_fusion.3.refs_1_), channel_id=1, source_target_pairs={{0,4},{1,5},{2,6},{3,7},{4,8},{5,9},{6,10},{7,11},{8,12},{9,13},{1... | collective-permute-start | bytes 1572872 | tf_op jit(solution)/shard_map/ppermute | solution.py:29
  40.5 11.7 %collective-permute-start.12 = (bf16[2,2,256,256]{3,2,1,0:T(8,128)(2,1)S(1)}, bf16[2,2,256,256]{3,2,1,0:T(8,128)(2,1)S(1)}, u32[]{:S(2)}, u32[]{:S(2)}) collective-permute-start(bf16[2,2,256,256]{3,2,1,0:T(8,128)(2,1)S(1)} %pad_maximum_fusion.5.refs_7_.refs_9_), channel_id=1, source_target_pairs={{0,1},{1,2},{2,3},{3,0},{4,5},{5,6},{6,7},{7,4},{8,9},{9,10},{10,1... | collective-permute-start | bytes 1572872 | tf_op jit(solution)/shard_map/ppermute | solution.py:29
  41.3 6.2 %copy-start.2 = (s32[16,4]{0,1:T(4,128)S(1)}, s32[16,4]{0,1:T(4,128)}, u32[]{:S(2)}) copy-start(s32[16,4]{0,1:T(4,128)} %param.9) | copy-start | bytes 772
  41.3 6.2 %copy-start.3 = (s32[16,4]{0,1:T(4,128)S(1)}, s32[16,4]{0,1:T(4,128)}, u32[]{:S(2)}) copy-start(s32[16,4]{0,1:T(4,128)} %param.10) | copy-start | bytes 772
  41.3 6.2 %copy-start.4 = (s32[1,2,16]{2,1,0:T(2,128)S(1)}, s32[1,2,16]{2,1,0:T(2,128)}, u32[]{:S(2)}) copy-start(s32[1,2,16]{2,1,0:T(2,128)} %sizes.3) | copy-start | bytes 388
  41.3 6.2 %copy-start.5 = (bf16[1,16,1,256,256]{4,3,2,1,0:T(8,128)(2,1)S(1)}, bf16[1,16,1,256,256]{4,3,2,1,0:T(8,128)(2,1)}, u32[]{:S(2)}) copy-start(bf16[1,16,1,256,256]{4,3,2,1,0:T(8,128)(2,1)} %wave.1) | copy-start | bytes 6291460
  41.4 17.1 %collective-permute-start.18 = (bf16[6,256,256]{2,1,0:T(8,128)(2,1)S(1)}, bf16[6,256,256]{2,1,0:T(8,128)(2,1)S(1)}, u32[]{:S(2)}, u32[]{:S(2)}) collective-permute-start(bf16[6,256,256]{2,1,0:T(8,128)(2,1)S(1)} %pad_maximum_fusion.1), channel_id=1, source_target_pairs={{0,3},{1,0},{2,1},{3,2},{4,7},{5,4},{6,5},{7,6},{8,11},{9,8},{10,9... | collective-permute-start | bytes 2359304 | tf_op jit(solution)/shard_map/ppermute | solution.py:29
  44.7 16.3 %collective-permute-start.16 = (bf16[6,256,256]{2,1,0:T(8,128)(2,1)S(1)}, bf16[6,256,256]{2,1,0:T(8,128)(2,1)S(1)}, u32[]{:S(2)}, u32[]{:S(2)}) collective-permute-start(bf16[6,256,256]{2,1,0:T(8,128)(2,1)S(1)} %pad_maximum_fusion), channel_id=1, source_target_pairs={{0,12},{1,13},{2,14},{3,15},{4,0},{5,1},{6,2},{7,3},{8,4},{9,5},{1... | collective-permute-start | bytes 2359304 | tf_op jit(solution)/shard_map/ppermute | solution.py:29
  52.5 8.4 %collective-permute-start.15 = (bf16[2,256,256]{2,1,0:T(8,128)(2,1)S(1)}, bf16[2,256,256]{2,1,0:T(8,128)(2,1)S(1)}, u32[]{:S(2)}, u32[]{:S(2)}) collective-permute-start(bf16[2,256,256]{2,1,0:T(8,128)(2,1)S(1)} %slice_bitcast_fusion.3), channel_id=1, source_target_pairs={{0,4},{1,5},{2,6},{3,7},{4,8},{5,9},{6,10},{7,11},{8,12},{9,13},{1... | collective-permute-start | bytes 786440 | tf_op jit(solution)/shard_map/ppermute | solution.py:29
  52.5 8.4 %collective-permute-start.17 = (bf16[2,256,256]{2,1,0:T(8,128)(2,1)S(1)}, bf16[2,256,256]{2,1,0:T(8,128)(2,1)S(1)}, u32[]{:S(2)}, u32[]{:S(2)}) collective-permute-start(bf16[2,256,256]{2,1,0:T(8,128)(2,1)S(1)} %slice_bitcast_fusion.1), channel_id=1, source_target_pairs={{0,1},{1,2},{2,3},{3,0},{4,5},{5,6},{6,7},{7,4},{8,9},{9,10},{10,1... | collective-permute-start | bytes 786440 | tf_op jit(solution)/shard_map/ppermute | solution.py:29

commit v6 on v5

--- a/solution.py
+++ b/solution.py
@@ -189,7 +189,8 @@
 
     some_ww = jnp.sum(some_ww, keepdims=True)
     some_wy = jnp.sum(some_wy, keepdims=True)
-    slope = jnp.where(some_ww > 0.0, some_wy / jnp.where(some_ww > 0.0, some_ww, 1.0), 0.0)
+    usable = some_ww > 1e-30
+    slope = jnp.where(usable, some_wy / jnp.where(usable, some_ww, 1.0), 0.0)
     wu, uu = zero, zero
     for i, (z_at, y_at) in enumerate(WHOLE):
         w = masked[left_sector(me, z_at, y_at)].astype(jnp.float32)
@@ -267,14 +268,15 @@
         uy = uu + slope * wu
         theta = alpha * alpha * total(wy)
         delta = theta - slope
-        beta = lax.rsqrt(alpha * alpha * total(uu - 2.0 * delta * wu + delta * delta * ww) + epsilon)
+        rest = total(uu - 2.0 * delta * wu + delta * delta * ww)
+        beta = lax.rsqrt(alpha * alpha * jnp.maximum(rest, 0.0) + epsilon)
         scale = alpha * beta
         upper = alpha * scale * total(wv - delta * wy)
         lower = scale * scale * total(uv - delta * uy - delta * (wv - delta * wy))
         cu = delta + lower
         cw = delta * slope - lower * delta + upper / beta
         squares = vv + cu * cu * uu + cw * cw * ww - 2.0 * (cu * uv + cw * wv - cu * cw * wu)
-        gamma = lax.rsqrt(scale * scale * total(squares) + epsilon)
+        gamma = lax.rsqrt(scale * scale * jnp.maximum(total(squares), 0.0) + epsilon)
         factor = gamma * scale
         own_slope = own[0, 6:7, :]
         own_delta = theta - own_slope

time: 83.4 us -> 83.4 us (level)
  no operation moved by 1% of the time
where the time goes in v6:
time: 83.4 us; the launch traced here: 83.2 us
  starting transfers between devices  27.6 us (33%)
  waiting for transfers between devices  20 us (24%)
  Pallas kernels  19.5 us (23%)
  blocking collectives  12.9 us (15%)
  local copies, waits for them, and re-layouts  2.02 us (2%)
    ppermute x18, starting transfers between devices, send(): return lax.ppermute(block, 'sector', along(axis, step))  27.6 us
    ppermute x18, waiting for transfers between devices, send(): return lax.ppermute(block, 'sector', along(axis, step))  20 us
    all_to_all x1, blocking collectives, per_device(): gathered = lax.all_to_all(sums, 'sector', 0, 0)  12.9 us
    pallas_call x1, Pallas kernels, per_device(): pl.pallas_call(second_kernel, out_shape=(blocks(sectors, bf16), blocks(se...  6.76 us
    pallas_call x1, Pallas kernels, per_device(): pl.pallas_call(inner_kernel, out_shape=(blocks(sectors, bf16), blocks(ter...  4.25 us
    pallas_call x1, Pallas kernels, per_device(): pl.pallas_call(first_kernel, out_shape=(blocks(len(WHOLE), bf16), blocks(...  3.25 us
    pallas_call x1, Pallas kernels, per_device(): pl.pallas_call(pick_kernel, out_shape=(blocks(2, bf16), blocks(2, bf16)),...  2.64 us
    pallas_call x1, Pallas kernels, per_device(): pl.pallas_call(functools.partial(last_kernel, cells), grid=(sectors // pe...  2.59 us
  transfers between devices with their start and end apart: 19, of which 7 were waited for; matrix products, arithmetic and copies ran while one was open for 0% of the time, Pallas kernels for 9%

profile of v6, /device:TPU:0, one launch (start us, length us, event | category | flops | bytes accessed | tf_op | source)
XLA Modules:
  0.0 83.2 jit_solution(6760917541703412456)
XLA Ops:
  0.6 2.6 %pick_left.1 = (bf16[2,256,256]{2,1,0:T(8,128)(2,1)}, bf16[2,256,256]{2,1,0:T(8,128)(2,1)}) custom-call(s32[1]{0:T(128)} %bitcast.sector, s32[4,16]{1,0:T(4,128)} %bitcast.25, s32[1,2,16]{2,1,0:T(2,128)} %sizes.3, bf16[1,14,1,256,256]{4,3,2,1,0:T(8,128)(2,1)} %left.1), custom_call_target="tpu_custom_call" | custom-call | tf_op jit(solution)/shard_map/pick_left/pallas_call | solution.py:315
  3.3 2.1 %collective-permute-start.4 = (bf16[2,256,256]{2,1,0:T(8,128)(2,1)}, bf16[2,256,256]{2,1,0:T(8,128)(2,1)S(1)}, u32[]{:S(2)}, u32[]{:S(2)}) collective-permute-start(bf16[2,256,256]{2,1,0:T(8,128)(2,1)} %get-tuple-element.31.half_b), channel_id=1, source_target_pairs={{0,4},{1,5},{2,6},{3,7},{4,8},{5,9},{6,10},{7,11},{8,12},{9,13},{1... | collective-permute-start | bytes 786440 | tf_op jit(solution)/shard_map/ppermute | solution.py:29
  5.4 3.0 %collective-permute-start.2 = (bf16[2,256,256]{2,1,0:T(8,128)(2,1)}, bf16[2,256,256]{2,1,0:T(8,128)(2,1)S(1)}, u32[]{:S(2)}, u32[]{:S(2)}) collective-permute-start(bf16[2,256,256]{2,1,0:T(8,128)(2,1)} %get-tuple-element.30.half_a), channel_id=1, source_target_pairs={{0,3},{1,0},{2,1},{3,2},{4,7},{5,4},{6,5},{7,6},{8,11},{9,8},{10,9... | collective-permute-start | bytes 786440 | tf_op jit(solution)/shard_map/ppermute | solution.py:29
  8.4 0.0 collective-permute-start.1
  8.4 2.2 %collective-permute-start.8 = (bf16[2,256,256]{2,1,0:T(8,128)(2,1)}, bf16[2,256,256]{2,1,0:T(8,128)(2,1)S(1)}, u32[]{:S(2)}, u32[]{:S(2)}) collective-permute-start(bf16[2,256,256]{2,1,0:T(8,128)(2,1)} %get-tuple-element.31.half_b), channel_id=1, source_target_pairs={{0,12},{1,13},{2,14},{3,15},{4,0},{5,1},{6,2},{7,3},{8,4},{9,5},{1... | collective-permute-start | bytes 786440 | tf_op jit(solution)/shard_map/ppermute | solution.py:29
  10.6 0.0 collective-permute-start
  10.6 0.0 copy-start
  10.6 1.0 %copy-done = bf16[2,256,256]{2,1,0:T(8,128)(2,1)S(1)} copy-done((bf16[2,256,256]{2,1,0:T(8,128)(2,1)S(1)}, bf16[2,256,256]{2,1,0:T(8,128)(2,1)}, u32[]{:S(2)}) %copy-start) | copy-done | bytes 262168
  11.6 0.0 copy-start.1
  11.6 0.9 %copy-done.1 = bf16[2,256,256]{2,1,0:T(8,128)(2,1)S(1)} copy-done((bf16[2,256,256]{2,1,0:T(8,128)(2,1)S(1)}, bf16[2,256,256]{2,1,0:T(8,128)(2,1)}, u32[]{:S(2)}) %copy-start.1) | copy-done | bytes 262168
  12.5 1.4 %collective-permute-done.4 = bf16[2,256,256]{2,1,0:T(8,128)(2,1)S(1)} collective-permute-done((bf16[2,256,256]{2,1,0:T(8,128)(2,1)}, bf16[2,256,256]{2,1,0:T(8,128)(2,1)S(1)}, u32[]{:S(2)}, u32[]{:S(2)}) %collective-permute-start.4) | collective-permute-done | bytes 262176 | tf_op jit(solution)/shard_map/ppermute | solution.py:29
  14.0 0.1 pad_maximum_fusion.4.refs_6_.refs_8_
  14.0 0.0 collective-permute-done.2
  14.1 3.5 %collective-permute-start.13 = (bf16[2,2,256,256]{3,2,1,0:T(8,128)(2,1)S(1)}, bf16[2,2,256,256]{3,2,1,0:T(8,128)(2,1)S(1)}, u32[]{:S(2)}, u32[]{:S(2)}) collective-permute-start(bf16[2,2,256,256]{3,2,1,0:T(8,128)(2,1)S(1)} %pad_maximum_fusion.4.refs_6_.refs_8_), channel_id=1, source_target_pairs={{0,3},{1,0},{2,1},{3,2},{4,7},{5,4},{6,5},{7,6},{8,11},{9,8},{10,9... | collective-permute-start | bytes 1572872 | tf_op jit(solution)/shard_map/ppermute | solution.py:29
  17.6 0.0 collective-permute-done.1
  17.6 0.1 pad_maximum_fusion.2.refs_0_
  17.6 0.0 collective-permute-done.8
  17.6 2.5 %collective-permute-start.9 = (bf16[2,2,256,256]{3,2,1,0:T(8,128)(2,1)S(1)}, bf16[2,2,256,256]{3,2,1,0:T(8,128)(2,1)S(1)}, u32[]{:S(2)}, u32[]{:S(2)}) collective-permute-start(bf16[2,2,256,256]{3,2,1,0:T(8,128)(2,1)S(1)} %pad_maximum_fusion.2.refs_0_), channel_id=1, source_target_pairs={{0,12},{1,13},{2,14},{3,15},{4,0},{5,1},{6,2},{7,3},{8,4},{9,5},{1... | collective-permute-start | bytes 1572872 | tf_op jit(solution)/shard_map/ppermute | solution.py:29
  20.2 0.0 collective-permute-start.3
  20.2 0.0 collective-permute-start.5
  20.2 7.8 %collective-permute-done.3 = bf16[2,256,256]{2,1,0:T(8,128)(2,1)S(1)} collective-permute-done((bf16[2,256,256]{2,1,0:T(8,128)(2,1)S(1)}, bf16[2,256,256]{2,1,0:T(8,128)(2,1)S(1)}, u32[]{:S(2)}, u32[]{:S(2)}) %collective-permute-start.3) | collective-permute-done | bytes 262176 | tf_op jit(solution)/shard_map/ppermute | solution.py:29
  28.0 0.0 collective-permute-done.5
  28.0 0.0 collective-permute-start.6
  28.0 1.2 %collective-permute-start.11 = (bf16[2,2,256,256]{3,2,1,0:T(8,128)(2,1)S(1)}, bf16[2,2,256,256]{3,2,1,0:T(8,128)(2,1)S(1)}, u32[]{:S(2)}, u32[]{:S(2)}) collective-permute-start(bf16[2,2,256,256]{3,2,1,0:T(8,128)(2,1)S(1)} %pad_maximum_fusion.4.refs_6_.refs_8_), channel_id=1, source_target_pairs={{0,1},{1,2},{2,3},{3,0},{4,5},{5,6},{6,7},{7,4},{8,9},{9,10},{10,1... | collective-permute-start | bytes 1572872 | tf_op jit(solution)/shard_map/ppermute | solution.py:29
  29.2 0.1 pad_maximum_fusion.5.refs_7_.refs_9_
  29.3 0.0 collective-permute-done.13.refs_10_.refs_12_
  29.3 2.2 %collective-permute-start.14 = (bf16[2,2,256,256]{3,2,1,0:T(8,128)(2,1)S(1)}, bf16[2,2,256,256]{3,2,1,0:T(8,128)(2,1)S(1)}, u32[]{:S(2)}, u32[]{:S(2)}) collective-permute-start(bf16[2,2,256,256]{3,2,1,0:T(8,128)(2,1)S(1)} %pad_maximum_fusion.5.refs_7_.refs_9_), channel_id=1, source_target_pairs={{0,3},{1,0},{2,1},{3,2},{4,7},{5,4},{6,5},{7,6},{8,11},{9,8},{10,9... | collective-permute-start | bytes 1572872 | tf_op jit(solution)/shard_map/ppermute | solution.py:29
  31.5 0.1 pad_maximum_fusion.3.refs_1_
  31.5 0.0 collective-permute-done.9.refs_4_
  31.5 3.2 %collective-permute-start.10 = (bf16[2,2,256,256]{3,2,1,0:T(8,128)(2,1)S(1)}, bf16[2,2,256,256]{3,2,1,0:T(8,128)(2,1)S(1)}, u32[]{:S(2)}, u32[]{:S(2)}) collective-permute-start(bf16[2,2,256,256]{3,2,1,0:T(8,128)(2,1)S(1)} %pad_maximum_fusion.3.refs_1_), channel_id=1, source_target_pairs={{0,12},{1,13},{2,14},{3,15},{4,0},{5,1},{6,2},{7,3},{8,4},{9,5},{1... | collective-permute-start | bytes 1572872 | tf_op jit(solution)/shard_map/ppermute | solution.py:29
  34.8 5.7 %collective-permute-done.6.refs_2_ = bf16[2,2,256,256]{3,2,1,0:T(8,128)(2,1)S(1)} collective-permute-done((bf16[2,2,256,256]{3,2,1,0:T(8,128)(2,1)S(1)}, bf16[2,2,256,256]{3,2,1,0:T(8,128)(2,1)S(1)}, u32[]{:S(2)}, u32[]{:S(2)}) %collective-permute-start.6) | collective-permute-done | bytes 524320 | tf_op jit(solution)/shard_map/ppermute | solution.py:29
  40.5 0.0 collective-permute-start.7
  40.5 0.0 collective-permute-done.11.refs_8_.refs_10_
  40.5 0.8 collective-permute-start.12
  41.3 0.0 collective-permute-done.14.refs_11_.refs_13_
  41.3 0.0 copy-start.2
  41.3 0.0 copy-start.3
  41.3 0.0 copy-start.4
  41.3 0.0 copy-start.5
  41.3 0.1 pad_maximum_fusion.1
  41.4 3.2 %collective-permute-start.18 = (bf16[6,256,256]{2,1,0:T(8,128)(2,1)S(1)}, bf16[6,256,256]{2,1,0:T(8,128)(2,1)S(1)}, u32[]{:S(2)}, u32[]{:S(2)}) collective-permute-start(bf16[6,256,256]{2,1,0:T(8,128)(2,1)S(1)} %pad_maximum_fusion.1), channel_id=1, source_target_pairs={{0,3},{1,0},{2,1},{3,2},{4,7},{5,4},{6,5},{7,6},{8,11},{9,8},{10,9... | collective-permute-start | bytes 2359304 | tf_op jit(solution)/shard_map/ppermute | solution.py:29
  44.6 0.0 collective-permute-done.10.refs_5_
  44.6 0.1 pad_maximum_fusion
  44.7 2.8 %collective-permute-start.16 = (bf16[6,256,256]{2,1,0:T(8,128)(2,1)S(1)}, bf16[6,256,256]{2,1,0:T(8,128)(2,1)S(1)}, u32[]{:S(2)}, u32[]{:S(2)}) collective-permute-start(bf16[6,256,256]{2,1,0:T(8,128)(2,1)S(1)} %pad_maximum_fusion), channel_id=1, source_target_pairs={{0,12},{1,13},{2,14},{3,15},{4,0},{5,1},{6,2},{7,3},{8,4},{9,5},{1... | collective-permute-start | bytes 2359304 | tf_op jit(solution)/shard_map/ppermute | solution.py:29
  47.5 0.0 collective-permute-done.right
  47.5 0.0 copy-done.2
  47.5 0.0 copy-done.3
  47.5 0.0 copy-done.4
  47.5 0.0 copy-done.5
  47.5 4.3 %inner_products.1 = (bf16[16,256,256]{2,1,0:T(8,128)(2,1)S(1)}, bf16[14,256,256]{2,1,0:T(8,128)(2,1)S(1)}, bf16[64,256,256]{2,1,0:T(8,128)(2,1)S(1)}, f32[8,128]{1,0:T(8,128)S(1)}) custom-call(s32[1]{0:T(128)} %bitcast.sector, s32[4,16]{1,0:T(4,128)S(1)} %bitcast.26, s32[4,16]{1,0:T(4,128)S(1)} %bitcast.28, s32[1,2,16]{2,1,0:T(2,128)S(1)} %copy-done.4, ...), custom_call_target="tpu_custom_call" | custom-call | flops 2147483648 | bytes 12582912 | tf_op jit(solution)/shard_map/inner_products/pallas_call | solution.py:341
  51.8 0.5 collective-permute-done.12.refs_9_.refs_11_
  52.3 0.2 collective-permute-done.7.refs_3_
  52.5 0.0 collective-permute-start.15
  52.5 0.9 %collective-permute-start.17 = (bf16[2,256,256]{2,1,0:T(8,128)(2,1)S(1)}, bf16[2,256,256]{2,1,0:T(8,128)(2,1)S(1)}, u32[]{:S(2)}, u32[]{:S(2)}) collective-permute-start(bf16[2,256,256]{2,1,0:T(8,128)(2,1)S(1)} %slice_bitcast_fusion.1), channel_id=1, source_target_pairs={{0,1},{1,2},{2,3},{3,0},{4,5},{5,6},{6,7},{7,4},{8,9},{9,10},{10,1... | collective-permute-start | bytes 786440 | tf_op jit(solution)/shard_map/ppermute | solution.py:29
  53.4 3.2 %first_image.1 = (bf16[9,256,256]{2,1,0:T(8,128)(2,1)S(1)}, f32[6,256,256]{2,1,0:T(8,128)S(1)}, f32[8,128]{1,0:T(8,128)S(1)}) custom-call(s32[1]{0:T(128)} %bitcast.sector, bf16[16,256,256]{2,1,0:T(8,128)(2,1)S(1)} %get-tuple-element.26.masked, bf16[64,256,256]{2,1,0:T(8,128)(2,1)S(1)} %get-tuple-element.28.inner, f32[8,128]{1,0:T(8,128)S(1)} %get-tuple-element.29.sums_wave, ...), custom_call_target="tpu_custom_call" | custom-call | tf_op jit(solution)/shard_map/first_image/pallas_call | solution.py:354
  56.7 1.9 %collective-permute-done.18.refs_15_ = bf16[6,256,256]{2,1,0:T(8,128)(2,1)S(1)} collective-permute-done((bf16[6,256,256]{2,1,0:T(8,128)(2,1)S(1)}, bf16[6,256,256]{2,1,0:T(8,128)(2,1)S(1)}, u32[]{:S(2)}, u32[]{:S(2)}) %collective-permute-start.18) | collective-permute-done | bytes 786464 | tf_op jit(solution)/shard_map/ppermute | solution.py:29
  58.6 2.3 %collective-permute-done.16.refs_7_ = bf16[6,256,256]{2,1,0:T(8,128)(2,1)S(1)} collective-permute-done((bf16[6,256,256]{2,1,0:T(8,128)(2,1)S(1)}, bf16[6,256,256]{2,1,0:T(8,128)(2,1)S(1)}, u32[]{:S(2)}, u32[]{:S(2)}) %collective-permute-start.16) | collective-permute-done | bytes 786464 | tf_op jit(solution)/shard_map/ppermute | solution.py:29
  60.9 0.0 collective-permute-done.15.refs_6_
  60.9 0.0 collective-permute-done.17.refs_14_
  60.9 6.8 %second_image.1 = (bf16[16,256,256]{2,1,0:T(8,128)(2,1)S(1)}, f32[16,256,256]{2,1,0:T(8,128)S(1)}, f32[16,8,128]{2,1,0:T(8,128)S(1)}) custom-call(s32[1]{0:T(128)} %bitcast.sector, s32[4,16]{1,0:T(4,128)S(1)} %bitcast.27, s32[4,16]{1,0:T(4,128)S(1)} %bitcast.29, bf16[16,256,256]{2,1,0:T(8,128)(2,1)S(1)} %get-tuple-element.26.masked, ...), custom_call_target="tpu_custom_call" | custom-call | flops 4831838208 | bytes 25165824 | tf_op jit(solution)/shard_map/second_image/pallas_call | solution.py:364
  67.7 12.9 %all_to_all.5.gathered = f32[16,8,128]{2,1,0:T(8,128)S(1)} all-to-all(f32[16,8,128]{2,1,0:T(8,128)S(1)} %get-tuple-element.47.own), channel_id=1, replica_groups=mesh['section'=8,'sector'=16] {'sector'}, dimensions={0} | all-to-all | bytes 131072 | tf_op jit(solution)/shard_map/all_to_all | solution.py:378
  80.6 2.6 %next_basis.1 = (f32[1,16,1,256,256]{4,3,2,1,0:T(8,128)}, f32[1,3]{1,0:T(1,128)}) custom-call(f32[16,8,128]{2,1,0:T(8,128)S(1)} %all_to_all.5.gathered, f32[16,8,128]{2,1,0:T(8,128)S(1)} %get-tuple-element.47.own, bf16[16,256,256]{2,1,0:T(8,128)(2,1)S(1)} %get-tuple-element.26.masked, bf16[16,256,256]{2,1,0:T(8,128)(2,1)S(1)} %get-tuple-element.48.field, ...), custom_call_target="tpu_custom_call" | custom-call | tf_op jit(solution)/shard_map/next_basis/pallas_call | solution.py:381
  (5 shorter events, 0.1 us)
Async XLA Ops:
  3.3 10.7 %collective-permute-start.4 = (bf16[2,256,256]{2,1,0:T(8,128)(2,1)}, bf16[2,256,256]{2,1,0:T(8,128)(2,1)S(1)}, u32[]{:S(2)}, u32[]{:S(2)}) collective-permute-start(bf16[2,256,256]{2,1,0:T(8,128)(2,1)} %get-tuple-element.31.half_b), channel_id=1, source_target_pairs={{0,4},{1,5},{2,6},{3,7},{4,8},{5,9},{6,10},{7,11},{8,12},{9,13},{1... | collective-permute-start | bytes 786440 | tf_op jit(solution)/shard_map/ppermute | solution.py:29
  5.4 8.7 %collective-permute-start.2 = (bf16[2,256,256]{2,1,0:T(8,128)(2,1)}, bf16[2,256,256]{2,1,0:T(8,128)(2,1)S(1)}, u32[]{:S(2)}, u32[]{:S(2)}) collective-permute-start(bf16[2,256,256]{2,1,0:T(8,128)(2,1)} %get-tuple-element.30.half_a), channel_id=1, source_target_pairs={{0,3},{1,0},{2,1},{3,2},{4,7},{5,4},{6,5},{7,6},{8,11},{9,8},{10,9... | collective-permute-start | bytes 786440 | tf_op jit(solution)/shard_map/ppermute | solution.py:29
  8.4 9.2 %collective-permute-start.1 = (bf16[2,256,256]{2,1,0:T(8,128)(2,1)}, bf16[2,256,256]{2,1,0:T(8,128)(2,1)S(1)}, u32[]{:S(2)}, u32[]{:S(2)}) collective-permute-start(bf16[2,256,256]{2,1,0:T(8,128)(2,1)} %get-tuple-element.30.half_a), channel_id=1, source_target_pairs={{0,1},{1,2},{2,3},{3,0},{4,5},{5,6},{6,7},{7,4},{8,9},{9,10},{10,1... | collective-permute-start | bytes 786440 | tf_op jit(solution)/shard_map/ppermute | solution.py:29
  8.4 9.2 %collective-permute-start.8 = (bf16[2,256,256]{2,1,0:T(8,128)(2,1)}, bf16[2,256,256]{2,1,0:T(8,128)(2,1)S(1)}, u32[]{:S(2)}, u32[]{:S(2)}) collective-permute-start(bf16[2,256,256]{2,1,0:T(8,128)(2,1)} %get-tuple-element.31.half_b), channel_id=1, source_target_pairs={{0,12},{1,13},{2,14},{3,15},{4,0},{5,1},{6,2},{7,3},{8,4},{9,5},{1... | collective-permute-start | bytes 786440 | tf_op jit(solution)/shard_map/ppermute | solution.py:29
  10.6 36.9 %collective-permute-start = (bf16[1,14,1,256,256]{4,3,2,1,0:T(8,128)(2,1)}, bf16[1,14,1,256,256]{4,3,2,1,0:T(8,128)(2,1)S(1)}, u32[]{:S(2)}, u32[]{:S(2)}) collective-permute-start(bf16[1,14,1,256,256]{4,3,2,1,0:T(8,128)(2,1)} %param.8), channel_id=1, source_target_pairs={{0,16},{16,0},{32,48},{48,32},{64,80},{80,64},{96,112},{112,96},{1... | collective-permute-start | bytes 5505032 | tf_op jit(solution)/shard_map/ppermute | solution.py:335
  10.6 1.0 %copy-start = (bf16[2,256,256]{2,1,0:T(8,128)(2,1)S(1)}, bf16[2,256,256]{2,1,0:T(8,128)(2,1)}, u32[]{:S(2)}) copy-start(bf16[2,256,256]{2,1,0:T(8,128)(2,1)} %get-tuple-element.31.half_b) | copy-start | bytes 786436
  11.6 0.9 %copy-start.1 = (bf16[2,256,256]{2,1,0:T(8,128)(2,1)S(1)}, bf16[2,256,256]{2,1,0:T(8,128)(2,1)}, u32[]{:S(2)}) copy-start(bf16[2,256,256]{2,1,0:T(8,128)(2,1)} %get-tuple-element.30.half_a) | copy-start | bytes 786436
  14.1 15.2 %collective-permute-start.13 = (bf16[2,2,256,256]{3,2,1,0:T(8,128)(2,1)S(1)}, bf16[2,2,256,256]{3,2,1,0:T(8,128)(2,1)S(1)}, u32[]{:S(2)}, u32[]{:S(2)}) collective-permute-start(bf16[2,2,256,256]{3,2,1,0:T(8,128)(2,1)S(1)} %pad_maximum_fusion.4.refs_6_.refs_8_), channel_id=1, source_target_pairs={{0,3},{1,0},{2,1},{3,2},{4,7},{5,4},{6,5},{7,6},{8,11},{9,8},{10,9... | collective-permute-start | bytes 1572872 | tf_op jit(solution)/shard_map/ppermute | solution.py:29
  17.6 13.9 %collective-permute-start.9 = (bf16[2,2,256,256]{3,2,1,0:T(8,128)(2,1)S(1)}, bf16[2,2,256,256]{3,2,1,0:T(8,128)(2,1)S(1)}, u32[]{:S(2)}, u32[]{:S(2)}) collective-permute-start(bf16[2,2,256,256]{3,2,1,0:T(8,128)(2,1)S(1)} %pad_maximum_fusion.2.refs_0_), channel_id=1, source_target_pairs={{0,12},{1,13},{2,14},{3,15},{4,0},{5,1},{6,2},{7,3},{8,4},{9,5},{1... | collective-permute-start | bytes 1572872 | tf_op jit(solution)/shard_map/ppermute | solution.py:29
  20.2 7.8 %collective-permute-start.3 = (bf16[2,256,256]{2,1,0:T(8,128)(2,1)S(1)}, bf16[2,256,256]{2,1,0:T(8,128)(2,1)S(1)}, u32[]{:S(2)}, u32[]{:S(2)}) collective-permute-start(bf16[2,256,256]{2,1,0:T(8,128)(2,1)S(1)} %collective-permute-done.1), channel_id=1, source_target_pairs={{0,1},{1,2},{2,3},{3,0},{4,5},{5,6},{6,7},{7,4},{8,9},{9,10},{10,1... | collective-permute-start | bytes 786440 | tf_op jit(solution)/shard_map/ppermute | solution.py:29
  20.2 7.8 %collective-permute-start.5 = (bf16[2,256,256]{2,1,0:T(8,128)(2,1)S(1)}, bf16[2,256,256]{2,1,0:T(8,128)(2,1)S(1)}, u32[]{:S(2)}, u32[]{:S(2)}) collective-permute-start(bf16[2,256,256]{2,1,0:T(8,128)(2,1)S(1)} %collective-permute-done.4), channel_id=1, source_target_pairs={{0,4},{1,5},{2,6},{3,7},{4,8},{5,9},{6,10},{7,11},{8,12},{9,13},{1... | collective-permute-start | bytes 786440 | tf_op jit(solution)/shard_map/ppermute | solution.py:29
  28.0 12.5 %collective-permute-start.6 = (bf16[2,2,256,256]{3,2,1,0:T(8,128)(2,1)S(1)}, bf16[2,2,256,256]{3,2,1,0:T(8,128)(2,1)S(1)}, u32[]{:S(2)}, u32[]{:S(2)}) collective-permute-start(bf16[2,2,256,256]{3,2,1,0:T(8,128)(2,1)S(1)} %pad_maximum_fusion.2.refs_0_), channel_id=1, source_target_pairs={{0,4},{1,5},{2,6},{3,7},{4,8},{5,9},{6,10},{7,11},{8,12},{9,13},{1... | collective-permute-start | bytes 1572872 | tf_op jit(solution)/shard_map/ppermute | solution.py:29
  28.0 12.5 %collective-permute-start.11 = (bf16[2,2,256,256]{3,2,1,0:T(8,128)(2,1)S(1)}, bf16[2,2,256,256]{3,2,1,0:T(8,128)(2,1)S(1)}, u32[]{:S(2)}, u32[]{:S(2)}) collective-permute-start(bf16[2,2,256,256]{3,2,1,0:T(8,128)(2,1)S(1)} %pad_maximum_fusion.4.refs_6_.refs_8_), channel_id=1, source_target_pairs={{0,1},{1,2},{2,3},{3,0},{4,5},{5,6},{6,7},{7,4},{8,9},{9,10},{10,1... | collective-permute-start | bytes 1572872 | tf_op jit(solution)/shard_map/ppermute | solution.py:29
  29.3 12.0 %collective-permute-start.14 = (bf16[2,2,256,256]{3,2,1,0:T(8,128)(2,1)S(1)}, bf16[2,2,256,256]{3,2,1,0:T(8,128)(2,1)S(1)}, u32[]{:S(2)}, u32[]{:S(2)}) collective-permute-start(bf16[2,2,256,256]{3,2,1,0:T(8,128)(2,1)S(1)} %pad_maximum_fusion.5.refs_7_.refs_9_), channel_id=1, source_target_pairs={{0,3},{1,0},{2,1},{3,2},{4,7},{5,4},{6,5},{7,6},{8,11},{9,8},{10,9... | collective-permute-start | bytes 1572872 | tf_op jit(solution)/shard_map/ppermute | solution.py:29
  31.5 13.1 %collective-permute-start.10 = (bf16[2,2,256,256]{3,2,1,0:T(8,128)(2,1)S(1)}, bf16[2,2,256,256]{3,2,1,0:T(8,128)(2,1)S(1)}, u32[]{:S(2)}, u32[]{:S(2)}) collective-permute-start(bf16[2,2,256,256]{3,2,1,0:T(8,128)(2,1)S(1)} %pad_maximum_fusion.3.refs_1_), channel_id=1, source_target_pairs={{0,12},{1,13},{2,14},{3,15},{4,0},{5,1},{6,2},{7,3},{8,4},{9,5},{1... | collective-permute-start | bytes 1572872 | tf_op jit(solution)/shard_map/ppermute | solution.py:29
  40.5 12.0 %collective-permute-start.7 = (bf16[2,2,256,256]{3,2,1,0:T(8,128)(2,1)S(1)}, bf16[2,2,256,256]{3,2,1,0:T(8,128)(2,1)S(1)}, u32[]{:S(2)}, u32[]{:S(2)}) collective-permute-start(bf16[2,2,256,256]{3,2,1,0:T(8,128)(2,1)S(1)} %pad_maximum_fusion.3.refs_1_), channel_id=1, source_target_pairs={{0,4},{1,5},{2,6},{3,7},{4,8},{5,9},{6,10},{7,11},{8,12},{9,13},{1... | collective-permute-start | bytes 1572872 | tf_op jit(solution)/shard_map/ppermute | solution.py:29
  40.5 11.7 %collective-permute-start.12 = (bf16[2,2,256,256]{3,2,1,0:T(8,128)(2,1)S(1)}, bf16[2,2,256,256]{3,2,1,0:T(8,128)(2,1)S(1)}, u32[]{:S(2)}, u32[]{:S(2)}) collective-permute-start(bf16[2,2,256,256]{3,2,1,0:T(8,128)(2,1)S(1)} %pad_maximum_fusion.5.refs_7_.refs_9_), channel_id=1, source_target_pairs={{0,1},{1,2},{2,3},{3,0},{4,5},{5,6},{6,7},{7,4},{8,9},{9,10},{10,1... | collective-permute-start | bytes 1572872 | tf_op jit(solution)/shard_map/ppermute | solution.py:29
  41.3 6.2 %copy-start.2 = (s32[16,4]{0,1:T(4,128)S(1)}, s32[16,4]{0,1:T(4,128)}, u32[]{:S(2)}) copy-start(s32[16,4]{0,1:T(4,128)} %param.9) | copy-start | bytes 772
  41.3 6.2 %copy-start.3 = (s32[16,4]{0,1:T(4,128)S(1)}, s32[16,4]{0,1:T(4,128)}, u32[]{:S(2)}) copy-start(s32[16,4]{0,1:T(4,128)} %param.10) | copy-start | bytes 772
  41.3 6.2 %copy-start.4 = (s32[1,2,16]{2,1,0:T(2,128)S(1)}, s32[1,2,16]{2,1,0:T(2,128)}, u32[]{:S(2)}) copy-start(s32[1,2,16]{2,1,0:T(2,128)} %sizes.3) | copy-start | bytes 388
  41.3 6.2 %copy-start.5 = (bf16[1,16,1,256,256]{4,3,2,1,0:T(8,128)(2,1)S(1)}, bf16[1,16,1,256,256]{4,3,2,1,0:T(8,128)(2,1)}, u32[]{:S(2)}) copy-start(bf16[1,16,1,256,256]{4,3,2,1,0:T(8,128)(2,1)} %wave.1) | copy-start | bytes 6291460
  41.4 17.1 %collective-permute-start.18 = (bf16[6,256,256]{2,1,0:T(8,128)(2,1)S(1)}, bf16[6,256,256]{2,1,0:T(8,128)(2,1)S(1)}, u32[]{:S(2)}, u32[]{:S(2)}) collective-permute-start(bf16[6,256,256]{2,1,0:T(8,128)(2,1)S(1)} %pad_maximum_fusion.1), channel_id=1, source_target_pairs={{0,3},{1,0},{2,1},{3,2},{4,7},{5,4},{6,5},{7,6},{8,11},{9,8},{10,9... | collective-permute-start | bytes 2359304 | tf_op jit(solution)/shard_map/ppermute | solution.py:29
  44.7 16.3 %collective-permute-start.16 = (bf16[6,256,256]{2,1,0:T(8,128)(2,1)S(1)}, bf16[6,256,256]{2,1,0:T(8,128)(2,1)S(1)}, u32[]{:S(2)}, u32[]{:S(2)}) collective-permute-start(bf16[6,256,256]{2,1,0:T(8,128)(2,1)S(1)} %pad_maximum_fusion), channel_id=1, source_target_pairs={{0,12},{1,13},{2,14},{3,15},{4,0},{5,1},{6,2},{7,3},{8,4},{9,5},{1... | collective-permute-start | bytes 2359304 | tf_op jit(solution)/shard_map/ppermute | solution.py:29
  52.5 8.4 %collective-permute-start.15 = (bf16[2,256,256]{2,1,0:T(8,128)(2,1)S(1)}, bf16[2,256,256]{2,1,0:T(8,128)(2,1)S(1)}, u32[]{:S(2)}, u32[]{:S(2)}) collective-permute-start(bf16[2,256,256]{2,1,0:T(8,128)(2,1)S(1)} %slice_bitcast_fusion.3), channel_id=1, source_target_pairs={{0,4},{1,5},{2,6},{3,7},{4,8},{5,9},{6,10},{7,11},{8,12},{9,13},{1... | collective-permute-start | bytes 786440 | tf_op jit(solution)/shard_map/ppermute | solution.py:29
  52.5 8.4 %collective-permute-start.17 = (bf16[2,256,256]{2,1,0:T(8,128)(2,1)S(1)}, bf16[2,256,256]{2,1,0:T(8,128)(2,1)S(1)}, u32[]{:S(2)}, u32[]{:S(2)}) collective-permute-start(bf16[2,256,256]{2,1,0:T(8,128)(2,1)S(1)} %slice_bitcast_fusion.1), channel_id=1, source_target_pairs={{0,1},{1,2},{2,3},{3,0},{4,5},{5,6},{6,7},{7,4},{8,9},{9,10},{10,1... | collective-permute-start | bytes 786440 | tf_op jit(solution)/shard_map/ppermute | solution.py:29

commit v7 on v6

--- a/solution.py
+++ b/solution.py
@@ -252,11 +252,8 @@
     sums[...] = jnp.broadcast_to(block[None], sums.shape)
 
 
-def last_kernel(cells, gathered, own, masked, field, image, out, projected, weights):
-    step = pl.program_id(0)
-
-    @pl.when(step == 0)
-    def _():
+def last_kernel(cells, gathered, own, masked, field, image, out, projected, weights, ready, sems):
+    def weigh():
         g = gathered[...]
         ww, wu, uu, wv, uv, vv, slope = (g[:, j, :] for j in range(7))
 
@@ -291,13 +288,21 @@
         row = weights[j : j + 1, :]
         return jnp.concatenate([row] * (out.shape[-1] // 128), axis=1)[None]
 
-    per_step = out.shape[1]
-    here = pl.ds(step * per_step, per_step)
-    out[0, :, 0] = (
-        image[here] * wide(0)
-        - field[here].astype(jnp.float32) * wide(1)
-        - masked[here].astype(jnp.float32) * wide(2)
-    )
+    weigh()
+    parts = sems.shape[0]
+    per_part = ready.shape[0] // parts
+    copies = []
+    for part in range(parts):
+        here = pl.ds(part * per_part, per_part)
+        ready[here] = (
+            image[here] * wide(0)
+            - field[here].astype(jnp.float32) * wide(1)
+            - masked[here].astype(jnp.float32) * wide(2)
+        )
+        copies.append(pltpu.make_async_copy(ready.at[here], out.at[0, here, 0], sems.at[part]))
+        copies[-1].start()
+    for copy in copies:
+        copy.wait()
 
 
 def per_device(wavefunction, left_env, right_env, term_table, source_table, live_sizes):
@@ -376,21 +381,20 @@
     )(sector, terms, sources, masked, right_live, field_some, part, inner, sums_first, *every)
 
     gathered = lax.all_to_all(sums, "sector", 0, 0)
-    per_step = 8
     cells = float(sectors * sectors * size * size)
     next_basis, projected = pl.pallas_call(
         functools.partial(last_kernel, cells),
-        grid=(sectors // per_step,),
         out_shape=(
             jax.ShapeDtypeStruct((1, sectors, 1, size, size), f32),
             jax.ShapeDtypeStruct((1, 3), f32),
         ),
         in_specs=[vmem] * 5,
-        out_specs=(
-            pl.BlockSpec((1, per_step, 1, size, size), lambda i: (0, i, 0, 0, 0)),
-            pl.BlockSpec((1, 3), lambda i: (0, 0)),
-        ),
-        scratch_shapes=[pltpu.VMEM((3, 128), f32)],
+        out_specs=(pl.BlockSpec(memory_space=pl.ANY), vmem),
+        scratch_shapes=[
+            pltpu.VMEM((3, 128), f32),
+            pltpu.VMEM((sectors, size, size), f32),
+            pltpu.SemaphoreType.DMA((8,)),
+        ],
         compiler_params=pltpu.CompilerParams(vmem_limit_bytes=12 * MIB),
         name="next_basis",
     )(gathered, sums, masked, field, image)

time: 83.4 us -> 84 us (level)
  no operation moved by 1% of the time
where the time goes in v7:
time: 84 us; the launch traced here: 83.7 us
  starting transfers between devices  27.6 us (33%)
  waiting for transfers between devices  20 us (24%)
  Pallas kernels  19.9 us (24%)
  blocking collectives  12.9 us (15%)
  local copies, waits for them, and re-layouts  2.02 us (2%)
  between operations  0.98 us (1%)
    ppermute x18, starting transfers between devices, send(): return lax.ppermute(block, 'sector', along(axis, step))  27.6 us
    ppermute x18, waiting for transfers between devices, send(): return lax.ppermute(block, 'sector', along(axis, step))  20 us
    all_to_all x1, blocking collectives, per_device(): gathered = lax.all_to_all(sums, 'sector', 0, 0)  12.9 us
    pallas_call x1, Pallas kernels, per_device(): pl.pallas_call(second_kernel, out_shape=(blocks(sectors, bf16), blocks(se...  6.76 us
    pallas_call x1, Pallas kernels, per_device(): pl.pallas_call(inner_kernel, out_shape=(blocks(sectors, bf16), blocks(ter...  4.25 us
    pallas_call x1, Pallas kernels, per_device(): pl.pallas_call(first_kernel, out_shape=(blocks(len(WHOLE), bf16), blocks(...  3.25 us
    pallas_call x1, Pallas kernels, per_device(): pl.pallas_call(functools.partial(last_kernel, cells), out_shape=(jax.Shap...  2.96 us
    pallas_call x1, Pallas kernels, per_device(): pl.pallas_call(pick_kernel, out_shape=(blocks(2, bf16), blocks(2, bf16)),...  2.64 us
  transfers between devices with their start and end apart: 19, of which 7 were waited for; matrix products, arithmetic and copies ran while one was open for 0% of the time, Pallas kernels for 9%

profile of v7, /device:TPU:0, one launch (start us, length us, event | category | flops | bytes accessed | tf_op | source)
XLA Modules:
  0.0 83.7 jit_solution(13251362778832536072)
XLA Ops:
  0.6 2.6 %pick_left.1 = (bf16[2,256,256]{2,1,0:T(8,128)(2,1)}, bf16[2,256,256]{2,1,0:T(8,128)(2,1)}) custom-call(s32[1]{0:T(128)} %bitcast.sector, s32[4,16]{1,0:T(4,128)} %bitcast.25, s32[1,2,16]{2,1,0:T(2,128)} %sizes.3, bf16[1,14,1,256,256]{4,3,2,1,0:T(8,128)(2,1)} %left.1), custom_call_target="tpu_custom_call" | custom-call | tf_op jit(solution)/shard_map/pick_left/pallas_call | solution.py:320
  3.3 2.1 %collective-permute-start.4 = (bf16[2,256,256]{2,1,0:T(8,128)(2,1)}, bf16[2,256,256]{2,1,0:T(8,128)(2,1)S(1)}, u32[]{:S(2)}, u32[]{:S(2)}) collective-permute-start(bf16[2,256,256]{2,1,0:T(8,128)(2,1)} %get-tuple-element.31.half_b), channel_id=1, source_target_pairs={{0,4},{1,5},{2,6},{3,7},{4,8},{5,9},{6,10},{7,11},{8,12},{9,13},{1... | collective-permute-start | bytes 786440 | tf_op jit(solution)/shard_map/ppermute | solution.py:29
  5.4 3.0 %collective-permute-start.2 = (bf16[2,256,256]{2,1,0:T(8,128)(2,1)}, bf16[2,256,256]{2,1,0:T(8,128)(2,1)S(1)}, u32[]{:S(2)}, u32[]{:S(2)}) collective-permute-start(bf16[2,256,256]{2,1,0:T(8,128)(2,1)} %get-tuple-element.30.half_a), channel_id=1, source_target_pairs={{0,3},{1,0},{2,1},{3,2},{4,7},{5,4},{6,5},{7,6},{8,11},{9,8},{10,9... | collective-permute-start | bytes 786440 | tf_op jit(solution)/shard_map/ppermute | solution.py:29
  8.4 0.0 collective-permute-start.1
  8.4 2.2 %collective-permute-start.8 = (bf16[2,256,256]{2,1,0:T(8,128)(2,1)}, bf16[2,256,256]{2,1,0:T(8,128)(2,1)S(1)}, u32[]{:S(2)}, u32[]{:S(2)}) collective-permute-start(bf16[2,256,256]{2,1,0:T(8,128)(2,1)} %get-tuple-element.31.half_b), channel_id=1, source_target_pairs={{0,12},{1,13},{2,14},{3,15},{4,0},{5,1},{6,2},{7,3},{8,4},{9,5},{1... | collective-permute-start | bytes 786440 | tf_op jit(solution)/shard_map/ppermute | solution.py:29
  10.6 0.0 collective-permute-start
  10.6 0.0 copy-start
  10.6 1.0 %copy-done = bf16[2,256,256]{2,1,0:T(8,128)(2,1)S(1)} copy-done((bf16[2,256,256]{2,1,0:T(8,128)(2,1)S(1)}, bf16[2,256,256]{2,1,0:T(8,128)(2,1)}, u32[]{:S(2)}) %copy-start) | copy-done | bytes 262168
  11.6 0.0 copy-start.1
  11.6 0.9 %copy-done.1 = bf16[2,256,256]{2,1,0:T(8,128)(2,1)S(1)} copy-done((bf16[2,256,256]{2,1,0:T(8,128)(2,1)S(1)}, bf16[2,256,256]{2,1,0:T(8,128)(2,1)}, u32[]{:S(2)}) %copy-start.1) | copy-done | bytes 262168
  12.5 1.4 %collective-permute-done.4 = bf16[2,256,256]{2,1,0:T(8,128)(2,1)S(1)} collective-permute-done((bf16[2,256,256]{2,1,0:T(8,128)(2,1)}, bf16[2,256,256]{2,1,0:T(8,128)(2,1)S(1)}, u32[]{:S(2)}, u32[]{:S(2)}) %collective-permute-start.4) | collective-permute-done | bytes 262176 | tf_op jit(solution)/shard_map/ppermute | solution.py:29
  14.0 0.1 pad_maximum_fusion.4.refs_6_.refs_8_
  14.0 0.0 collective-permute-done.2
  14.1 3.5 %collective-permute-start.13 = (bf16[2,2,256,256]{3,2,1,0:T(8,128)(2,1)S(1)}, bf16[2,2,256,256]{3,2,1,0:T(8,128)(2,1)S(1)}, u32[]{:S(2)}, u32[]{:S(2)}) collective-permute-start(bf16[2,2,256,256]{3,2,1,0:T(8,128)(2,1)S(1)} %pad_maximum_fusion.4.refs_6_.refs_8_), channel_id=1, source_target_pairs={{0,3},{1,0},{2,1},{3,2},{4,7},{5,4},{6,5},{7,6},{8,11},{9,8},{10,9... | collective-permute-start | bytes 1572872 | tf_op jit(solution)/shard_map/ppermute | solution.py:29
  17.6 0.0 collective-permute-done.1
  17.6 0.1 pad_maximum_fusion.2.refs_0_
  17.6 0.0 collective-permute-done.8
  17.6 2.5 %collective-permute-start.9 = (bf16[2,2,256,256]{3,2,1,0:T(8,128)(2,1)S(1)}, bf16[2,2,256,256]{3,2,1,0:T(8,128)(2,1)S(1)}, u32[]{:S(2)}, u32[]{:S(2)}) collective-permute-start(bf16[2,2,256,256]{3,2,1,0:T(8,128)(2,1)S(1)} %pad_maximum_fusion.2.refs_0_), channel_id=1, source_target_pairs={{0,12},{1,13},{2,14},{3,15},{4,0},{5,1},{6,2},{7,3},{8,4},{9,5},{1... | collective-permute-start | bytes 1572872 | tf_op jit(solution)/shard_map/ppermute | solution.py:29
  20.2 0.0 collective-permute-start.3
  20.2 0.0 collective-permute-start.5
  20.2 7.8 %collective-permute-done.3 = bf16[2,256,256]{2,1,0:T(8,128)(2,1)S(1)} collective-permute-done((bf16[2,256,256]{2,1,0:T(8,128)(2,1)S(1)}, bf16[2,256,256]{2,1,0:T(8,128)(2,1)S(1)}, u32[]{:S(2)}, u32[]{:S(2)}) %collective-permute-start.3) | collective-permute-done | bytes 262176 | tf_op jit(solution)/shard_map/ppermute | solution.py:29
  28.0 0.0 collective-permute-done.5
  28.0 0.0 collective-permute-start.6
  28.0 1.2 %collective-permute-start.11 = (bf16[2,2,256,256]{3,2,1,0:T(8,128)(2,1)S(1)}, bf16[2,2,256,256]{3,2,1,0:T(8,128)(2,1)S(1)}, u32[]{:S(2)}, u32[]{:S(2)}) collective-permute-start(bf16[2,2,256,256]{3,2,1,0:T(8,128)(2,1)S(1)} %pad_maximum_fusion.4.refs_6_.refs_8_), channel_id=1, source_target_pairs={{0,1},{1,2},{2,3},{3,0},{4,5},{5,6},{6,7},{7,4},{8,9},{9,10},{10,1... | collective-permute-start | bytes 1572872 | tf_op jit(solution)/shard_map/ppermute | solution.py:29
  29.2 0.1 pad_maximum_fusion.5.refs_7_.refs_9_
  29.3 0.0 collective-permute-done.13.refs_10_.refs_12_
  29.3 2.2 %collective-permute-start.14 = (bf16[2,2,256,256]{3,2,1,0:T(8,128)(2,1)S(1)}, bf16[2,2,256,256]{3,2,1,0:T(8,128)(2,1)S(1)}, u32[]{:S(2)}, u32[]{:S(2)}) collective-permute-start(bf16[2,2,256,256]{3,2,1,0:T(8,128)(2,1)S(1)} %pad_maximum_fusion.5.refs_7_.refs_9_), channel_id=1, source_target_pairs={{0,3},{1,0},{2,1},{3,2},{4,7},{5,4},{6,5},{7,6},{8,11},{9,8},{10,9... | collective-permute-start | bytes 1572872 | tf_op jit(solution)/shard_map/ppermute | solution.py:29
  31.5 0.1 pad_maximum_fusion.3.refs_1_
  31.5 0.0 collective-permute-done.9.refs_4_
  31.5 3.2 %collective-permute-start.10 = (bf16[2,2,256,256]{3,2,1,0:T(8,128)(2,1)S(1)}, bf16[2,2,256,256]{3,2,1,0:T(8,128)(2,1)S(1)}, u32[]{:S(2)}, u32[]{:S(2)}) collective-permute-start(bf16[2,2,256,256]{3,2,1,0:T(8,128)(2,1)S(1)} %pad_maximum_fusion.3.refs_1_), channel_id=1, source_target_pairs={{0,12},{1,13},{2,14},{3,15},{4,0},{5,1},{6,2},{7,3},{8,4},{9,5},{1... | collective-permute-start | bytes 1572872 | tf_op jit(solution)/shard_map/ppermute | solution.py:29
  34.8 5.7 %collective-permute-done.6.refs_2_ = bf16[2,2,256,256]{3,2,1,0:T(8,128)(2,1)S(1)} collective-permute-done((bf16[2,2,256,256]{3,2,1,0:T(8,128)(2,1)S(1)}, bf16[2,2,256,256]{3,2,1,0:T(8,128)(2,1)S(1)}, u32[]{:S(2)}, u32[]{:S(2)}) %collective-permute-start.6) | collective-permute-done | bytes 524320 | tf_op jit(solution)/shard_map/ppermute | solution.py:29
  40.5 0.0 collective-permute-start.7
  40.5 0.0 collective-permute-done.11.refs_8_.refs_10_
  40.5 0.8 collective-permute-start.12
  41.3 0.0 collective-permute-done.14.refs_11_.refs_13_
  41.3 0.0 copy-start.2
  41.3 0.0 copy-start.3
  41.3 0.0 copy-start.4
  41.3 0.0 copy-start.5
  41.3 0.1 pad_maximum_fusion.1
  41.4 3.2 %collective-permute-start.18 = (bf16[6,256,256]{2,1,0:T(8,128)(2,1)S(1)}, bf16[6,256,256]{2,1,0:T(8,128)(2,1)S(1)}, u32[]{:S(2)}, u32[]{:S(2)}) collective-permute-start(bf16[6,256,256]{2,1,0:T(8,128)(2,1)S(1)} %pad_maximum_fusion.1), channel_id=1, source_target_pairs={{0,3},{1,0},{2,1},{3,2},{4,7},{5,4},{6,5},{7,6},{8,11},{9,8},{10,9... | collective-permute-start | bytes 2359304 | tf_op jit(solution)/shard_map/ppermute | solution.py:29
  44.6 0.0 collective-permute-done.10.refs_5_
  44.6 0.1 pad_maximum_fusion
  44.7 2.8 %collective-permute-start.16 = (bf16[6,256,256]{2,1,0:T(8,128)(2,1)S(1)}, bf16[6,256,256]{2,1,0:T(8,128)(2,1)S(1)}, u32[]{:S(2)}, u32[]{:S(2)}) collective-permute-start(bf16[6,256,256]{2,1,0:T(8,128)(2,1)S(1)} %pad_maximum_fusion), channel_id=1, source_target_pairs={{0,12},{1,13},{2,14},{3,15},{4,0},{5,1},{6,2},{7,3},{8,4},{9,5},{1... | collective-permute-start | bytes 2359304 | tf_op jit(solution)/shard_map/ppermute | solution.py:29
  47.5 0.0 collective-permute-done.right
  47.5 0.0 copy-done.2
  47.5 0.0 copy-done.3
  47.5 0.0 copy-done.4
  47.5 0.0 copy-done.5
  47.5 4.3 %inner_products.1 = (bf16[16,256,256]{2,1,0:T(8,128)(2,1)S(1)}, bf16[14,256,256]{2,1,0:T(8,128)(2,1)S(1)}, bf16[64,256,256]{2,1,0:T(8,128)(2,1)S(1)}, f32[8,128]{1,0:T(8,128)S(1)}) custom-call(s32[1]{0:T(128)} %bitcast.sector, s32[4,16]{1,0:T(4,128)S(1)} %bitcast.26, s32[4,16]{1,0:T(4,128)S(1)} %bitcast.28, s32[1,2,16]{2,1,0:T(2,128)S(1)} %copy-done.4, ...), custom_call_target="tpu_custom_call" | custom-call | flops 2147483648 | bytes 12582912 | tf_op jit(solution)/shard_map/inner_products/pallas_call | solution.py:346
  51.8 0.5 collective-permute-done.12.refs_9_.refs_11_
  52.3 0.2 collective-permute-done.7.refs_3_
  52.5 0.0 collective-permute-start.15
  52.5 0.9 %collective-permute-start.17 = (bf16[2,256,256]{2,1,0:T(8,128)(2,1)S(1)}, bf16[2,256,256]{2,1,0:T(8,128)(2,1)S(1)}, u32[]{:S(2)}, u32[]{:S(2)}) collective-permute-start(bf16[2,256,256]{2,1,0:T(8,128)(2,1)S(1)} %slice_bitcast_fusion.1), channel_id=1, source_target_pairs={{0,1},{1,2},{2,3},{3,0},{4,5},{5,6},{6,7},{7,4},{8,9},{9,10},{10,1... | collective-permute-start | bytes 786440 | tf_op jit(solution)/shard_map/ppermute | solution.py:29
  53.4 3.2 %first_image.1 = (bf16[9,256,256]{2,1,0:T(8,128)(2,1)S(1)}, f32[6,256,256]{2,1,0:T(8,128)S(1)}, f32[8,128]{1,0:T(8,128)S(1)}) custom-call(s32[1]{0:T(128)} %bitcast.sector, bf16[16,256,256]{2,1,0:T(8,128)(2,1)S(1)} %get-tuple-element.26.masked, bf16[64,256,256]{2,1,0:T(8,128)(2,1)S(1)} %get-tuple-element.28.inner, f32[8,128]{1,0:T(8,128)S(1)} %get-tuple-element.29.sums_wave, ...), custom_call_target="tpu_custom_call" | custom-call | tf_op jit(solution)/shard_map/first_image/pallas_call | solution.py:359
  56.7 1.9 %collective-permute-done.18.refs_15_ = bf16[6,256,256]{2,1,0:T(8,128)(2,1)S(1)} collective-permute-done((bf16[6,256,256]{2,1,0:T(8,128)(2,1)S(1)}, bf16[6,256,256]{2,1,0:T(8,128)(2,1)S(1)}, u32[]{:S(2)}, u32[]{:S(2)}) %collective-permute-start.18) | collective-permute-done | bytes 786464 | tf_op jit(solution)/shard_map/ppermute | solution.py:29
  58.6 2.3 %collective-permute-done.16.refs_7_ = bf16[6,256,256]{2,1,0:T(8,128)(2,1)S(1)} collective-permute-done((bf16[6,256,256]{2,1,0:T(8,128)(2,1)S(1)}, bf16[6,256,256]{2,1,0:T(8,128)(2,1)S(1)}, u32[]{:S(2)}, u32[]{:S(2)}) %collective-permute-start.16) | collective-permute-done | bytes 786464 | tf_op jit(solution)/shard_map/ppermute | solution.py:29
  60.9 0.0 collective-permute-done.15.refs_6_
  60.9 0.0 collective-permute-done.17.refs_14_
  60.9 6.8 %second_image.1 = (bf16[16,256,256]{2,1,0:T(8,128)(2,1)S(1)}, f32[16,256,256]{2,1,0:T(8,128)S(1)}, f32[16,8,128]{2,1,0:T(8,128)S(1)}) custom-call(s32[1]{0:T(128)} %bitcast.sector, s32[4,16]{1,0:T(4,128)S(1)} %bitcast.27, s32[4,16]{1,0:T(4,128)S(1)} %bitcast.29, bf16[16,256,256]{2,1,0:T(8,128)(2,1)S(1)} %get-tuple-element.26.masked, ...), custom_call_target="tpu_custom_call" | custom-call | flops 4831838208 | bytes 25165824 | tf_op jit(solution)/shard_map/second_image/pallas_call | solution.py:369
  67.7 12.9 %all_to_all.5.gathered = f32[16,8,128]{2,1,0:T(8,128)S(1)} all-to-all(f32[16,8,128]{2,1,0:T(8,128)S(1)} %get-tuple-element.47.own), channel_id=1, replica_groups=mesh['section'=8,'sector'=16] {'sector'}, dimensions={0} | all-to-all | bytes 131072 | tf_op jit(solution)/shard_map/all_to_all | solution.py:383
  80.6 3.0 %next_basis.1 = (f32[1,16,1,256,256]{4,3,2,1,0:T(8,128)}, f32[1,3]{1,0:T(1,128)}) custom-call(f32[16,8,128]{2,1,0:T(8,128)S(1)} %all_to_all.5.gathered, f32[16,8,128]{2,1,0:T(8,128)S(1)} %get-tuple-element.47.own, bf16[16,256,256]{2,1,0:T(8,128)(2,1)S(1)} %get-tuple-element.26.masked, bf16[16,256,256]{2,1,0:T(8,128)(2,1)S(1)} %get-tuple-element.48.field, ...), custom_call_target="tpu_custom_call" | custom-call | tf_op jit(solution)/shard_map/next_basis/pallas_call | solution.py:385
  (5 shorter events, 0.1 us)
Async XLA Ops:
  3.3 10.7 %collective-permute-start.4 = (bf16[2,256,256]{2,1,0:T(8,128)(2,1)}, bf16[2,256,256]{2,1,0:T(8,128)(2,1)S(1)}, u32[]{:S(2)}, u32[]{:S(2)}) collective-permute-start(bf16[2,256,256]{2,1,0:T(8,128)(2,1)} %get-tuple-element.31.half_b), channel_id=1, source_target_pairs={{0,4},{1,5},{2,6},{3,7},{4,8},{5,9},{6,10},{7,11},{8,12},{9,13},{1... | collective-permute-start | bytes 786440 | tf_op jit(solution)/shard_map/ppermute | solution.py:29
  5.4 8.7 %collective-permute-start.2 = (bf16[2,256,256]{2,1,0:T(8,128)(2,1)}, bf16[2,256,256]{2,1,0:T(8,128)(2,1)S(1)}, u32[]{:S(2)}, u32[]{:S(2)}) collective-permute-start(bf16[2,256,256]{2,1,0:T(8,128)(2,1)} %get-tuple-element.30.half_a), channel_id=1, source_target_pairs={{0,3},{1,0},{2,1},{3,2},{4,7},{5,4},{6,5},{7,6},{8,11},{9,8},{10,9... | collective-permute-start | bytes 786440 | tf_op jit(solution)/shard_map/ppermute | solution.py:29
  8.4 9.2 %collective-permute-start.1 = (bf16[2,256,256]{2,1,0:T(8,128)(2,1)}, bf16[2,256,256]{2,1,0:T(8,128)(2,1)S(1)}, u32[]{:S(2)}, u32[]{:S(2)}) collective-permute-start(bf16[2,256,256]{2,1,0:T(8,128)(2,1)} %get-tuple-element.30.half_a), channel_id=1, source_target_pairs={{0,1},{1,2},{2,3},{3,0},{4,5},{5,6},{6,7},{7,4},{8,9},{9,10},{10,1... | collective-permute-start | bytes 786440 | tf_op jit(solution)/shard_map/ppermute | solution.py:29
  8.4 9.2 %collective-permute-start.8 = (bf16[2,256,256]{2,1,0:T(8,128)(2,1)}, bf16[2,256,256]{2,1,0:T(8,128)(2,1)S(1)}, u32[]{:S(2)}, u32[]{:S(2)}) collective-permute-start(bf16[2,256,256]{2,1,0:T(8,128)(2,1)} %get-tuple-element.31.half_b), channel_id=1, source_target_pairs={{0,12},{1,13},{2,14},{3,15},{4,0},{5,1},{6,2},{7,3},{8,4},{9,5},{1... | collective-permute-start | bytes 786440 | tf_op jit(solution)/shard_map/ppermute | solution.py:29
  10.6 36.9 %collective-permute-start = (bf16[1,14,1,256,256]{4,3,2,1,0:T(8,128)(2,1)}, bf16[1,14,1,256,256]{4,3,2,1,0:T(8,128)(2,1)S(1)}, u32[]{:S(2)}, u32[]{:S(2)}) collective-permute-start(bf16[1,14,1,256,256]{4,3,2,1,0:T(8,128)(2,1)} %param.8), channel_id=1, source_target_pairs={{0,16},{16,0},{32,48},{48,32},{64,80},{80,64},{96,112},{112,96},{1... | collective-permute-start | bytes 5505032 | tf_op jit(solution)/shard_map/ppermute | solution.py:340
  10.6 1.0 %copy-start = (bf16[2,256,256]{2,1,0:T(8,128)(2,1)S(1)}, bf16[2,256,256]{2,1,0:T(8,128)(2,1)}, u32[]{:S(2)}) copy-start(bf16[2,256,256]{2,1,0:T(8,128)(2,1)} %get-tuple-element.31.half_b) | copy-start | bytes 786436
  11.6 0.9 %copy-start.1 = (bf16[2,256,256]{2,1,0:T(8,128)(2,1)S(1)}, bf16[2,256,256]{2,1,0:T(8,128)(2,1)}, u32[]{:S(2)}) copy-start(bf16[2,256,256]{2,1,0:T(8,128)(2,1)} %get-tuple-element.30.half_a) | copy-start | bytes 786436
  14.1 15.2 %collective-permute-start.13 = (bf16[2,2,256,256]{3,2,1,0:T(8,128)(2,1)S(1)}, bf16[2,2,256,256]{3,2,1,0:T(8,128)(2,1)S(1)}, u32[]{:S(2)}, u32[]{:S(2)}) collective-permute-start(bf16[2,2,256,256]{3,2,1,0:T(8,128)(2,1)S(1)} %pad_maximum_fusion.4.refs_6_.refs_8_), channel_id=1, source_target_pairs={{0,3},{1,0},{2,1},{3,2},{4,7},{5,4},{6,5},{7,6},{8,11},{9,8},{10,9... | collective-permute-start | bytes 1572872 | tf_op jit(solution)/shard_map/ppermute | solution.py:29
  17.6 13.9 %collective-permute-start.9 = (bf16[2,2,256,256]{3,2,1,0:T(8,128)(2,1)S(1)}, bf16[2,2,256,256]{3,2,1,0:T(8,128)(2,1)S(1)}, u32[]{:S(2)}, u32[]{:S(2)}) collective-permute-start(bf16[2,2,256,256]{3,2,1,0:T(8,128)(2,1)S(1)} %pad_maximum_fusion.2.refs_0_), channel_id=1, source_target_pairs={{0,12},{1,13},{2,14},{3,15},{4,0},{5,1},{6,2},{7,3},{8,4},{9,5},{1... | collective-permute-start | bytes 1572872 | tf_op jit(solution)/shard_map/ppermute | solution.py:29
  20.2 7.8 %collective-permute-start.3 = (bf16[2,256,256]{2,1,0:T(8,128)(2,1)S(1)}, bf16[2,256,256]{2,1,0:T(8,128)(2,1)S(1)}, u32[]{:S(2)}, u32[]{:S(2)}) collective-permute-start(bf16[2,256,256]{2,1,0:T(8,128)(2,1)S(1)} %collective-permute-done.1), channel_id=1, source_target_pairs={{0,1},{1,2},{2,3},{3,0},{4,5},{5,6},{6,7},{7,4},{8,9},{9,10},{10,1... | collective-permute-start | bytes 786440 | tf_op jit(solution)/shard_map/ppermute | solution.py:29
  20.2 7.8 %collective-permute-start.5 = (bf16[2,256,256]{2,1,0:T(8,128)(2,1)S(1)}, bf16[2,256,256]{2,1,0:T(8,128)(2,1)S(1)}, u32[]{:S(2)}, u32[]{:S(2)}) collective-permute-start(bf16[2,256,256]{2,1,0:T(8,128)(2,1)S(1)} %collective-permute-done.4), channel_id=1, source_target_pairs={{0,4},{1,5},{2,6},{3,7},{4,8},{5,9},{6,10},{7,11},{8,12},{9,13},{1... | collective-permute-start | bytes 786440 | tf_op jit(solution)/shard_map/ppermute | solution.py:29
  28.0 12.5 %collective-permute-start.6 = (bf16[2,2,256,256]{3,2,1,0:T(8,128)(2,1)S(1)}, bf16[2,2,256,256]{3,2,1,0:T(8,128)(2,1)S(1)}, u32[]{:S(2)}, u32[]{:S(2)}) collective-permute-start(bf16[2,2,256,256]{3,2,1,0:T(8,128)(2,1)S(1)} %pad_maximum_fusion.2.refs_0_), channel_id=1, source_target_pairs={{0,4},{1,5},{2,6},{3,7},{4,8},{5,9},{6,10},{7,11},{8,12},{9,13},{1... | collective-permute-start | bytes 1572872 | tf_op jit(solution)/shard_map/ppermute | solution.py:29
  28.0 12.5 %collective-permute-start.11 = (bf16[2,2,256,256]{3,2,1,0:T(8,128)(2,1)S(1)}, bf16[2,2,256,256]{3,2,1,0:T(8,128)(2,1)S(1)}, u32[]{:S(2)}, u32[]{:S(2)}) collective-permute-start(bf16[2,2,256,256]{3,2,1,0:T(8,128)(2,1)S(1)} %pad_maximum_fusion.4.refs_6_.refs_8_), channel_id=1, source_target_pairs={{0,1},{1,2},{2,3},{3,0},{4,5},{5,6},{6,7},{7,4},{8,9},{9,10},{10,1... | collective-permute-start | bytes 1572872 | tf_op jit(solution)/shard_map/ppermute | solution.py:29
  29.3 12.0 %collective-permute-start.14 = (bf16[2,2,256,256]{3,2,1,0:T(8,128)(2,1)S(1)}, bf16[2,2,256,256]{3,2,1,0:T(8,128)(2,1)S(1)}, u32[]{:S(2)}, u32[]{:S(2)}) collective-permute-start(bf16[2,2,256,256]{3,2,1,0:T(8,128)(2,1)S(1)} %pad_maximum_fusion.5.refs_7_.refs_9_), channel_id=1, source_target_pairs={{0,3},{1,0},{2,1},{3,2},{4,7},{5,4},{6,5},{7,6},{8,11},{9,8},{10,9... | collective-permute-start | bytes 1572872 | tf_op jit(solution)/shard_map/ppermute | solution.py:29
  31.5 13.1 %collective-permute-start.10 = (bf16[2,2,256,256]{3,2,1,0:T(8,128)(2,1)S(1)}, bf16[2,2,256,256]{3,2,1,0:T(8,128)(2,1)S(1)}, u32[]{:S(2)}, u32[]{:S(2)}) collective-permute-start(bf16[2,2,256,256]{3,2,1,0:T(8,128)(2,1)S(1)} %pad_maximum_fusion.3.refs_1_), channel_id=1, source_target_pairs={{0,12},{1,13},{2,14},{3,15},{4,0},{5,1},{6,2},{7,3},{8,4},{9,5},{1... | collective-permute-start | bytes 1572872 | tf_op jit(solution)/shard_map/ppermute | solution.py:29
  40.5 12.0 %collective-permute-start.7 = (bf16[2,2,256,256]{3,2,1,0:T(8,128)(2,1)S(1)}, bf16[2,2,256,256]{3,2,1,0:T(8,128)(2,1)S(1)}, u32[]{:S(2)}, u32[]{:S(2)}) collective-permute-start(bf16[2,2,256,256]{3,2,1,0:T(8,128)(2,1)S(1)} %pad_maximum_fusion.3.refs_1_), channel_id=1, source_target_pairs={{0,4},{1,5},{2,6},{3,7},{4,8},{5,9},{6,10},{7,11},{8,12},{9,13},{1... | collective-permute-start | bytes 1572872 | tf_op jit(solution)/shard_map/ppermute | solution.py:29
  40.5 11.7 %collective-permute-start.12 = (bf16[2,2,256,256]{3,2,1,0:T(8,128)(2,1)S(1)}, bf16[2,2,256,256]{3,2,1,0:T(8,128)(2,1)S(1)}, u32[]{:S(2)}, u32[]{:S(2)}) collective-permute-start(bf16[2,2,256,256]{3,2,1,0:T(8,128)(2,1)S(1)} %pad_maximum_fusion.5.refs_7_.refs_9_), channel_id=1, source_target_pairs={{0,1},{1,2},{2,3},{3,0},{4,5},{5,6},{6,7},{7,4},{8,9},{9,10},{10,1... | collective-permute-start | bytes 1572872 | tf_op jit(solution)/shard_map/ppermute | solution.py:29
  41.3 6.2 %copy-start.2 = (s32[16,4]{0,1:T(4,128)S(1)}, s32[16,4]{0,1:T(4,128)}, u32[]{:S(2)}) copy-start(s32[16,4]{0,1:T(4,128)} %param.9) | copy-start | bytes 772
  41.3 6.2 %copy-start.3 = (s32[16,4]{0,1:T(4,128)S(1)}, s32[16,4]{0,1:T(4,128)}, u32[]{:S(2)}) copy-start(s32[16,4]{0,1:T(4,128)} %param.10) | copy-start | bytes 772
  41.3 6.2 %copy-start.4 = (s32[1,2,16]{2,1,0:T(2,128)S(1)}, s32[1,2,16]{2,1,0:T(2,128)}, u32[]{:S(2)}) copy-start(s32[1,2,16]{2,1,0:T(2,128)} %sizes.3) | copy-start | bytes 388
  41.3 6.2 %copy-start.5 = (bf16[1,16,1,256,256]{4,3,2,1,0:T(8,128)(2,1)S(1)}, bf16[1,16,1,256,256]{4,3,2,1,0:T(8,128)(2,1)}, u32[]{:S(2)}) copy-start(bf16[1,16,1,256,256]{4,3,2,1,0:T(8,128)(2,1)} %wave.1) | copy-start | bytes 6291460
  41.4 17.1 %collective-permute-start.18 = (bf16[6,256,256]{2,1,0:T(8,128)(2,1)S(1)}, bf16[6,256,256]{2,1,0:T(8,128)(2,1)S(1)}, u32[]{:S(2)}, u32[]{:S(2)}) collective-permute-start(bf16[6,256,256]{2,1,0:T(8,128)(2,1)S(1)} %pad_maximum_fusion.1), channel_id=1, source_target_pairs={{0,3},{1,0},{2,1},{3,2},{4,7},{5,4},{6,5},{7,6},{8,11},{9,8},{10,9... | collective-permute-start | bytes 2359304 | tf_op jit(solution)/shard_map/ppermute | solution.py:29
  44.7 16.3 %collective-permute-start.16 = (bf16[6,256,256]{2,1,0:T(8,128)(2,1)S(1)}, bf16[6,256,256]{2,1,0:T(8,128)(2,1)S(1)}, u32[]{:S(2)}, u32[]{:S(2)}) collective-permute-start(bf16[6,256,256]{2,1,0:T(8,128)(2,1)S(1)} %pad_maximum_fusion), channel_id=1, source_target_pairs={{0,12},{1,13},{2,14},{3,15},{4,0},{5,1},{6,2},{7,3},{8,4},{9,5},{1... | collective-permute-start | bytes 2359304 | tf_op jit(solution)/shard_map/ppermute | solution.py:29
  52.5 8.4 %collective-permute-start.15 = (bf16[2,256,256]{2,1,0:T(8,128)(2,1)S(1)}, bf16[2,256,256]{2,1,0:T(8,128)(2,1)S(1)}, u32[]{:S(2)}, u32[]{:S(2)}) collective-permute-start(bf16[2,256,256]{2,1,0:T(8,128)(2,1)S(1)} %slice_bitcast_fusion.3), channel_id=1, source_target_pairs={{0,4},{1,5},{2,6},{3,7},{4,8},{5,9},{6,10},{7,11},{8,12},{9,13},{1... | collective-permute-start | bytes 786440 | tf_op jit(solution)/shard_map/ppermute | solution.py:29
  52.5 8.4 %collective-permute-start.17 = (bf16[2,256,256]{2,1,0:T(8,128)(2,1)S(1)}, bf16[2,256,256]{2,1,0:T(8,128)(2,1)S(1)}, u32[]{:S(2)}, u32[]{:S(2)}) collective-permute-start(bf16[2,256,256]{2,1,0:T(8,128)(2,1)S(1)} %slice_bitcast_fusion.1), channel_id=1, source_target_pairs={{0,1},{1,2},{2,3},{3,0},{4,5},{5,6},{6,7},{7,4},{8,9},{9,10},{10,1... | collective-permute-start | bytes 786440 | tf_op jit(solution)/shard_map/ppermute | solution.py:29
